TPU v7x, 32 devices: a whole 2x2x4 slice. The times are simulated.
32 devices in a mesh: band: 16 (over z, y, x), lon: 2 (over core).
Axes of the slice: x: 2, y: 2, z: 4, core: 2. Of those that a mesh axis runs over, the one named last changes fastest.
Arguments:
- background: float32 [2, 16, 256, 256], P(None, None, ('lon', 'band')), may hold values from -6 to 6
- scale_x: float32 [16, 256, 256], P(None, ('lon', 'band')), may hold values from 0.04 to 0.24
- scale_y: float32 [16, 256, 256], P(None, ('lon', 'band')), may hold values from 0.04 to 0.24
- filter_bands: float32 [2, 5, 16], replicated, may hold values from -0.3 to 0.3
- band_rows: int32 [16], replicated, may hold values from 8 to 32, as said below
Outputs:
- increment: float32 [2, 16, 256, 256], P(None, None, ('lon', 'band'))
- band_field: float32 [2, 16, 512, 256], P(None, None, 'band', 'lon')
Inputs may be any that keep to these rules, and one draw needn't show every extreme that they name: `band_rows`: bands follow one another from the first row and their rows sum to 256; one band has exactly 32 rows and one exactly 8 rows.
All inputs are finite; a program needn't handle non-finite values.
Results may differ from a plain program's by a relative error of at most 0.0003.
Values sent between devices are 32-bit elements; how exact they have to be, the bound alone decides.
No kernel may reach another device: no remote copies, remote signals or barrier semaphores. Data moves between devices by JAX's collectives and lax.ppermute only.
A program may use at most 64 MiB of HBM per device.

v0:
```python
import jax
import jax.numpy as jnp
from jax import lax
from jax.sharding import PartitionSpec as P

STEPS = 8
CAP = 32


def extended(block, sides, width, periodic):
    for axis, dim in sides:
        count = lax.axis_size(axis)
        forward = [(i, i + 1) for i in range(count - 1)]
        if periodic:
            forward.append((count - 1, 0))
        backward = [(target, source) for source, target in forward]
        low = lax.ppermute(
            lax.slice_in_dim(block, block.shape[dim] - width, None, axis=dim), axis, forward
        )
        high = lax.ppermute(lax.slice_in_dim(block, 0, width, axis=dim), axis, backward)
        block = jnp.concatenate([low, block, high], axis=dim)
    return block


def spread(field, along_x, along_y, x_axis, y_axis):
    flux_x = along_x * (jnp.roll(field, -1, x_axis) - field)
    flux_y = along_y * (jnp.roll(field, -1, y_axis) - field)
    return field + flux_x - jnp.roll(flux_x, 1, x_axis) + flux_y - jnp.roll(flux_y, 1, y_axis)


def vertical(field, filter_bands):
    levels = field.shape[1]
    padded = jnp.pad(field, ((0, 0), (2, 2), (0, 0), (0, 0)))
    total = field
    for offset in range(5):
        weight = filter_bands[:, offset, :][:, :, None, None]
        total = total + weight * padded[:, offset : offset + levels]
    return total


def cut_rows(block, starts, lengths):
    padded = jnp.pad(block, ((0, 0), (0, 0), (0, CAP)))

    def one_band(start, length):
        piece = lax.dynamic_slice_in_dim(padded, start, CAP, 2)
        keep = (jnp.arange(CAP) < length).astype(jnp.float32)
        return piece * keep

    return jax.vmap(one_band)(starts, lengths)


def unpack_bands(arrived):
    count, channels, width, height = arrived.shape
    return jnp.transpose(arrived, (1, 3, 0, 2)).reshape(channels, height, count * width)


def pack_strips(block, count):
    channels, height, columns = block.shape
    split = block.reshape(channels, height, count, columns // count)
    return jnp.transpose(split, (2, 0, 3, 1))


def place_rows(arrived, starts, total_rows):
    count, channels, width, height = arrived.shape
    empty = jnp.zeros((channels, width, total_rows + height), jnp.float32)

    def add_band(index, whole):
        current = lax.dynamic_slice_in_dim(whole, starts[index], height, 2)
        return lax.dynamic_update_slice_in_dim(whole, current + arrived[index], starts[index], 2)

    whole = lax.fori_loop(0, count, add_band, empty)
    return whole[:, :, :total_rows]


def band_margin(block, length_here, depth):
    wide = extended(block, (("lon", 2),), depth, True)
    channels, height, columns = wide.shape
    lower = lax.dynamic_slice_in_dim(wide, length_here - depth, depth, 1)
    edges = jnp.concatenate([wide[:, :depth], lower], 1)
    beside_all = extended(edges, (("band", 1),), depth, False)
    grown = jnp.concatenate(
        [beside_all[:, :depth], wide, jnp.zeros((channels, depth, columns), jnp.float32)], 1
    )
    return lax.dynamic_update_slice_in_dim(
        grown, beside_all[:, 3 * depth :], depth + length_here, 1
    )


def diffuse_bands(field, coefs, length_here, depth):
    channels, height, columns = field.shape
    grown_coefs = band_margin(coefs, length_here, depth)
    levels = coefs.shape[0] // 2
    keep = (jnp.arange(height) < length_here).astype(jnp.float32)[:, None]
    for round_index in range(STEPS // depth):
        grown = band_margin(field, length_here, depth)
        grown = grown.reshape((channels // levels, levels) + grown.shape[1:])
        for step in range(depth):
            grown = spread(grown, grown_coefs[:levels], grown_coefs[levels:], 3, 2)
        field = (
            grown[:, :, depth : depth + height, depth : depth + columns].reshape(field.shape) * keep
        )
    return field


def shards(background, scale_x, scale_y, filter_bands, band_rows):
    variables, levels, width, rows = background.shape
    count = lax.axis_size("band")
    along_y = scale_y * (jnp.arange(rows) < rows - 1).astype(jnp.float32)
    starts = jnp.cumsum(band_rows) - band_rows
    depth = 4
    stacked = background.reshape(variables * levels, width, rows)
    length_here = band_rows[lax.axis_index("band")]
    package = jnp.concatenate([stacked, scale_x, along_y], 0)
    sent = cut_rows(package, starts, band_rows)
    arrived = unpack_bands(lax.all_to_all(sent, "band", split_axis=0, concat_axis=0, tiled=True))
    field = diffuse_bands(
        arrived[: variables * levels], arrived[variables * levels :], length_here, depth
    )
    band_field = vertical(field.reshape(variables, levels, CAP, field.shape[2]), filter_bands)
    outgoing = pack_strips(band_field.reshape(variables * levels, CAP, field.shape[2]), count)
    returned = lax.all_to_all(outgoing, "band", split_axis=0, concat_axis=0, tiled=True)
    increment = place_rows(returned, starts, rows).reshape(background.shape)
    return (increment, band_field)


def solution(mesh):
    in_specs = (
        P(None, None, ("lon", "band"), None),
        P(None, ("lon", "band"), None),
        P(None, ("lon", "band"), None),
        P(),
        P(),
    )
    out_specs = (P(None, None, ("lon", "band"), None), P(None, None, "band", "lon"))
    return jax.shard_map(shards, mesh=mesh, in_specs=in_specs, out_specs=out_specs, check_vma=False)
```

profile of v0, /device:TPU:0, one launch (start us, length us, event | category | flops | bytes accessed | tf_op | source)
XLA Modules:
  0.0 343.1 jit_solution(12506712419323878986)
XLA Ops:
  2.3 1.2 fusion.44
  4.8 1.4 copy.79
  6.2 1.3 copy.80
  7.5 1.8 select_maximum_fusion
  10.1 2.0 fusion.53
  12.0 3.4 reshape.105
  15.5 8.5 %all-to-all-start = ((f32[16,1,16384]{2,1,0:T(1,128)}), f32[16,1,16384]{2,1,0:T(1,128)S(1)}, u32[]{:S(2)}, u32[]{:S(2)}) async-start(f32[16,1,16384]{2,1,0:T(1,128)} %reshape.105), calls=%async_computation | async-start | bytes 2097152 | tf_op jit(solution)/shard_map/all_to_all | solution.py:115
  27.2 21.2 %all-to-all-done = f32[16,1,16384]{2,1,0:T(1,128)S(1)} async-done(((f32[16,1,16384]{2,1,0:T(1,128)}), f32[16,1,16384]{2,1,0:T(1,128)S(1)}, u32[]{:S(2)}, u32[]{:S(2)}) %all-to-all-start) | async-done | bytes 1048608 | tf_op jit(solution)/shard_map/all_to_all | solution.py:115
  48.9 3.1 reduce.1
  53.1 2.7 fusion.49
  55.8 3.1 copy.82
  59.6 4.1 %copy.87 = f32[32,32,16,8]{1,3,2,0:T(8,128)} copy(f32[32,32,16,8]{0,3,1,2:T(8,128)} %get-tuple-element.128) | data formatting | bytes 1048576 | tf_op jit(solution)/shard_map/slice | solution.py:117
  66.6 3.9 %fusion.46 = (f32[32,4,136]{1,2,0:T(8,128)}, f32[32,4,136]{1,2,0:T(8,128)}, f32[32,4,136]{1,2,0:T(8,128)}, f32[32,4,136]{1,2,0:T(8,128)S(1)}) fusion(f32[32,32,136]{1,2,0:T(8,128)S(1)} %pad_maximum_fusion.1, s32[]{:T(128)S(6)} %select_n.33, f32[32,32,136]{1,2,0:T(8,128)S(1)} %pad_maximum_fusion), kind=kLoop, calls=%fused_computation.106 | loop fusion | bytes 557060 | tf_op jit(solution)/shard_map/slice | solution.py:79
  70.5 2.8 copy.83
  73.4 2.4 collective-permute-start.2
  75.8 2.8 copy.88
  78.6 4.9 %collective-permute-start.6 = (f32[32,4,136]{2,0,1:T(8,128)S(1)}, f32[32,4,136]{2,0,1:T(8,128)S(1)}, u32[]{:S(2)}, u32[]{:S(2)}) collective-permute-start(f32[32,4,136]{2,0,1:T(8,128)S(1)} %copy.88), channel_id=1, source_target_pairs={{0,2},{2,4},{4,6},{6,8},{8,10},{10,12},{12,14},{14,16},{16,18},{18... | collective-permute-start | bytes 208904 | tf_op jit(solution)/shard_map/ppermute | solution.py:17
  84.1 2.8 copy.90
  87.0 1.3 collective-permute-start.7
  88.3 1.2 copy.85
  89.5 1.7 collective-permute-start.3
  91.2 2.2 copy.84
  93.4 2.2 copy.89
  95.6 6.3 %maximum_maximum_fusion.1 = (f32[32,40,136]{1,2,0:T(8,128)}, f32[32,40,136]{1,2,0:T(8,128)S(1)}) fusion(f32[32,32,4]{1,2,0:T(4,128)S(1)} %collective-permute-done.5, f32[32,32,128]{1,2,0:T(8,128)} %bitcast.95, f32[32,32,4]{1,2,0:T(4,128)S(1)} %collective-permute-done.4, f32[32,4,136]{1,2,0:T(8,128)} %copy.89, f32[40]{0:T(128)S(1)} %pad.95.clone, ...), kind=kLoop, calls=%fused_computation.9 | loop fusion | flops 1392640 | bytes 2646176 | tf_op jit(solution)/shard_map/concatenate | solution.py:81
  101.8 2.2 copy.86
  104.0 14.1 %dynamic_update_slice.16 = f32[32,40,136]{1,2,0:T(8,128)S(1)} dynamic-update-slice(f32[32,40,136]{1,2,0:T(8,128)S(1)} %get-tuple-element.142, f32[32,4,136]{1,2,0:T(8,128)} %copy.86, s32[]{:T(128)} %constant.50.clone.1, s32[]{:T(128)S(6)} %select_n.34, s32[]{:T(128)} %constant.50.clone.1) | dynamic-update-slice | bytes 139268 | tf_op jit(solution)/shard_map/dynamic_update_slice | solution.py:84
  118.1 1.7 slice.399
  119.8 2.1 slice.404
  122.6 13.0 %dynamic_update_slice.17 = f32[32,40,136]{1,2,0:T(8,128)} dynamic-update-slice(f32[32,40,136]{1,2,0:T(8,128)} %get-tuple-element.141, f32[32,4,136]{1,2,0:T(8,128)S(1)} %copy.91, s32[]{:T(128)} %constant.50.clone.1, s32[]{:T(128)S(6)} %select_n.34, s32[]{:T(128)} %constant.50.clone.1) | dynamic-update-slice | bytes 139268 | tf_op jit(solution)/shard_map/dynamic_update_slice | solution.py:84
  135.6 1.9 fusion.45
  138.5 2.6 fusion
  152.2 4.9 %fusion.40 = f32[2,16,32,128]{2,3,1,0:T(8,128)} fusion(f32[2,16,39,136]{2,3,1,0:T(8,128)S(1)} %bitcast.83, f32[2,16,1,136]{2,3,1,0:T(8,128)S(1)} %slice.430, f32[2,16,40,136]{2,3,1,0:T(8,128)S(1)} %get-tuple-element.113, f32[2,16,40,135]{2,3,1,0:T(8,128)S(1)} %bitcast.97, f32[2,16,40,1]{2,3,1,0:T(1,128)S(1)} %slice.426, ...), kind=kLoop, calls=%fused_computation.77 | loop fusion | flops 786432 | bytes 3489792 | tf_op jit(solution)/shard_map/sub | solution.py:28
  157.1 2.2 copy.92
  160.2 1.4 collective-permute-done.8
  163.0 5.2 %collective-permute-start.10 = (f32[32,4,136]{2,0,1:T(8,128)S(1)}, f32[32,4,136]{2,0,1:T(8,128)S(1)}, u32[]{:S(2)}, u32[]{:S(2)}) collective-permute-start(f32[32,4,136]{2,0,1:T(8,128)S(1)} %copy.101), channel_id=1, source_target_pairs={{0,2},{2,4},{4,6},{6,8},{8,10},{10,12},{12,14},{14,16},{16,18},{18... | collective-permute-start | bytes 208904 | tf_op jit(solution)/shard_map/ppermute | solution.py:17
  168.8 1.3 collective-permute-start.11
  171.9 5.5 %collective-permute-done.11 = f32[32,4,136]{2,0,1:T(8,128)S(1)} collective-permute-done((f32[32,4,136]{2,0,1:T(8,128)S(1)}, f32[32,4,136]{2,0,1:T(8,128)S(1)}, u32[]{:S(2)}, u32[]{:S(2)}) %collective-permute-start.11) | collective-permute-done | bytes 69664 | tf_op jit(solution)/shard_map/ppermute | solution.py:20
  178.1 1.2 dynamic_update_slice.18
  179.3 2.0 copy.98
  181.3 1.9 slice.438
  196.3 3.6 %fusion.38 = f32[2,16,32,128]{2,3,1,0:T(8,128)S(1)} fusion(f32[2,16,39,136]{2,3,1,0:T(8,128)S(1)} %bitcast.84, f32[2,16,1,136]{2,3,1,0:T(8,128)S(1)} %slice.468, f32[2,16,40,136]{2,3,1,0:T(8,128)S(1)} %get-tuple-element.105, f32[2,16,40,135]{2,3,1,0:T(8,128)S(1)} %bitcast.98, f32[2,16,40,1]{2,3,1,0:T(1,128)S(1)} %slice.464, ...), kind=kLoop, calls=%fused_computation.71 | loop fusion | flops 917504 | bytes 3489920 | tf_op jit(solution)/shard_map/mul | solution.py:100
  199.9 1.3 fusion.33
  201.2 1.6 copy.99
  202.8 3.1 reshape.107
  205.9 7.5 %all-to-all-start.1 = ((f32[16,1,8192]{2,1,0:T(1,128)}), f32[16,1,8192]{2,1,0:T(1,128)S(1)}, u32[]{:S(2)}, u32[]{:S(2)}) async-start(f32[16,1,8192]{2,1,0:T(1,128)} %reshape.107), calls=%async_computation.1 | async-start | bytes 1048576 | tf_op jit(solution)/shard_map/all_to_all | solution.py:121
  213.4 1.4 copy.100
  214.8 13.0 %all-to-all-done.1 = f32[16,1,8192]{2,1,0:T(1,128)S(1)} async-done(((f32[16,1,8192]{2,1,0:T(1,128)}), f32[16,1,8192]{2,1,0:T(1,128)S(1)}, u32[]{:S(2)}, u32[]{:S(2)}) %all-to-all-start.1) | async-done | bytes 524320 | tf_op jit(solution)/shard_map/all_to_all | solution.py:121
  227.8 1.8 reduce.2
  230.4 111.8 %while.13 = (s32[]{:T(128)}, f32[32,8,288]{2,1,0:T(8,128)S(1)}, s32[16]{0:T(128)S(1)}, f32[16,32,8,32]{3,2,1,0:T(8,128)S(1)}, s32[]{:T(128)}, /*index=5*/s32[]{:T(128)}, s32[]{:T(128)}) while((s32[]{:T(128)}, f32[32,8,288]{2,1,0:T(8,128)S(1)}, s32[16]{0:T(128)S(1)}, f32[16,32,8,32]{3,2,1,0:T(8,128)S(1)}, s32[]{:T(128)}, /*index=5*/s32[]{:T(128)}, ...), condition=%wide.region_2.3_spmd, body=%wide.region_1.2_spmd.sunk | while | flops 8197 | bytes 163975 | solution.py:71
  235.7 4.8 %dynamic_update_slice.20 = f32[32,8,288]{2,1,0:T(8,128)S(1)} dynamic-update-slice(f32[32,8,288]{2,1,0:T(8,128)S(1)} %get-tuple-element.178, f32[32,8,32]{2,1,0:T(8,128)S(1)} %bitcast_add_fusion.2, s32[]{:T(128)} %constant.50.clone.1..sunk, s32[]{:T(128)} %constant.50.clone.1..sunk, s32[]{:T(128)S(6)} %select_n.41) | dynamic-update-slice | bytes 65540 | tf_op jit(solution)/shard_map/while/body/eval_jaxpr/dynamic_update_slice | solution.py:69
  243.0 4.8 %dynamic_update_slice.20 = f32[32,8,288]{2,1,0:T(8,128)S(1)} dynamic-update-slice(f32[32,8,288]{2,1,0:T(8,128)S(1)} %get-tuple-element.178, f32[32,8,32]{2,1,0:T(8,128)S(1)} %bitcast_add_fusion.2, s32[]{:T(128)} %constant.50.clone.1..sunk, s32[]{:T(128)} %constant.50.clone.1..sunk, s32[]{:T(128)S(6)} %select_n.41) | dynamic-update-slice | bytes 65540 | tf_op jit(solution)/shard_map/while/body/eval_jaxpr/dynamic_update_slice | solution.py:69
  250.2 4.8 %dynamic_update_slice.20 = f32[32,8,288]{2,1,0:T(8,128)S(1)} dynamic-update-slice(f32[32,8,288]{2,1,0:T(8,128)S(1)} %get-tuple-element.178, f32[32,8,32]{2,1,0:T(8,128)S(1)} %bitcast_add_fusion.2, s32[]{:T(128)} %constant.50.clone.1..sunk, s32[]{:T(128)} %constant.50.clone.1..sunk, s32[]{:T(128)S(6)} %select_n.41) | dynamic-update-slice | bytes 65540 | tf_op jit(solution)/shard_map/while/body/eval_jaxpr/dynamic_update_slice | solution.py:69
  257.5 4.8 %dynamic_update_slice.20 = f32[32,8,288]{2,1,0:T(8,128)S(1)} dynamic-update-slice(f32[32,8,288]{2,1,0:T(8,128)S(1)} %get-tuple-element.178, f32[32,8,32]{2,1,0:T(8,128)S(1)} %bitcast_add_fusion.2, s32[]{:T(128)} %constant.50.clone.1..sunk, s32[]{:T(128)} %constant.50.clone.1..sunk, s32[]{:T(128)S(6)} %select_n.41) | dynamic-update-slice | bytes 65540 | tf_op jit(solution)/shard_map/while/body/eval_jaxpr/dynamic_update_slice | solution.py:69
  264.7 4.8 %dynamic_update_slice.20 = f32[32,8,288]{2,1,0:T(8,128)S(1)} dynamic-update-slice(f32[32,8,288]{2,1,0:T(8,128)S(1)} %get-tuple-element.178, f32[32,8,32]{2,1,0:T(8,128)S(1)} %bitcast_add_fusion.2, s32[]{:T(128)} %constant.50.clone.1..sunk, s32[]{:T(128)} %constant.50.clone.1..sunk, s32[]{:T(128)S(6)} %select_n.41) | dynamic-update-slice | bytes 65540 | tf_op jit(solution)/shard_map/while/body/eval_jaxpr/dynamic_update_slice | solution.py:69
  272.0 4.8 %dynamic_update_slice.20 = f32[32,8,288]{2,1,0:T(8,128)S(1)} dynamic-update-slice(f32[32,8,288]{2,1,0:T(8,128)S(1)} %get-tuple-element.178, f32[32,8,32]{2,1,0:T(8,128)S(1)} %bitcast_add_fusion.2, s32[]{:T(128)} %constant.50.clone.1..sunk, s32[]{:T(128)} %constant.50.clone.1..sunk, s32[]{:T(128)S(6)} %select_n.41) | dynamic-update-slice | bytes 65540 | tf_op jit(solution)/shard_map/while/body/eval_jaxpr/dynamic_update_slice | solution.py:69
  279.3 4.8 %dynamic_update_slice.20 = f32[32,8,288]{2,1,0:T(8,128)S(1)} dynamic-update-slice(f32[32,8,288]{2,1,0:T(8,128)S(1)} %get-tuple-element.178, f32[32,8,32]{2,1,0:T(8,128)S(1)} %bitcast_add_fusion.2, s32[]{:T(128)} %constant.50.clone.1..sunk, s32[]{:T(128)} %constant.50.clone.1..sunk, s32[]{:T(128)S(6)} %select_n.41) | dynamic-update-slice | bytes 65540 | tf_op jit(solution)/shard_map/while/body/eval_jaxpr/dynamic_update_slice | solution.py:69
  286.5 4.8 %dynamic_update_slice.20 = f32[32,8,288]{2,1,0:T(8,128)S(1)} dynamic-update-slice(f32[32,8,288]{2,1,0:T(8,128)S(1)} %get-tuple-element.178, f32[32,8,32]{2,1,0:T(8,128)S(1)} %bitcast_add_fusion.2, s32[]{:T(128)} %constant.50.clone.1..sunk, s32[]{:T(128)} %constant.50.clone.1..sunk, s32[]{:T(128)S(6)} %select_n.41) | dynamic-update-slice | bytes 65540 | tf_op jit(solution)/shard_map/while/body/eval_jaxpr/dynamic_update_slice | solution.py:69
  293.8 4.8 %dynamic_update_slice.20 = f32[32,8,288]{2,1,0:T(8,128)S(1)} dynamic-update-slice(f32[32,8,288]{2,1,0:T(8,128)S(1)} %get-tuple-element.178, f32[32,8,32]{2,1,0:T(8,128)S(1)} %bitcast_add_fusion.2, s32[]{:T(128)} %constant.50.clone.1..sunk, s32[]{:T(128)} %constant.50.clone.1..sunk, s32[]{:T(128)S(6)} %select_n.41) | dynamic-update-slice | bytes 65540 | tf_op jit(solution)/shard_map/while/body/eval_jaxpr/dynamic_update_slice | solution.py:69
  301.0 4.8 %dynamic_update_slice.20 = f32[32,8,288]{2,1,0:T(8,128)S(1)} dynamic-update-slice(f32[32,8,288]{2,1,0:T(8,128)S(1)} %get-tuple-element.178, f32[32,8,32]{2,1,0:T(8,128)S(1)} %bitcast_add_fusion.2, s32[]{:T(128)} %constant.50.clone.1..sunk, s32[]{:T(128)} %constant.50.clone.1..sunk, s32[]{:T(128)S(6)} %select_n.41) | dynamic-update-slice | bytes 65540 | tf_op jit(solution)/shard_map/while/body/eval_jaxpr/dynamic_update_slice | solution.py:69
  308.3 4.8 %dynamic_update_slice.20 = f32[32,8,288]{2,1,0:T(8,128)S(1)} dynamic-update-slice(f32[32,8,288]{2,1,0:T(8,128)S(1)} %get-tuple-element.178, f32[32,8,32]{2,1,0:T(8,128)S(1)} %bitcast_add_fusion.2, s32[]{:T(128)} %constant.50.clone.1..sunk, s32[]{:T(128)} %constant.50.clone.1..sunk, s32[]{:T(128)S(6)} %select_n.41) | dynamic-update-slice | bytes 65540 | tf_op jit(solution)/shard_map/while/body/eval_jaxpr/dynamic_update_slice | solution.py:69
  315.5 4.8 %dynamic_update_slice.20 = f32[32,8,288]{2,1,0:T(8,128)S(1)} dynamic-update-slice(f32[32,8,288]{2,1,0:T(8,128)S(1)} %get-tuple-element.178, f32[32,8,32]{2,1,0:T(8,128)S(1)} %bitcast_add_fusion.2, s32[]{:T(128)} %constant.50.clone.1..sunk, s32[]{:T(128)} %constant.50.clone.1..sunk, s32[]{:T(128)S(6)} %select_n.41) | dynamic-update-slice | bytes 65540 | tf_op jit(solution)/shard_map/while/body/eval_jaxpr/dynamic_update_slice | solution.py:69
  322.8 4.8 %dynamic_update_slice.20 = f32[32,8,288]{2,1,0:T(8,128)S(1)} dynamic-update-slice(f32[32,8,288]{2,1,0:T(8,128)S(1)} %get-tuple-element.178, f32[32,8,32]{2,1,0:T(8,128)S(1)} %bitcast_add_fusion.2, s32[]{:T(128)} %constant.50.clone.1..sunk, s32[]{:T(128)} %constant.50.clone.1..sunk, s32[]{:T(128)S(6)} %select_n.41) | dynamic-update-slice | bytes 65540 | tf_op jit(solution)/shard_map/while/body/eval_jaxpr/dynamic_update_slice | solution.py:69
  330.1 4.8 %dynamic_update_slice.20 = f32[32,8,288]{2,1,0:T(8,128)S(1)} dynamic-update-slice(f32[32,8,288]{2,1,0:T(8,128)S(1)} %get-tuple-element.178, f32[32,8,32]{2,1,0:T(8,128)S(1)} %bitcast_add_fusion.2, s32[]{:T(128)} %constant.50.clone.1..sunk, s32[]{:T(128)} %constant.50.clone.1..sunk, s32[]{:T(128)S(6)} %select_n.41) | dynamic-update-slice | bytes 65540 | tf_op jit(solution)/shard_map/while/body/eval_jaxpr/dynamic_update_slice | solution.py:69
  337.3 4.8 %dynamic_update_slice.20 = f32[32,8,288]{2,1,0:T(8,128)S(1)} dynamic-update-slice(f32[32,8,288]{2,1,0:T(8,128)S(1)} %get-tuple-element.178, f32[32,8,32]{2,1,0:T(8,128)S(1)} %bitcast_add_fusion.2, s32[]{:T(128)} %constant.50.clone.1..sunk, s32[]{:T(128)} %constant.50.clone.1..sunk, s32[]{:T(128)S(6)} %select_n.41) | dynamic-update-slice | bytes 65540 | tf_op jit(solution)/shard_map/while/body/eval_jaxpr/dynamic_update_slice | solution.py:69
  (162 shorter events, 54.2 us)
Async XLA Ops:
  0.6 5.6 %copy-start.6 = (f32[16,8,256]{2,1,0:T(8,128)S(1)}, f32[16,8,256]{2,1,0:T(8,128)}, u32[]{:S(2)}) copy-start(f32[16,8,256]{2,1,0:T(8,128)} %param.8) | copy-start | bytes 393220
  12.0 11.9 %copy-start.8 = (s32[16]{0:T(128)S(1)}, s32[16]{0:T(128)}, u32[]{:S(2)}) copy-start(s32[16]{0:T(128)} %param.11) | copy-start | bytes 196
  15.5 32.9 %all-to-all-start = ((f32[16,1,16384]{2,1,0:T(1,128)}), f32[16,1,16384]{2,1,0:T(1,128)S(1)}, u32[]{:S(2)}, u32[]{:S(2)}) async-start(f32[16,1,16384]{2,1,0:T(1,128)} %reshape.105), calls=%async_computation | async-start | bytes 2097152 | tf_op jit(solution)/shard_map/all_to_all | solution.py:115
  27.2 68.3 %copy-start.12 = (f32[40]{0:T(128)}, f32[40]{0:T(128)S(1)}, u32[]{:S(2)}) copy-start(f32[40]{0:T(128)S(1)} %pad.95.clone) | copy-start | bytes 484
  59.0 6.3 %copy-start.3 = (f32[32,32,16,8]{1,3,2,0:T(8,128)}, f32[32,32,16,8]{1,3,2,0:T(8,128)S(1)}, u32[]{:S(2)}) copy-start(f32[32,32,16,8]{1,3,2,0:T(8,128)S(1)} %copy.82) | copy-start | bytes 1572868
  59.0 6.2 %collective-permute-start = (f32[32,32,4]{1,2,0:T(4,128)S(1)}, f32[32,32,4]{1,2,0:T(4,128)S(1)}, u32[]{:S(2)}, u32[]{:S(2)}) collective-permute-start(f32[32,32,4]{1,2,0:T(4,128)S(1)} %get-tuple-element.130), channel_id=1, source_target_pairs={{0,1},{1,0},{2,3},{3,2},{4,5},{5,4},{6,7},{7,6},{8,9},{9,8},{10,11... | collective-permute-start | bytes 49160 | tf_op jit(solution)/shard_map/ppermute | solution.py:17
  59.1 6.1 %collective-permute-start.1 = (f32[32,32,4]{1,2,0:T(4,128)S(1)}, f32[32,32,4]{1,2,0:T(4,128)S(1)}, u32[]{:S(2)}, u32[]{:S(2)}) collective-permute-start(f32[32,32,4]{1,2,0:T(4,128)S(1)} %get-tuple-element.131), channel_id=1, source_target_pairs={{1,0},{0,1},{3,2},{2,3},{5,4},{4,5},{7,6},{6,7},{9,8},{8,9},{11,10... | collective-permute-start | bytes 49160 | tf_op jit(solution)/shard_map/ppermute | solution.py:20
  64.6 1.3 collective-permute-start.4
  64.7 1.6 copy-start.4
  64.7 1.4 collective-permute-start.5
  73.4 17.8 %collective-permute-start.2 = (f32[32,4,136]{2,0,1:T(8,128)S(1)}, f32[32,4,136]{2,0,1:T(8,128)S(1)}, u32[]{:S(2)}, u32[]{:S(2)}) collective-permute-start(f32[32,4,136]{2,0,1:T(8,128)S(1)} %copy.83), channel_id=1, source_target_pairs={{0,2},{2,4},{4,6},{6,8},{8,10},{10,12},{12,14},{14,16},{16,18},{18... | collective-permute-start | bytes 208904 | tf_op jit(solution)/shard_map/ppermute | solution.py:17
  78.6 14.8 %collective-permute-start.6 = (f32[32,4,136]{2,0,1:T(8,128)S(1)}, f32[32,4,136]{2,0,1:T(8,128)S(1)}, u32[]{:S(2)}, u32[]{:S(2)}) collective-permute-start(f32[32,4,136]{2,0,1:T(8,128)S(1)} %copy.88), channel_id=1, source_target_pairs={{0,2},{2,4},{4,6},{6,8},{8,10},{10,12},{12,14},{14,16},{16,18},{18... | collective-permute-start | bytes 208904 | tf_op jit(solution)/shard_map/ppermute | solution.py:17
  84.1 75.2 %copy-start.10 = (f32[32]{0:T(128)}, f32[32]{0:T(128)S(1)}, u32[]{:S(2)}) copy-start(f32[32]{0:T(128)S(1)} %compare_convert_fusion) | copy-start | bytes 388
  87.0 34.9 %collective-permute-start.7 = (f32[32,4,136]{2,0,1:T(8,128)S(1)}, f32[32,4,136]{2,0,1:T(8,128)S(1)}, u32[]{:S(2)}, u32[]{:S(2)}) collective-permute-start(f32[32,4,136]{2,0,1:T(8,128)S(1)} %copy.90), channel_id=1, source_target_pairs={{2,0},{4,2},{6,4},{8,6},{10,8},{12,10},{14,12},{16,14},{18,16},{20... | collective-permute-start | bytes 208904 | tf_op jit(solution)/shard_map/ppermute | solution.py:20
  89.5 12.3 %collective-permute-start.3 = (f32[32,4,136]{2,0,1:T(8,128)S(1)}, f32[32,4,136]{2,0,1:T(8,128)S(1)}, u32[]{:S(2)}, u32[]{:S(2)}) collective-permute-start(f32[32,4,136]{2,0,1:T(8,128)S(1)} %copy.85), channel_id=1, source_target_pairs={{2,0},{4,2},{6,4},{8,6},{10,8},{12,10},{14,12},{16,14},{18,16},{20... | collective-permute-start | bytes 208904 | tf_op jit(solution)/shard_map/ppermute | solution.py:20
  118.1 3.7 %copy-start = (f32[32,40,136]{1,2,0:T(8,128)}, f32[32,40,136]{1,2,0:T(8,128)S(1)}, u32[]{:S(2)}) copy-start(f32[32,40,136]{1,2,0:T(8,128)S(1)} %dynamic_update_slice.16) | copy-start | bytes 2088964
  135.6 2.3 copy-start.1
  135.6 3.0 copy-start.5
  159.6 8.5 %copy-start.7 = (f32[2,5,16]{2,0,1:T(2,128)S(1)}, f32[2,5,16]{2,0,1:T(2,128)}, u32[]{:S(2)}) copy-start(f32[2,5,16]{2,0,1:T(2,128)} %param.10) | copy-start | bytes 1924
  159.7 11.6 %copy-start.13 = (f32[40]{0:T(128)S(1)}, f32[40]{0:T(128)}, u32[]{:S(2)}) copy-start(f32[40]{0:T(128)} %copy-done.12) | copy-start | bytes 484
  159.7 2.0 collective-permute-start.8
  159.7 2.6 collective-permute-start.9
  163.0 8.2 %collective-permute-start.10 = (f32[32,4,136]{2,0,1:T(8,128)S(1)}, f32[32,4,136]{2,0,1:T(8,128)S(1)}, u32[]{:S(2)}, u32[]{:S(2)}) collective-permute-start(f32[32,4,136]{2,0,1:T(8,128)S(1)} %copy.101), channel_id=1, source_target_pairs={{0,2},{2,4},{4,6},{6,8},{8,10},{10,12},{12,14},{14,16},{16,18},{18... | collective-permute-start | bytes 208904 | tf_op jit(solution)/shard_map/ppermute | solution.py:17
  168.8 8.6 %collective-permute-start.11 = (f32[32,4,136]{2,0,1:T(8,128)S(1)}, f32[32,4,136]{2,0,1:T(8,128)S(1)}, u32[]{:S(2)}, u32[]{:S(2)}) collective-permute-start(f32[32,4,136]{2,0,1:T(8,128)S(1)} %copy.102), channel_id=1, source_target_pairs={{2,0},{4,2},{6,4},{8,6},{10,8},{12,10},{14,12},{16,14},{18,16},{20... | collective-permute-start | bytes 208904 | tf_op jit(solution)/shard_map/ppermute | solution.py:20
  181.3 2.3 copy-start.2
  195.6 0.7 copy-start.11
  196.3 3.6 %copy-start.9 = (f32[2,16]{1,0:T(2,128)S(1)}, f32[2,16]{1,0:T(2,128)}, u32[]{:S(2)}) copy-start(f32[2,16]{1,0:T(2,128)} %get-tuple-element.140) | copy-start | bytes 388
  205.9 21.8 %all-to-all-start.1 = ((f32[16,1,8192]{2,1,0:T(1,128)}), f32[16,1,8192]{2,1,0:T(1,128)S(1)}, u32[]{:S(2)}, u32[]{:S(2)}) async-start(f32[16,1,8192]{2,1,0:T(1,128)} %reshape.107), calls=%async_computation.1 | async-start | bytes 1048576 | tf_op jit(solution)/shard_map/all_to_all | solution.py:121
  214.8 15.5 %copy-start.14 = (s32[16]{0:T(128)S(1)}, s32[16]{0:T(128)}, u32[]{:S(2)}) copy-start(s32[16]{0:T(128)} %get-tuple-element.172) | copy-start | bytes 196
where the time goes:
time: 348 us; the launch traced here: 343 us
  local copies, waits for them, and re-layouts  186 us (53%)
  other arithmetic  47.4 us (14%)
  waiting for transfers between devices  43.5 us (12%)
  starting transfers between devices  34.4 us (10%)
  loops' own time  27.8 us (8%)
  between operations  4.14 us (1%)
    dynamic_update_slice x16, local copies, waits for them, and re-layouts, add_band(): lax.dynamic_update_slice_in_dim(whole, current + arrived[index], starts[i...  73 us
    dynamic_update_slice x4, local copies, waits for them, and re-layouts, band_margin(): lax.dynamic_update_slice_in_dim(grown, beside_all[:, 3 * depth:], depth +...  30.2 us
    another operation x1, loops' own time, place_rows(): whole = lax.fori_loop(0, count, add_band, empty)  27.8 us
    all_to_all x1, waiting for transfers between devices, shards(): lax.all_to_all(sent, 'band', split_axis=0, concat_axis=0, tiled=True)  21.2 us
    all_to_all x1, waiting for transfers between devices, shards(): lax.all_to_all(outgoing, 'band', split_axis=0, concat_axis=0, tiled=True)  13 us
    ppermute x6, starting transfers between devices, extended(): lax.ppermute(lax.slice_in_dim(block, block.shape[dim] - width, None, axis...  12.7 us
    unnamed x38, local copies, waits for them, and re-layouts  12.5 us
    sub x7, other arithmetic, spread(): field + flux_x - jnp.roll(flux_x, 1, x_axis) + flux_y  11 us
  transfers between devices with their start and end apart: 14, of which 8 were waited for; matrix products, arithmetic and copies ran while one was open for 14% of the time, Pallas kernels for 0%

commit v1 on v0

v1 whole, which is shorter than its diff:
```python
import functools
import math

import jax
import jax.numpy as jnp
from jax import lax
from jax.experimental import pallas as pl
from jax.experimental.pallas import tpu as pltpu
from jax.sharding import PartitionSpec as P

STEPS = 8
CAP = 32
LANES = 128
TAPS = 5
VMEM = pl.BlockSpec(memory_space=pltpu.VMEM)
SMEM = pl.BlockSpec(memory_space=pltpu.SMEM)
ANY = pl.BlockSpec(memory_space=pl.ANY)


def regroup_kernel(background, scale_x, scale_y, out, sems):
    variables, levels = background.shape[:2]
    groups = out.shape[0]
    part = levels // groups
    copies = []
    for q in range(groups):
        near = pl.ds(q * part, part)
        sources = [background.at[v, near] for v in range(variables)]
        sources += [scale_x.at[near], scale_y.at[near]]
        for i, source in enumerate(sources):
            copies.append(
                pltpu.make_async_copy(source, out.at[q, pl.ds(i * part, part)], sems.at[q, i])
            )
    for copy in copies:
        copy.start()
    for copy in copies:
        copy.wait()


def diffuse_kernel(
    groups, band_rows, low, mine, high, bands, *rest
):
    strips, field, along_x, along_y, result = rest[:groups], *rest[groups:]
    _, channels, width, rows = mine.shape
    part = channels // 4
    pairs = 2 * part
    sources = [low] + [mine.at[s] for s in range(groups)] + [high]
    columns = len(sources) * width
    inside = lax.broadcasted_iota(jnp.int32, (pairs, rows), 1) < rows - 1
    for s, source in enumerate(sources):
        flow = jnp.swapaxes(source[...], 0, 1)
        field[pl.ds(s * width, width)] = flow[:, :pairs]
        coef_x = flow[:, pairs : pairs + part]
        coef_y = flow[:, pairs + part :]
        along_x[pl.ds(s * width, width)] = jnp.concatenate([coef_x, coef_x], 1)
        coef_y = jnp.concatenate([coef_y, coef_y], 1)
        along_y[pl.ds(s * width, width)] = jnp.where(inside[None], coef_y, 0.0)

    for step in range(STEPS):
        first, last = step + 1, columns - 1 - step
        here = field[first]
        before = along_x[first - 1] * (here - field[first - 1])
        for c in range(first, last):
            after = field[c + 1]
            flux_x = along_x[c] * (after - here)
            flux_y = along_y[c] * (pltpu.roll(here, rows - 1, 1) - here)
            field[c] = here + flux_x - before + flux_y - pltpu.roll(flux_y, 1, 1)
            here, before = after, flux_x

    me = lax.rem(lax.axis_index("band"), groups)
    for s in range(groups):
        block = jnp.swapaxes(field[pl.ds((s + 1) * width, width)], 0, 1)
        for half in range(rows // LANES):
            result[half, :, pl.ds(s * width, width)] = block[:, :, half * LANES : (half + 1) * LANES]
        strips_block = block
        for k in range(groups):
            @pl.when(jnp.bitwise_xor(me, k) == s)
            def _(k=k, strips_block=strips_block):
                strips[k][...] = strips_block

    halves = rows // LANES
    lane = lax.broadcasted_iota(jnp.int32, (groups * width, LANES), 1)

    def one_band(b, start):
        half = start // LANES
        offset = start - half * LANES
        beyond = lax.rem(half + 1, halves)
        for v in range(2):
            packed = None
            for l in range(part):
                i = v * part + l
                window = jnp.where(lane >= offset, result[half, i], result[beyond, i])
                shift = lax.rem(LANES + l * CAP - offset, LANES)
                turned = pltpu.roll(window, shift, 1)
                packed = turned if l == 0 else jnp.where(lane >= l * CAP, turned, packed)
            bands[b, v] = packed
        return start + band_rows[b]

    lax.fori_loop(0, bands.shape[0], one_band, jnp.int32(0))


def filtered(weights, v, l, levels, at):
    total = at(v, l)
    for tap in range(TAPS):
        other = l + tap - TAPS // 2
        if 0 <= other < levels:
            total = total + weights[v, tap, l] * at(v, other)
    return total


def increment_kernel(groups, weights, *refs):
    pieces, out, whole = refs[:groups], refs[groups], refs[groups + 1]
    variables, levels = out.shape[:2]
    part = levels // groups
    me = lax.rem(lax.axis_index("band"), groups)
    for k in range(groups):
        near = pl.ds(jnp.bitwise_xor(me, k) * part, part)
        for v in range(variables):
            whole[v, near] = pieces[k][pl.ds(v * part, part)]
    for v in range(variables):
        for l in range(levels):
            out[v, l] = filtered(weights, v, l, levels, lambda a, b: whole[a, b])


def band_kernel(groups, band_rows, weights, arrived, out, whole):
    variables, levels, height, columns = out.shape
    part = levels // groups
    count = arrived.shape[0]
    here = band_rows[lax.axis_index("band")]
    for v in range(variables):
        for q in range(groups):
            tall = jnp.concatenate([arrived[s, v] for s in range(q, count, groups)], 0)
            flat = jnp.transpose(tall)
            for l in range(part):
                whole[v, q * part + l] = flat[l * height : (l + 1) * height]
    keep = lax.broadcasted_iota(jnp.int32, (height, columns), 0) < here
    for v in range(variables):
        for l in range(levels):
            total = filtered(weights, v, l, levels, lambda a, b: whole[a, b])
            out[v, l] = jnp.where(keep, total, 0.0)


def shards(mesh_shape, background, scale_x, scale_y, filter_bands, band_rows):
    variables, levels, width, rows = background.shape
    count, blocks = mesh_shape["band"], mesh_shape["lon"]
    groups = math.isqrt(count)
    part = levels // groups
    channels = (variables + 2) * part
    f32 = jnp.float32

    def struct(*shape):
        return jax.ShapeDtypeStruct(shape, f32)

    parted = pl.pallas_call(
        regroup_kernel,
        out_shape=struct(groups, channels, width, rows),
        in_specs=[ANY] * 3,
        out_specs=ANY,
        scratch_shapes=[pltpu.SemaphoreType.DMA((groups, variables + 2))],
        name="regroup",
    )(background, scale_x, scale_y)
    near = [[g * groups + i for i in range(groups)] for g in range(count // groups)]
    mine = lax.all_to_all(
        parted, "band", split_axis=0, concat_axis=0, tiled=True, axis_index_groups=near
    )

    def shifted(by):
        total = count * blocks
        pairs = []
        for source in range(total):
            target = (source + by) % total
            pairs.append(
                (
                    source % count * blocks + source // count,
                    target % count * blocks + target // count,
                )
            )
        return pairs

    axes = ("band", "lon")
    low = lax.ppermute(mine[groups - 1], axes, shifted(groups))
    high = lax.ppermute(mine[0], axes, shifted(-groups))
    span = groups * width
    wide = (groups + 2) * width
    outs = pl.pallas_call(
        functools.partial(diffuse_kernel, groups),
        out_shape=[struct(count, variables, span, LANES)]
        + [struct(variables * part, width, rows)] * groups,
        in_specs=[SMEM] + [VMEM] * 3,
        out_specs=[VMEM] * (groups + 1),
        scratch_shapes=[pltpu.VMEM((wide, variables * part, rows), f32)] * 3
        + [pltpu.VMEM((rows // LANES, variables * part, span, LANES), f32)],
        name="diffuse",
    )(band_rows, low, mine, high)
    bands, strips = outs[0], outs[1:]
    arrived = lax.all_to_all(bands, "band", split_axis=0, concat_axis=0, tiled=True)
    pieces = [strips[0]] + [
        lax.ppermute(strips[k], "band", [(i, i ^ k) for i in range(count)])
        for k in range(1, groups)
    ]
    increment = pl.pallas_call(
        functools.partial(increment_kernel, groups),
        out_shape=struct(*background.shape),
        in_specs=[SMEM] + [VMEM] * groups,
        out_specs=VMEM,
        scratch_shapes=[pltpu.VMEM((variables, levels, width, rows), f32)],
        name="increment",
    )(filter_bands, *pieces)
    band_field = pl.pallas_call(
        functools.partial(band_kernel, groups),
        out_shape=struct(variables, levels, CAP, count * width),
        in_specs=[SMEM, SMEM, VMEM],
        out_specs=VMEM,
        scratch_shapes=[pltpu.VMEM((variables, levels, CAP, count * width), f32)],
        name="bands",
    )(band_rows, filter_bands, arrived)
    return increment, band_field


def solution(mesh):
    in_specs = (
        P(None, None, ("lon", "band"), None),
        P(None, ("lon", "band"), None),
        P(None, ("lon", "band"), None),
        P(),
        P(),
    )
    out_specs = (P(None, None, ("lon", "band"), None), P(None, None, "band", "lon"))
    return jax.shard_map(
        functools.partial(shards, dict(mesh.shape)),
        mesh=mesh,
        in_specs=in_specs,
        out_specs=out_specs,
        check_vma=False,
    )
```

time: 348 us -> 87.1 us (0.25); the launches traced: 343 us -> 86.7 us
  local copies, waits for them, and re-layouts: 186 us -> 2.7 us
  other arithmetic: 47.4 us -> 0 us
  Pallas kernels: 0 us -> 44.2 us
  waiting for transfers between devices: 43.5 us -> 13.4 us
  loops' own time: 27.8 us -> 0 us
  starting transfers between devices: 34.4 us -> 12.1 us
  blocking collectives: 0 us -> 13.7 us
    dynamic_update_slice x20 -> x0, local copies, waits for them, and re-layouts: 103 us -> none  [the longest x16 73 us: add_band(): lax.dynamic_update_slice_in_dim(whole, current + arrived[index], starts[i...]
    pallas_call x0 -> x4, Pallas kernels: none -> 44.2 us  [the longest x1 23.2 us: shards(): pl.pallas_call(functools.partial(diffuse_kernel, groups), out_shape=[stru...]
    slice x52 -> x0, local copies, waits for them, and re-layouts: 38.2 us -> none  [the longest x4 8.08 us: band_margin(): edges = jnp.concatenate([wide[:, :depth], lower], 1)]
    all_to_all x2 -> x1, waiting for transfers between devices: 34.1 us -> 2.85 us  [shards(): lax.all_to_all(bands, 'band', split_axis=0, concat_axis=0, tiled=True)]
    another operation x1 -> x0, loops' own time: 27.8 us -> none  [place_rows(): whole = lax.fori_loop(0, count, add_band, empty)]
    dynamic_slice x19 -> x0, local copies, waits for them, and re-layouts: 15.5 us -> none  [the longest x16 9.25 us: add_band(): current = lax.dynamic_slice_in_dim(whole, starts[index], height, 2)]
    mul x11 -> x0, other arithmetic: 14.1 us -> none  [the longest x8 9.39 us: spread(): flux_x = along_x * (jnp.roll(field, -1, x_axis) - field)]
    all_to_all x0 -> x1, blocking collectives: none -> 13.7 us  [shards(): lax.all_to_all(parted, 'band', split_axis=0, concat_axis=0, tiled=True, a...]
  transfers between devices with their start and end apart: 14 -> 6, of which waited for: 8 -> 6; matrix products, arithmetic and copies ran while one was open for 14% -> 1% of each run, Pallas kernels for 0% -> 2%
where the time goes in v1:
time: 87.1 us; the launch traced here: 86.7 us
  Pallas kernels  44.2 us (51%)
  blocking collectives  13.7 us (16%)
  waiting for transfers between devices  13.4 us (15%)
  starting transfers between devices  12.1 us (14%)
  local copies, waits for them, and re-layouts  2.7 us (3%)
    pallas_call x1, Pallas kernels, shards(): pl.pallas_call(functools.partial(diffuse_kernel, groups), out_shape=[stru...  23.2 us
    pallas_call x1, Pallas kernels, shards(): pl.pallas_call(regroup_kernel, out_shape=struct(groups, channels, width,...  17.1 us
    all_to_all x1, blocking collectives, shards(): lax.all_to_all(parted, 'band', split_axis=0, concat_axis=0, tiled=True, a...  13.7 us
    ppermute x3, waiting for transfers between devices, shards(): lax.ppermute(strips[k], 'band', [(i, i ^ k) for i in range(count)])  5.05 us
    all_to_all x1, starting transfers between devices, shards(): lax.all_to_all(bands, 'band', split_axis=0, concat_axis=0, tiled=True)  4.91 us
    ppermute x1, waiting for transfers between devices, shards(): low = lax.ppermute(mine[groups - 1], axes, shifted(groups))  3.94 us
    ppermute x3, starting transfers between devices, shards(): lax.ppermute(strips[k], 'band', [(i, i ^ k) for i in range(count)])  3.55 us
    all_to_all x1, waiting for transfers between devices, shards(): lax.all_to_all(bands, 'band', split_axis=0, concat_axis=0, tiled=True)  2.85 us
  transfers between devices with their start and end apart: 6, of which 6 were waited for; matrix products, arithmetic and copies ran while one was open for 1% of the time, Pallas kernels for 2%

profile of v1, /device:TPU:0, one launch (start us, length us, event | category | flops | bytes accessed | tf_op | source)
XLA Modules:
  0.0 86.7 jit_solution(1888410300564598344)
XLA Ops:
  0.6 17.1 %regroup.1 = f32[4,16,8,256]{3,2,1,0:T(8,128)} custom-call(f32[2,16,8,256]{3,2,1,0:T(8,128)} %background.1, f32[16,8,256]{2,1,0:T(8,128)} %scale_x.1, f32[16,8,256]{2,1,0:T(8,128)} %scale_y.1), custom_call_target="tpu_custom_call" | custom-call | tf_op jit(solution)/shard_map/regroup/pallas_call | solution.py:153
  17.8 13.7 %all_to_all.10.mine = f32[4,16,8,256]{3,2,1,0:T(8,128)S(1)} all-to-all(f32[4,16,8,256]{3,2,1,0:T(8,128)} %regroup.1), channel_id=1, replica_groups={{0,2,4,6},{8,10,12,14},{16,18,20,22},{24,26,28,30},{1,3,5,7},{9,11,13,1..., dimensions={0} | all-to-all | bytes 1048576 | tf_op jit(solution)/shard_map/all_to_all | solution.py:162
  31.5 0.0 copy-start
  31.5 1.6 %collective-permute-start = (f32[16,8,256]{2,1,0:T(8,128)S(1)}, f32[16,8,256]{2,1,0:T(8,128)S(1)}, u32[]{:S(2)}, u32[]{:S(2)}) collective-permute-start(f32[16,8,256]{2,1,0:T(8,128)S(1)} %get-tuple-element.13), channel_id=1, source_target_pairs={{0,8},{2,10},{4,12},{6,14},{8,16},{10,18},{12,20},{14,22},{16,24},... | collective-permute-start | bytes 393224 | tf_op jit(solution)/shard_map/ppermute | solution.py:180
  33.1 2.0 %collective-permute-start.1 = (f32[16,8,256]{2,1,0:T(8,128)S(1)}, f32[16,8,256]{2,1,0:T(8,128)S(1)}, u32[]{:S(2)}, u32[]{:S(2)}) collective-permute-start(f32[16,8,256]{2,1,0:T(8,128)S(1)} %get-tuple-element.12), channel_id=1, source_target_pairs={{0,25},{2,27},{4,29},{6,31},{8,0},{10,2},{12,4},{14,6},{16,8},{18,... | collective-permute-start | bytes 393224 | tf_op jit(solution)/shard_map/ppermute | solution.py:181
  35.1 3.9 %collective-permute-done.low = f32[16,8,256]{2,1,0:T(8,128)S(1)} collective-permute-done((f32[16,8,256]{2,1,0:T(8,128)S(1)}, f32[16,8,256]{2,1,0:T(8,128)S(1)}, u32[]{:S(2)}, u32[]{:S(2)}) %collective-permute-start) | collective-permute-done | bytes 131104 | tf_op jit(solution)/shard_map/ppermute | solution.py:180
  39.0 0.0 copy-start.2
  39.0 1.5 %collective-permute-done.1.high = f32[16,8,256]{2,1,0:T(8,128)S(1)} collective-permute-done((f32[16,8,256]{2,1,0:T(8,128)S(1)}, f32[16,8,256]{2,1,0:T(8,128)S(1)}, u32[]{:S(2)}, u32[]{:S(2)}) %collective-permute-start.1) | collective-permute-done | bytes 131104 | tf_op jit(solution)/shard_map/ppermute | solution.py:181
  40.5 0.0 copy-done
  40.5 0.0 copy-done.2
  40.5 0.0 copy-start.3
  40.5 0.6 copy-done.3
  41.2 23.2 %diffuse.1 = (f32[16,2,32,128]{3,2,1,0:T(8,128)}, f32[8,8,256]{2,1,0:T(8,128)}, f32[8,8,256]{2,1,0:T(8,128)}, f32[8,8,256]{2,1,0:T(8,128)}, f32[8,8,256]{2,1,0:T(8,128)}) custom-call(s32[16]{0:T(128)} %band_rows.3, f32[16,8,256]{2,1,0:T(8,128)} %copy-done.2, f32[4,16,8,256]{3,2,1,0:T(8,128)} %copy-done, f32[16,8,256]{2,1,0:T(8,128)} %copy-done.3), custom_call_target="tpu_custom_call" | custom-call | tf_op jit(solution)/shard_map/diffuse/pallas_call | solution.py:184
  64.4 0.0 copy-start.10
  64.4 0.0 copy-start.9
  64.4 0.0 copy-start.8
  64.4 4.9 %all-to-all-start.1 = ((f32[16,2,32,128]{3,2,1,0:T(8,128)}), f32[16,2,32,128]{3,2,1,0:T(8,128)S(1)}, u32[]{:S(2)}, u32[]{:S(2)}) async-start(f32[16,2,32,128]{3,2,1,0:T(8,128)} %get-tuple-element.11), calls=%async_computation.1 | async-start | bytes 1048576 | tf_op jit(solution)/shard_map/all_to_all | solution.py:195
  69.3 0.0 copy-start.7
  69.3 0.0 copy-done.10
  69.4 2.0 %collective-permute-start.2 = (f32[8,8,256]{2,1,0:T(8,128)S(1)}, f32[8,8,256]{2,1,0:T(8,128)S(1)}, u32[]{:S(2)}, u32[]{:S(2)}) collective-permute-start(f32[8,8,256]{2,1,0:T(8,128)S(1)} %copy-done.10), channel_id=1, source_target_pairs={{0,2},{2,0},{4,6},{6,4},{8,10},{10,8},{12,14},{14,12},{16,18},{18,... | collective-permute-start | bytes 196616 | tf_op jit(solution)/shard_map/ppermute | solution.py:197
  71.3 0.0 copy-done.9
  71.3 1.5 %collective-permute-start.3 = (f32[8,8,256]{2,1,0:T(8,128)S(1)}, f32[8,8,256]{2,1,0:T(8,128)S(1)}, u32[]{:S(2)}, u32[]{:S(2)}) collective-permute-start(f32[8,8,256]{2,1,0:T(8,128)S(1)} %copy-done.9), channel_id=1, source_target_pairs={{0,4},{2,6},{4,0},{6,2},{8,12},{10,14},{12,8},{14,10},{16,20},{18,... | collective-permute-start | bytes 196616 | tf_op jit(solution)/shard_map/ppermute | solution.py:197
  72.8 0.0 copy-done.8
  72.8 0.1 collective-permute-start.4
  72.9 0.0 copy-done.7
  72.9 0.6 copy.7.weights
  73.5 2.0 %collective-permute-done.2.refs_1_ = f32[8,8,256]{2,1,0:T(8,128)S(1)} collective-permute-done((f32[8,8,256]{2,1,0:T(8,128)S(1)}, f32[8,8,256]{2,1,0:T(8,128)S(1)}, u32[]{:S(2)}, u32[]{:S(2)}) %collective-permute-start.2) | collective-permute-done | bytes 65568 | tf_op jit(solution)/shard_map/ppermute | solution.py:197
  75.6 0.0 copy-start.4
  75.6 1.9 %collective-permute-done.3.refs_2_ = f32[8,8,256]{2,1,0:T(8,128)S(1)} collective-permute-done((f32[8,8,256]{2,1,0:T(8,128)S(1)}, f32[8,8,256]{2,1,0:T(8,128)S(1)}, u32[]{:S(2)}, u32[]{:S(2)}) %collective-permute-start.3) | collective-permute-done | bytes 65568 | tf_op jit(solution)/shard_map/ppermute | solution.py:197
  77.4 0.0 copy-start.5
  77.4 1.1 %collective-permute-done.4.refs_3_ = f32[8,8,256]{2,1,0:T(8,128)S(1)} collective-permute-done((f32[8,8,256]{2,1,0:T(8,128)S(1)}, f32[8,8,256]{2,1,0:T(8,128)S(1)}, u32[]{:S(2)}, u32[]{:S(2)}) %collective-permute-start.4) | collective-permute-done | bytes 65568 | tf_op jit(solution)/shard_map/ppermute | solution.py:197
  78.6 0.0 copy-start.6
  78.6 0.0 copy-done.4
  78.6 0.0 copy-done.5
  78.6 0.6 copy-done.6
  79.2 1.8 %increment.1 = f32[2,16,8,256]{3,2,1,0:T(8,128)} custom-call(f32[2,5,16]{2,1,0:T(8,128)} %copy.7.weights, f32[8,8,256]{2,1,0:T(8,128)} %get-tuple-element.7.refs_0_, f32[8,8,256]{2,1,0:T(8,128)} %copy-done.4, f32[8,8,256]{2,1,0:T(8,128)} %copy-done.5, f32[8,8,256]{2,1,0:T(8,128)} %copy-done.6), custom_call_target="tpu_custom_call" | custom-call | tf_op jit(solution)/shard_map/increment/pallas_call | solution.py:200
  81.0 2.9 %all-to-all-done.1.arrived = f32[16,2,32,128]{3,2,1,0:T(8,128)S(1)} async-done(((f32[16,2,32,128]{3,2,1,0:T(8,128)}), f32[16,2,32,128]{3,2,1,0:T(8,128)S(1)}, u32[]{:S(2)}, u32[]{:S(2)}) %all-to-all-start.1) | async-done | bytes 524320 | tf_op jit(solution)/shard_map/all_to_all | solution.py:195
  83.8 0.0 copy-start.1
  83.8 0.8 copy-done.1
  84.6 2.1 %bands.1 = f32[2,16,32,128]{3,2,1,0:T(8,128)} custom-call(s32[16]{0:T(128)} %band_rows.3, f32[2,5,16]{2,1,0:T(8,128)} %copy.7.weights, f32[16,2,32,128]{3,2,1,0:T(8,128)} %copy-done.1), custom_call_target="tpu_custom_call" | custom-call | tf_op jit(solution)/shard_map/bands/pallas_call | solution.py:208
  (1 shorter events, 0.0 us)
Async XLA Ops:
  31.5 9.1 %copy-start = (f32[4,16,8,256]{3,2,1,0:T(8,128)}, f32[4,16,8,256]{3,2,1,0:T(8,128)S(1)}, u32[]{:S(2)}) copy-start(f32[4,16,8,256]{3,2,1,0:T(8,128)S(1)} %all_to_all.10.mine) | copy-start | bytes 1572868
  31.5 7.5 %collective-permute-start = (f32[16,8,256]{2,1,0:T(8,128)S(1)}, f32[16,8,256]{2,1,0:T(8,128)S(1)}, u32[]{:S(2)}, u32[]{:S(2)}) collective-permute-start(f32[16,8,256]{2,1,0:T(8,128)S(1)} %get-tuple-element.13), channel_id=1, source_target_pairs={{0,8},{2,10},{4,12},{6,14},{8,16},{10,18},{12,20},{14,22},{16,24},... | collective-permute-start | bytes 393224 | tf_op jit(solution)/shard_map/ppermute | solution.py:180
  33.1 7.4 %collective-permute-start.1 = (f32[16,8,256]{2,1,0:T(8,128)S(1)}, f32[16,8,256]{2,1,0:T(8,128)S(1)}, u32[]{:S(2)}, u32[]{:S(2)}) collective-permute-start(f32[16,8,256]{2,1,0:T(8,128)S(1)} %get-tuple-element.12), channel_id=1, source_target_pairs={{0,25},{2,27},{4,29},{6,31},{8,0},{10,2},{12,4},{14,6},{16,8},{18,... | collective-permute-start | bytes 393224 | tf_op jit(solution)/shard_map/ppermute | solution.py:181
  39.0 1.5 %copy-start.2 = (f32[16,8,256]{2,1,0:T(8,128)}, f32[16,8,256]{2,1,0:T(8,128)S(1)}, u32[]{:S(2)}) copy-start(f32[16,8,256]{2,1,0:T(8,128)S(1)} %collective-permute-done.low) | copy-start | bytes 393220
  40.5 0.6 copy-start.3
  64.4 4.9 %copy-start.10 = (f32[8,8,256]{2,1,0:T(8,128)S(1)}, f32[8,8,256]{2,1,0:T(8,128)}, u32[]{:S(2)}) copy-start(f32[8,8,256]{2,1,0:T(8,128)} %get-tuple-element.8) | copy-start | bytes 196612
  64.4 6.9 %copy-start.9 = (f32[8,8,256]{2,1,0:T(8,128)S(1)}, f32[8,8,256]{2,1,0:T(8,128)}, u32[]{:S(2)}) copy-start(f32[8,8,256]{2,1,0:T(8,128)} %get-tuple-element.9) | copy-start | bytes 196612
  64.4 8.4 %copy-start.8 = (f32[8,8,256]{2,1,0:T(8,128)S(1)}, f32[8,8,256]{2,1,0:T(8,128)}, u32[]{:S(2)}) copy-start(f32[8,8,256]{2,1,0:T(8,128)} %get-tuple-element.10) | copy-start | bytes 196612
  64.4 19.4 %all-to-all-start.1 = ((f32[16,2,32,128]{3,2,1,0:T(8,128)}), f32[16,2,32,128]{3,2,1,0:T(8,128)S(1)}, u32[]{:S(2)}, u32[]{:S(2)}) async-start(f32[16,2,32,128]{3,2,1,0:T(8,128)} %get-tuple-element.11), calls=%async_computation.1 | async-start | bytes 1048576 | tf_op jit(solution)/shard_map/all_to_all | solution.py:195
  69.3 3.6 %copy-start.7 = (f32[2,5,16]{2,0,1:T(2,128)S(1)}, f32[2,5,16]{2,0,1:T(2,128)}, u32[]{:S(2)}) copy-start(f32[2,5,16]{2,0,1:T(2,128)} %param.8) | copy-start | bytes 1924
  69.4 6.2 %collective-permute-start.2 = (f32[8,8,256]{2,1,0:T(8,128)S(1)}, f32[8,8,256]{2,1,0:T(8,128)S(1)}, u32[]{:S(2)}, u32[]{:S(2)}) collective-permute-start(f32[8,8,256]{2,1,0:T(8,128)S(1)} %copy-done.10), channel_id=1, source_target_pairs={{0,2},{2,0},{4,6},{6,4},{8,10},{10,8},{12,14},{14,12},{16,18},{18,... | collective-permute-start | bytes 196616 | tf_op jit(solution)/shard_map/ppermute | solution.py:197
  71.3 6.1 %collective-permute-start.3 = (f32[8,8,256]{2,1,0:T(8,128)S(1)}, f32[8,8,256]{2,1,0:T(8,128)S(1)}, u32[]{:S(2)}, u32[]{:S(2)}) collective-permute-start(f32[8,8,256]{2,1,0:T(8,128)S(1)} %copy-done.9), channel_id=1, source_target_pairs={{0,4},{2,6},{4,0},{6,2},{8,12},{10,14},{12,8},{14,10},{16,20},{18,... | collective-permute-start | bytes 196616 | tf_op jit(solution)/shard_map/ppermute | solution.py:197
  72.8 5.8 %collective-permute-start.4 = (f32[8,8,256]{2,1,0:T(8,128)S(1)}, f32[8,8,256]{2,1,0:T(8,128)S(1)}, u32[]{:S(2)}, u32[]{:S(2)}) collective-permute-start(f32[8,8,256]{2,1,0:T(8,128)S(1)} %copy-done.8), channel_id=1, source_target_pairs={{0,6},{2,4},{4,2},{6,0},{8,14},{10,12},{12,10},{14,8},{16,22},{18,... | collective-permute-start | bytes 196616 | tf_op jit(solution)/shard_map/ppermute | solution.py:197
  75.6 3.0 %copy-start.4 = (f32[8,8,256]{2,1,0:T(8,128)}, f32[8,8,256]{2,1,0:T(8,128)S(1)}, u32[]{:S(2)}) copy-start(f32[8,8,256]{2,1,0:T(8,128)S(1)} %collective-permute-done.2.refs_1_) | copy-start | bytes 196612
  77.4 1.2 %copy-start.5 = (f32[8,8,256]{2,1,0:T(8,128)}, f32[8,8,256]{2,1,0:T(8,128)S(1)}, u32[]{:S(2)}) copy-start(f32[8,8,256]{2,1,0:T(8,128)S(1)} %collective-permute-done.3.refs_2_) | copy-start | bytes 196612
  78.6 0.6 copy-start.6
  83.8 0.8 copy-start.1

commit v2 on v1

--- a/solution.py
+++ b/solution.py
@@ -12,72 +12,70 @@
 CAP = 32
 LANES = 128
 TAPS = 5
+BLOCK = 16
+UNROLL = 4
 VMEM = pl.BlockSpec(memory_space=pltpu.VMEM)
 SMEM = pl.BlockSpec(memory_space=pltpu.SMEM)
-ANY = pl.BlockSpec(memory_space=pl.ANY)
-
-
-def regroup_kernel(background, scale_x, scale_y, out, sems):
+
+
+def regroup_kernel(background, scale_x, scale_y, out):
     variables, levels = background.shape[:2]
     groups = out.shape[0]
     part = levels // groups
-    copies = []
     for q in range(groups):
         near = pl.ds(q * part, part)
-        sources = [background.at[v, near] for v in range(variables)]
-        sources += [scale_x.at[near], scale_y.at[near]]
-        for i, source in enumerate(sources):
-            copies.append(
-                pltpu.make_async_copy(source, out.at[q, pl.ds(i * part, part)], sems.at[q, i])
-            )
-    for copy in copies:
-        copy.start()
-    for copy in copies:
-        copy.wait()
-
-
-def diffuse_kernel(
-    groups, band_rows, low, mine, high, bands, *rest
-):
-    strips, field, along_x, along_y, result = rest[:groups], *rest[groups:]
-    _, channels, width, rows = mine.shape
+        sources = [background[v, near] for v in range(variables)]
+        sources += [scale_x[near], scale_y[near]]
+        out[q] = jnp.swapaxes(jnp.concatenate(sources, 0), 0, 1)
+
+
+def diffuse_kernel(groups, band_rows, low, mine, high, bands, *rest):
+    strips, field, along_x, along_y, down_y, result = rest[:groups], *rest[groups:]
+    _, width, channels, rows = mine.shape
     part = channels // 4
     pairs = 2 * part
     sources = [low] + [mine.at[s] for s in range(groups)] + [high]
     columns = len(sources) * width
-    inside = lax.broadcasted_iota(jnp.int32, (pairs, rows), 1) < rows - 1
+    upper = lax.broadcasted_iota(jnp.int32, (1, pairs, rows), 1) < part
+    inside = lax.broadcasted_iota(jnp.int32, (1, pairs, rows), 2) < rows - 1
     for s, source in enumerate(sources):
-        flow = jnp.swapaxes(source[...], 0, 1)
-        field[pl.ds(s * width, width)] = flow[:, :pairs]
-        coef_x = flow[:, pairs : pairs + part]
-        coef_y = flow[:, pairs + part :]
-        along_x[pl.ds(s * width, width)] = jnp.concatenate([coef_x, coef_x], 1)
-        coef_y = jnp.concatenate([coef_y, coef_y], 1)
-        along_y[pl.ds(s * width, width)] = jnp.where(inside[None], coef_y, 0.0)
+        near = pl.ds(s * width, width)
+        field[near] = source[:, :pairs]
+        coefs = source[:, pairs:]
+        swapped = pltpu.roll(coefs, part, 1)
+        along_x[near] = jnp.where(upper, coefs, swapped)
+        flow_y = jnp.where(inside, jnp.where(upper, swapped, coefs), 0.0)
+        along_y[near] = flow_y
+        down_y[near] = pltpu.roll(flow_y, 1, 2)
 
     for step in range(STEPS):
         first, last = step + 1, columns - 1 - step
-        here = field[first]
-        before = along_x[first - 1] * (here - field[first - 1])
-        for c in range(first, last):
-            after = field[c + 1]
-            flux_x = along_x[c] * (after - here)
-            flux_y = along_y[c] * (pltpu.roll(here, rows - 1, 1) - here)
-            field[c] = here + flux_x - before + flux_y - pltpu.roll(flux_y, 1, 1)
-            here, before = after, flux_x
+        before = along_x[first - 1] * (field[first] - field[first - 1])
+        for c in range(first, last, BLOCK):
+            m = min(BLOCK, last - c)
+            near = pl.ds(c, m)
+            both = field[pl.ds(c, m + 1)]
+            here, after = both[:m], both[1:]
+            flux_x = along_x[near] * (after - here)
+            left = jnp.concatenate([before[None], flux_x[:-1]], 0)
+            flux_y = along_y[near] * (pltpu.roll(here, rows - 1, 2) - here)
+            under = down_y[near] * (here - pltpu.roll(here, 1, 2))
+            field[near] = here + flux_x - left + flux_y - under
+            before = flux_x[m - 1]
 
     me = lax.rem(lax.axis_index("band"), groups)
+    halves = rows // LANES
     for s in range(groups):
         block = jnp.swapaxes(field[pl.ds((s + 1) * width, width)], 0, 1)
-        for half in range(rows // LANES):
+        for half in range(halves):
             result[half, :, pl.ds(s * width, width)] = block[:, :, half * LANES : (half + 1) * LANES]
-        strips_block = block
-        for k in range(groups):
-            @pl.when(jnp.bitwise_xor(me, k) == s)
-            def _(k=k, strips_block=strips_block):
-                strips[k][...] = strips_block
-
-    halves = rows // LANES
+    for k in range(groups):
+        s = jnp.bitwise_xor(me, k)
+        for half in range(halves):
+            strips[k][:, :, half * LANES : (half + 1) * LANES] = result[
+                half, :, pl.ds(pl.multiple_of(s * width, width), width)
+            ]
+
     lane = lax.broadcasted_iota(jnp.int32, (groups * width, LANES), 1)
 
     def one_band(b, start):
@@ -95,7 +93,7 @@
             bands[b, v] = packed
         return start + band_rows[b]
 
-    lax.fori_loop(0, bands.shape[0], one_band, jnp.int32(0))
+    lax.fori_loop(0, bands.shape[0], one_band, jnp.int32(0), unroll=UNROLL)
 
 
 def filtered(weights, v, l, levels, at):
@@ -152,10 +150,9 @@
 
     parted = pl.pallas_call(
         regroup_kernel,
-        out_shape=struct(groups, channels, width, rows),
-        in_specs=[ANY] * 3,
-        out_specs=ANY,
-        scratch_shapes=[pltpu.SemaphoreType.DMA((groups, variables + 2))],
+        out_shape=struct(groups, width, channels, rows),
+        in_specs=[VMEM] * 3,
+        out_specs=VMEM,
         name="regroup",
     )(background, scale_x, scale_y)
     near = [[g * groups + i for i in range(groups)] for g in range(count // groups)]
@@ -187,7 +184,7 @@
         + [struct(variables * part, width, rows)] * groups,
         in_specs=[SMEM] + [VMEM] * 3,
         out_specs=[VMEM] * (groups + 1),
-        scratch_shapes=[pltpu.VMEM((wide, variables * part, rows), f32)] * 3
+        scratch_shapes=[pltpu.VMEM((wide, variables * part, rows), f32)] * 4
         + [pltpu.VMEM((rows // LANES, variables * part, span, LANES), f32)],
         name="diffuse",
     )(band_rows, low, mine, high)

time: 87.1 us -> 53.2 us (0.61)
  Pallas kernels: 44.2 us -> 10.3 us
    pallas_call x1, Pallas kernels: 23.2 us -> 4.51 us  [shards(): pl.pallas_call(functools.partial(diffuse_kernel, groups), out_shape=[stru...]
    pallas_call x1, Pallas kernels: 17.1 us -> 1.93 us  [shards(): pl.pallas_call(regroup_kernel, out_shape=struct(groups, width, channels,...]
  transfers between devices with their start and end apart: 6 -> 6, of which waited for: 6 -> 6; matrix products, arithmetic and copies ran while one was open for 1% -> 1% of each run, Pallas kernels for 2% -> 3%
where the time goes in v2:
time: 53.2 us; the launch traced here: 52.8 us
  blocking collectives  13.7 us (26%)
  waiting for transfers between devices  13.4 us (25%)
  starting transfers between devices  12.1 us (23%)
  Pallas kernels  10.3 us (19%)
  local copies, waits for them, and re-layouts  2.7 us (5%)
  between operations  0.69 us (1%)
    all_to_all x1, blocking collectives, shards(): lax.all_to_all(parted, 'band', split_axis=0, concat_axis=0, tiled=True, a...  13.7 us
    ppermute x3, waiting for transfers between devices, shards(): lax.ppermute(strips[k], 'band', [(i, i ^ k) for i in range(count)])  5.05 us
    all_to_all x1, starting transfers between devices, shards(): lax.all_to_all(bands, 'band', split_axis=0, concat_axis=0, tiled=True)  4.91 us
    pallas_call x1, Pallas kernels, shards(): pl.pallas_call(functools.partial(diffuse_kernel, groups), out_shape=[stru...  4.51 us
    ppermute x1, waiting for transfers between devices, shards(): low = lax.ppermute(mine[groups - 1], axes, shifted(groups))  3.94 us
    ppermute x3, starting transfers between devices, shards(): lax.ppermute(strips[k], 'band', [(i, i ^ k) for i in range(count)])  3.55 us
    all_to_all x1, waiting for transfers between devices, shards(): lax.all_to_all(bands, 'band', split_axis=0, concat_axis=0, tiled=True)  2.85 us
    unnamed x23, local copies, waits for them, and re-layouts  2.68 us
  transfers between devices with their start and end apart: 6, of which 6 were waited for; matrix products, arithmetic and copies ran while one was open for 1% of the time, Pallas kernels for 3%

profile of v2, /device:TPU:0, one launch (start us, length us, event | category | flops | bytes accessed | tf_op | source)
XLA Modules:
  0.0 52.8 jit_solution(14431491813099321451)
XLA Ops:
  0.6 1.9 %regroup.1 = f32[4,8,16,256]{3,2,1,0:T(8,128)} custom-call(f32[2,16,8,256]{3,2,1,0:T(8,128)} %background.1, f32[16,8,256]{2,1,0:T(8,128)} %scale_x.1, f32[16,8,256]{2,1,0:T(8,128)} %scale_y.1), custom_call_target="tpu_custom_call" | custom-call | tf_op jit(solution)/shard_map/regroup/pallas_call | solution.py:151
  2.6 13.7 %all_to_all.10.mine = f32[4,8,16,256]{3,2,1,0:T(8,128)S(1)} all-to-all(f32[4,8,16,256]{3,2,1,0:T(8,128)} %regroup.1), channel_id=1, replica_groups={{0,2,4,6},{8,10,12,14},{16,18,20,22},{24,26,28,30},{1,3,5,7},{9,11,13,1..., dimensions={0} | all-to-all | bytes 1048576 | tf_op jit(solution)/shard_map/all_to_all | solution.py:159
  16.2 0.0 copy-start
  16.3 1.6 %collective-permute-start = (f32[8,16,256]{2,1,0:T(8,128)S(1)}, f32[8,16,256]{2,1,0:T(8,128)S(1)}, u32[]{:S(2)}, u32[]{:S(2)}) collective-permute-start(f32[8,16,256]{2,1,0:T(8,128)S(1)} %get-tuple-element.13), channel_id=1, source_target_pairs={{0,8},{2,10},{4,12},{6,14},{8,16},{10,18},{12,20},{14,22},{16,24},... | collective-permute-start | bytes 393224 | tf_op jit(solution)/shard_map/ppermute | solution.py:177
  17.9 2.0 %collective-permute-start.1 = (f32[8,16,256]{2,1,0:T(8,128)S(1)}, f32[8,16,256]{2,1,0:T(8,128)S(1)}, u32[]{:S(2)}, u32[]{:S(2)}) collective-permute-start(f32[8,16,256]{2,1,0:T(8,128)S(1)} %get-tuple-element.12), channel_id=1, source_target_pairs={{0,25},{2,27},{4,29},{6,31},{8,0},{10,2},{12,4},{14,6},{16,8},{18,... | collective-permute-start | bytes 393224 | tf_op jit(solution)/shard_map/ppermute | solution.py:178
  19.9 3.9 %collective-permute-done.low = f32[8,16,256]{2,1,0:T(8,128)S(1)} collective-permute-done((f32[8,16,256]{2,1,0:T(8,128)S(1)}, f32[8,16,256]{2,1,0:T(8,128)S(1)}, u32[]{:S(2)}, u32[]{:S(2)}) %collective-permute-start) | collective-permute-done | bytes 131104 | tf_op jit(solution)/shard_map/ppermute | solution.py:177
  23.8 0.0 copy-start.2
  23.8 1.5 %collective-permute-done.1.high = f32[8,16,256]{2,1,0:T(8,128)S(1)} collective-permute-done((f32[8,16,256]{2,1,0:T(8,128)S(1)}, f32[8,16,256]{2,1,0:T(8,128)S(1)}, u32[]{:S(2)}, u32[]{:S(2)}) %collective-permute-start.1) | collective-permute-done | bytes 131104 | tf_op jit(solution)/shard_map/ppermute | solution.py:178
  25.3 0.0 copy-done
  25.3 0.0 copy-done.2
  25.3 0.0 copy-start.3
  25.3 0.6 %copy-done.3 = f32[8,16,256]{2,1,0:T(8,128)} copy-done((f32[8,16,256]{2,1,0:T(8,128)}, f32[8,16,256]{2,1,0:T(8,128)S(1)}, u32[]{:S(2)}) %copy-start.3) | copy-done | bytes 131096
  26.0 4.5 %diffuse.1 = (f32[16,2,32,128]{3,2,1,0:T(8,128)}, f32[8,8,256]{2,1,0:T(8,128)}, f32[8,8,256]{2,1,0:T(8,128)}, f32[8,8,256]{2,1,0:T(8,128)}, f32[8,8,256]{2,1,0:T(8,128)}) custom-call(s32[16]{0:T(128)} %band_rows.3, f32[8,16,256]{2,1,0:T(8,128)} %copy-done.2, f32[4,8,16,256]{3,2,1,0:T(8,128)} %copy-done, f32[8,16,256]{2,1,0:T(8,128)} %copy-done.3), custom_call_target="tpu_custom_call" | custom-call | tf_op jit(solution)/shard_map/diffuse/pallas_call | solution.py:181
  30.5 0.0 copy-start.10
  30.5 0.0 copy-start.9
  30.5 0.0 copy-start.8
  30.5 4.9 %all-to-all-start.1 = ((f32[16,2,32,128]{3,2,1,0:T(8,128)}), f32[16,2,32,128]{3,2,1,0:T(8,128)S(1)}, u32[]{:S(2)}, u32[]{:S(2)}) async-start(f32[16,2,32,128]{3,2,1,0:T(8,128)} %get-tuple-element.11), calls=%async_computation.1 | async-start | bytes 1048576 | tf_op jit(solution)/shard_map/all_to_all | solution.py:192
  35.4 0.0 copy-start.7
  35.4 0.0 copy-done.10
  35.4 2.0 %collective-permute-start.2 = (f32[8,8,256]{2,1,0:T(8,128)S(1)}, f32[8,8,256]{2,1,0:T(8,128)S(1)}, u32[]{:S(2)}, u32[]{:S(2)}) collective-permute-start(f32[8,8,256]{2,1,0:T(8,128)S(1)} %copy-done.10), channel_id=1, source_target_pairs={{0,2},{2,0},{4,6},{6,4},{8,10},{10,8},{12,14},{14,12},{16,18},{18,... | collective-permute-start | bytes 196616 | tf_op jit(solution)/shard_map/ppermute | solution.py:194
  37.4 0.0 copy-done.9
  37.4 1.5 %collective-permute-start.3 = (f32[8,8,256]{2,1,0:T(8,128)S(1)}, f32[8,8,256]{2,1,0:T(8,128)S(1)}, u32[]{:S(2)}, u32[]{:S(2)}) collective-permute-start(f32[8,8,256]{2,1,0:T(8,128)S(1)} %copy-done.9), channel_id=1, source_target_pairs={{0,4},{2,6},{4,0},{6,2},{8,12},{10,14},{12,8},{14,10},{16,20},{18,... | collective-permute-start | bytes 196616 | tf_op jit(solution)/shard_map/ppermute | solution.py:194
  38.9 0.0 copy-done.8
  38.9 0.1 collective-permute-start.4
  39.0 0.0 copy-done.7
  39.0 0.6 %copy.7.weights = f32[2,5,16]{2,1,0:T(8,128)} copy(f32[2,5,16]{2,0,1:T(2,128)S(1)} %copy-done.7) | data formatting | bytes 1280 | tf_op args[3]
  39.6 2.0 %collective-permute-done.2.refs_1_ = f32[8,8,256]{2,1,0:T(8,128)S(1)} collective-permute-done((f32[8,8,256]{2,1,0:T(8,128)S(1)}, f32[8,8,256]{2,1,0:T(8,128)S(1)}, u32[]{:S(2)}, u32[]{:S(2)}) %collective-permute-start.2) | collective-permute-done | bytes 65568 | tf_op jit(solution)/shard_map/ppermute | solution.py:194
  41.6 0.0 copy-start.4
  41.6 1.9 %collective-permute-done.3.refs_2_ = f32[8,8,256]{2,1,0:T(8,128)S(1)} collective-permute-done((f32[8,8,256]{2,1,0:T(8,128)S(1)}, f32[8,8,256]{2,1,0:T(8,128)S(1)}, u32[]{:S(2)}, u32[]{:S(2)}) %collective-permute-start.3) | collective-permute-done | bytes 65568 | tf_op jit(solution)/shard_map/ppermute | solution.py:194
  43.5 0.0 copy-start.5
  43.5 1.1 %collective-permute-done.4.refs_3_ = f32[8,8,256]{2,1,0:T(8,128)S(1)} collective-permute-done((f32[8,8,256]{2,1,0:T(8,128)S(1)}, f32[8,8,256]{2,1,0:T(8,128)S(1)}, u32[]{:S(2)}, u32[]{:S(2)}) %collective-permute-start.4) | collective-permute-done | bytes 65568 | tf_op jit(solution)/shard_map/ppermute | solution.py:194
  44.7 0.0 copy-start.6
  44.7 0.0 copy-done.4
  44.7 0.0 copy-done.5
  44.7 0.6 %copy-done.6 = f32[8,8,256]{2,1,0:T(8,128)} copy-done((f32[8,8,256]{2,1,0:T(8,128)}, f32[8,8,256]{2,1,0:T(8,128)S(1)}, u32[]{:S(2)}) %copy-start.6) | copy-done | bytes 65560
  45.3 1.8 %increment.1 = f32[2,16,8,256]{3,2,1,0:T(8,128)} custom-call(f32[2,5,16]{2,1,0:T(8,128)} %copy.7.weights, f32[8,8,256]{2,1,0:T(8,128)} %get-tuple-element.7.refs_0_, f32[8,8,256]{2,1,0:T(8,128)} %copy-done.4, f32[8,8,256]{2,1,0:T(8,128)} %copy-done.5, f32[8,8,256]{2,1,0:T(8,128)} %copy-done.6), custom_call_target="tpu_custom_call" | custom-call | tf_op jit(solution)/shard_map/increment/pallas_call | solution.py:197
  47.1 2.9 %all-to-all-done.1.arrived = f32[16,2,32,128]{3,2,1,0:T(8,128)S(1)} async-done(((f32[16,2,32,128]{3,2,1,0:T(8,128)}), f32[16,2,32,128]{3,2,1,0:T(8,128)S(1)}, u32[]{:S(2)}, u32[]{:S(2)}) %all-to-all-start.1) | async-done | bytes 524320 | tf_op jit(solution)/shard_map/all_to_all | solution.py:192
  49.9 0.0 copy-start.1
  49.9 0.8 %copy-done.1 = f32[16,2,32,128]{3,2,1,0:T(8,128)} copy-done((f32[16,2,32,128]{3,2,1,0:T(8,128)}, f32[16,2,32,128]{3,2,1,0:T(8,128)S(1)}, u32[]{:S(2)}) %copy-start.1) | copy-done | bytes 524312
  50.7 2.1 %bands.1 = f32[2,16,32,128]{3,2,1,0:T(8,128)} custom-call(s32[16]{0:T(128)} %band_rows.3, f32[2,5,16]{2,1,0:T(8,128)} %copy.7.weights, f32[16,2,32,128]{3,2,1,0:T(8,128)} %copy-done.1), custom_call_target="tpu_custom_call" | custom-call | tf_op jit(solution)/shard_map/bands/pallas_call | solution.py:205
  (1 shorter events, 0.0 us)
Async XLA Ops:
  16.2 9.1 %copy-start = (f32[4,8,16,256]{3,2,1,0:T(8,128)}, f32[4,8,16,256]{3,2,1,0:T(8,128)S(1)}, u32[]{:S(2)}) copy-start(f32[4,8,16,256]{3,2,1,0:T(8,128)S(1)} %all_to_all.10.mine) | copy-start | bytes 1572868
  16.3 7.5 %collective-permute-start = (f32[8,16,256]{2,1,0:T(8,128)S(1)}, f32[8,16,256]{2,1,0:T(8,128)S(1)}, u32[]{:S(2)}, u32[]{:S(2)}) collective-permute-start(f32[8,16,256]{2,1,0:T(8,128)S(1)} %get-tuple-element.13), channel_id=1, source_target_pairs={{0,8},{2,10},{4,12},{6,14},{8,16},{10,18},{12,20},{14,22},{16,24},... | collective-permute-start | bytes 393224 | tf_op jit(solution)/shard_map/ppermute | solution.py:177
  17.9 7.4 %collective-permute-start.1 = (f32[8,16,256]{2,1,0:T(8,128)S(1)}, f32[8,16,256]{2,1,0:T(8,128)S(1)}, u32[]{:S(2)}, u32[]{:S(2)}) collective-permute-start(f32[8,16,256]{2,1,0:T(8,128)S(1)} %get-tuple-element.12), channel_id=1, source_target_pairs={{0,25},{2,27},{4,29},{6,31},{8,0},{10,2},{12,4},{14,6},{16,8},{18,... | collective-permute-start | bytes 393224 | tf_op jit(solution)/shard_map/ppermute | solution.py:178
  23.8 1.5 %copy-start.2 = (f32[8,16,256]{2,1,0:T(8,128)}, f32[8,16,256]{2,1,0:T(8,128)S(1)}, u32[]{:S(2)}) copy-start(f32[8,16,256]{2,1,0:T(8,128)S(1)} %collective-permute-done.low) | copy-start | bytes 393220
  25.3 0.6 %copy-start.3 = (f32[8,16,256]{2,1,0:T(8,128)}, f32[8,16,256]{2,1,0:T(8,128)S(1)}, u32[]{:S(2)}) copy-start(f32[8,16,256]{2,1,0:T(8,128)S(1)} %collective-permute-done.1.high) | copy-start | bytes 393220
  30.5 4.9 %copy-start.10 = (f32[8,8,256]{2,1,0:T(8,128)S(1)}, f32[8,8,256]{2,1,0:T(8,128)}, u32[]{:S(2)}) copy-start(f32[8,8,256]{2,1,0:T(8,128)} %get-tuple-element.8) | copy-start | bytes 196612
  30.5 6.9 %copy-start.9 = (f32[8,8,256]{2,1,0:T(8,128)S(1)}, f32[8,8,256]{2,1,0:T(8,128)}, u32[]{:S(2)}) copy-start(f32[8,8,256]{2,1,0:T(8,128)} %get-tuple-element.9) | copy-start | bytes 196612
  30.5 8.4 %copy-start.8 = (f32[8,8,256]{2,1,0:T(8,128)S(1)}, f32[8,8,256]{2,1,0:T(8,128)}, u32[]{:S(2)}) copy-start(f32[8,8,256]{2,1,0:T(8,128)} %get-tuple-element.10) | copy-start | bytes 196612
  30.5 19.4 %all-to-all-start.1 = ((f32[16,2,32,128]{3,2,1,0:T(8,128)}), f32[16,2,32,128]{3,2,1,0:T(8,128)S(1)}, u32[]{:S(2)}, u32[]{:S(2)}) async-start(f32[16,2,32,128]{3,2,1,0:T(8,128)} %get-tuple-element.11), calls=%async_computation.1 | async-start | bytes 1048576 | tf_op jit(solution)/shard_map/all_to_all | solution.py:192
  35.4 3.6 %copy-start.7 = (f32[2,5,16]{2,0,1:T(2,128)S(1)}, f32[2,5,16]{2,0,1:T(2,128)}, u32[]{:S(2)}) copy-start(f32[2,5,16]{2,0,1:T(2,128)} %param.8) | copy-start | bytes 1924
  35.4 6.2 %collective-permute-start.2 = (f32[8,8,256]{2,1,0:T(8,128)S(1)}, f32[8,8,256]{2,1,0:T(8,128)S(1)}, u32[]{:S(2)}, u32[]{:S(2)}) collective-permute-start(f32[8,8,256]{2,1,0:T(8,128)S(1)} %copy-done.10), channel_id=1, source_target_pairs={{0,2},{2,0},{4,6},{6,4},{8,10},{10,8},{12,14},{14,12},{16,18},{18,... | collective-permute-start | bytes 196616 | tf_op jit(solution)/shard_map/ppermute | solution.py:194
  37.4 6.1 %collective-permute-start.3 = (f32[8,8,256]{2,1,0:T(8,128)S(1)}, f32[8,8,256]{2,1,0:T(8,128)S(1)}, u32[]{:S(2)}, u32[]{:S(2)}) collective-permute-start(f32[8,8,256]{2,1,0:T(8,128)S(1)} %copy-done.9), channel_id=1, source_target_pairs={{0,4},{2,6},{4,0},{6,2},{8,12},{10,14},{12,8},{14,10},{16,20},{18,... | collective-permute-start | bytes 196616 | tf_op jit(solution)/shard_map/ppermute | solution.py:194
  38.9 5.8 %collective-permute-start.4 = (f32[8,8,256]{2,1,0:T(8,128)S(1)}, f32[8,8,256]{2,1,0:T(8,128)S(1)}, u32[]{:S(2)}, u32[]{:S(2)}) collective-permute-start(f32[8,8,256]{2,1,0:T(8,128)S(1)} %copy-done.8), channel_id=1, source_target_pairs={{0,6},{2,4},{4,2},{6,0},{8,14},{10,12},{12,10},{14,8},{16,22},{18,... | collective-permute-start | bytes 196616 | tf_op jit(solution)/shard_map/ppermute | solution.py:194
  41.6 3.0 %copy-start.4 = (f32[8,8,256]{2,1,0:T(8,128)}, f32[8,8,256]{2,1,0:T(8,128)S(1)}, u32[]{:S(2)}) copy-start(f32[8,8,256]{2,1,0:T(8,128)S(1)} %collective-permute-done.2.refs_1_) | copy-start | bytes 196612
  43.5 1.2 %copy-start.5 = (f32[8,8,256]{2,1,0:T(8,128)}, f32[8,8,256]{2,1,0:T(8,128)S(1)}, u32[]{:S(2)}) copy-start(f32[8,8,256]{2,1,0:T(8,128)S(1)} %collective-permute-done.3.refs_2_) | copy-start | bytes 196612
  44.7 0.6 %copy-start.6 = (f32[8,8,256]{2,1,0:T(8,128)}, f32[8,8,256]{2,1,0:T(8,128)S(1)}, u32[]{:S(2)}) copy-start(f32[8,8,256]{2,1,0:T(8,128)S(1)} %collective-permute-done.4.refs_3_) | copy-start | bytes 196612
  49.9 0.8 %copy-start.1 = (f32[16,2,32,128]{3,2,1,0:T(8,128)}, f32[16,2,32,128]{3,2,1,0:T(8,128)S(1)}, u32[]{:S(2)}) copy-start(f32[16,2,32,128]{3,2,1,0:T(8,128)S(1)} %all-to-all-done.1.arrived) | copy-start | bytes 1572868

commit v3 on v2

v3 whole, which is shorter than its diff:
```python
import functools
import math

import jax
import jax.numpy as jnp
from jax import lax
from jax.experimental import pallas as pl
from jax.experimental.pallas import tpu as pltpu
from jax.sharding import PartitionSpec as P

STEPS = 8
CAP = 32
LANES = 128
TAPS = 5
BLOCK = 16
UNROLL = 4
VMEM = pl.BlockSpec(memory_space=pltpu.VMEM)
SMEM = pl.BlockSpec(memory_space=pltpu.SMEM)
HBM = pl.BlockSpec(memory_space=pltpu.HBM)
ROOM = pltpu.CompilerParams(vmem_limit_bytes=8 * 2**20)


def regroup_kernel(background, scale_x, scale_y, out, field, along_x, along_y, sems):
    variables, levels = background.shape[:2]
    groups = out.shape[0]
    part = levels // groups
    copies = []
    for q in range(groups):
        near = pl.ds(q * part, part)
        copies.append(
            [
                pltpu.make_async_copy(background.at[:, near], field.at[:, near], sems.at[q, 0]),
                pltpu.make_async_copy(scale_x.at[near], along_x.at[near], sems.at[q, 1]),
                pltpu.make_async_copy(scale_y.at[near], along_y.at[near], sems.at[q, 2]),
            ]
        )
        for copy in copies[q]:
            copy.start()
    for q in range(groups):
        near = pl.ds(q * part, part)
        for copy in copies[q]:
            copy.wait()
        sources = [field[v, near] for v in range(variables)]
        sources += [along_x[near], along_y[near]]
        out[q] = jnp.swapaxes(jnp.concatenate(sources, 0), 0, 1)


def spread_out(source, near, field, along_x, along_y, down_y):
    _, channels, rows = source.shape
    part = channels // 4
    pairs = 2 * part
    upper = lax.broadcasted_iota(jnp.int32, (1, pairs, rows), 1) < part
    inside = lax.broadcasted_iota(jnp.int32, (1, pairs, rows), 2) < rows - 1
    field[near] = source[:, :pairs]
    coefs = source[:, pairs:]
    swapped = pltpu.roll(coefs, part, 1)
    along_x[near] = jnp.where(upper, coefs, swapped)
    flow_y = jnp.where(inside, jnp.where(upper, swapped, coefs), 0.0)
    along_y[near] = flow_y
    down_y[near] = pltpu.roll(flow_y, 1, 2)


def advance(field, along_x, along_y, down_y, first, last, before, behind):
    rows = field.shape[-1]
    if before is None:
        before = along_x[first - 1] * (field[first] - field[first - 1])
    entry = before
    for c in range(first, last, BLOCK):
        m = min(BLOCK, last - c)
        near = pl.ds(c, m)
        if c + m == last and behind is not None:
            here = field[near]
            after = here[1:]
            ahead = [along_x[pl.ds(c, m - 1)] * (after - here[:-1]), behind[None]]
            flux_x = jnp.concatenate(ahead, 0)
        else:
            both = field[pl.ds(c, m + 1)]
            here, after = both[:m], both[1:]
            flux_x = along_x[near] * (after - here)
        left = jnp.concatenate([before[None], flux_x[:-1]], 0)
        flux_y = along_y[near] * (pltpu.roll(here, rows - 1, 2) - here)
        under = down_y[near] * (here - pltpu.roll(here, 1, 2))
        field[near] = here + flux_x - left + flux_y - under
        before = flux_x[m - 1]
    return entry, before


def turn(columns, result, at):
    block = jnp.swapaxes(columns, 0, 1)
    for half in range(result.shape[0]):
        result[half, :, at] = block[:, :, half * LANES : (half + 1) * LANES]


def pack(result, band_rows, bands, at):
    halves, channels, count, _ = result.shape
    part = channels // 2
    lane = lax.broadcasted_iota(jnp.int32, (count, LANES), 1)

    def one_band(b, start):
        half = start // LANES
        offset = start - half * LANES
        beyond = lax.rem(half + 1, halves)
        for v in range(2):
            packed = None
            for l in range(part):
                i = v * part + l
                window = jnp.where(lane >= offset, result[half, i], result[beyond, i])
                shift = lax.rem(LANES + l * CAP - offset, LANES)
                turned = pltpu.roll(window, shift, 1)
                packed = turned if l == 0 else jnp.where(lane >= l * CAP, turned, packed)
            for source, target in at:
                bands[b, v, target] = packed[source]
        return start + band_rows[b]

    lax.fori_loop(0, bands.shape[0], one_band, jnp.int32(0), unroll=UNROLL)


def inner_kernel(band_rows, mine, field, along_x, along_y, down_y, sides, result, bands):
    groups, width, channels, rows = mine.shape
    for s in range(groups):
        spread_out(mine.at[s], pl.ds(s * width, width), field, along_x, along_y, down_y)
    span = groups * width
    for step in range(STEPS):
        entry, leave = advance(
            field, along_x, along_y, down_y, step + 1, span - 1 - step, None, None
        )
        sides[0, step] = entry
        sides[1, step] = leave
    for s in range(1, groups - 1):
        turn(field[pl.ds(s * width, width)], result, pl.ds((s - 1) * width, width))
    pack(result, band_rows, bands, [(slice(None), slice(None))])


def outer_kernel(groups, band_rows, low, high, *refs):
    inner, sides, inner_result, inner_bands, bands = refs[:4], *refs[4:8]
    strips = refs[8 : 8 + groups]
    ends, result, whole = refs[8 + groups : 12 + groups], *refs[12 + groups :]
    width, _, rows = low.shape
    span = groups * width
    for side, (halo, own) in enumerate(((low, 0), (high, span - width))):
        arrays = [end.at[side] for end in ends]
        spread_out(halo, pl.ds(side * width, width), *arrays)
        for end, array in zip(arrays, inner):
            end[pl.ds((1 - side) * width, width)] = array[pl.ds(own, width)]
    for step in range(STEPS):
        first = step + 1
        arrays = [end.at[0] for end in ends]
        advance(*arrays, first, first + width, None, sides[0, step])
        first = width - 1 - step
        arrays = [end.at[1] for end in ends]
        advance(*arrays, first, first + width, sides[1, step], None)
    field = ends[0]
    turn(field[0, pl.ds(width, width)], result, pl.ds(0, width))
    turn(field[1, pl.ds(0, width)], result, pl.ds(width, width))

    me = lax.rem(lax.axis_index("band"), groups)
    whole[:, :, pl.ds(width, span - 2 * width)] = inner_result[...]
    whole[:, :, pl.ds(0, width)] = result[:, :, pl.ds(0, width)]
    whole[:, :, pl.ds(span - width, width)] = result[:, :, pl.ds(width, width)]
    for k in range(groups):
        s = jnp.bitwise_xor(me, k)
        for half in range(rows // LANES):
            strips[k][:, :, half * LANES : (half + 1) * LANES] = whole[
                half, :, pl.ds(pl.multiple_of(s * width, width), width)
            ]

    bands[:, :, pl.ds(width, span - 2 * width)] = inner_bands[...]
    edges = [
        (slice(0, width), pl.ds(0, width)),
        (slice(width, 2 * width), pl.ds(span - width, width)),
    ]
    pack(result, band_rows, bands, edges)


def filtered(weights, v, l, levels, at):
    total = at(v, l)
    for tap in range(TAPS):
        other = l + tap - TAPS // 2
        if 0 <= other < levels:
            total = total + weights[tap, v, l] * at(v, other)
    return total


def increment_kernel(groups, weights, *refs):
    pieces, out, whole = refs[:groups], refs[groups], refs[groups + 1]
    variables, levels = out.shape[:2]
    part = levels // groups
    me = lax.rem(lax.axis_index("band"), groups)
    for k in range(groups):
        near = pl.ds(jnp.bitwise_xor(me, k) * part, part)
        for v in range(variables):
            whole[v, near] = pieces[k][pl.ds(v * part, part)]
    for v in range(variables):
        for l in range(levels):
            out[v, l] = filtered(weights, v, l, levels, lambda a, b: whole[a, b])


def band_kernel(groups, band_rows, weights, arrived, out, whole, ready, sems):
    variables, levels, height, columns = out.shape
    part = levels // groups
    count = arrived.shape[0]
    here = band_rows[lax.axis_index("band")]
    keep = lax.broadcasted_iota(jnp.int32, (height, columns), 0) < here
    copies = []
    for v in range(variables):
        for q in range(groups):
            tall = jnp.concatenate([arrived[s, v] for s in range(q, count, groups)], 0)
            flat = jnp.transpose(tall)
            for l in range(part):
                whole[v, q * part + l] = flat[l * height : (l + 1) * height]
        for l in range(levels):
            total = filtered(weights, v, l, levels, lambda a, b: whole[a, b])
            ready[v, l] = jnp.where(keep, total, 0.0)
        copies.append(pltpu.make_async_copy(ready.at[v], out.at[v], sems.at[v]))
        copies[v].start()
    for copy in copies:
        copy.wait()


def shards(mesh_shape, background, scale_x, scale_y, filter_bands, band_rows):
    variables, levels, width, rows = background.shape
    count, blocks = mesh_shape["band"], mesh_shape["lon"]
    groups = math.isqrt(count)
    part = levels // groups
    channels = (variables + 2) * part
    f32 = jnp.float32

    def struct(*shape):
        return jax.ShapeDtypeStruct(shape, f32)

    parted = pl.pallas_call(
        regroup_kernel,
        out_shape=struct(groups, width, channels, rows),
        in_specs=[HBM] * 3,
        out_specs=VMEM,
        scratch_shapes=[pltpu.VMEM(a.shape, f32) for a in (background, scale_x, scale_y)]
        + [pltpu.SemaphoreType.DMA((groups, 3))],
        compiler_params=ROOM,
        name="regroup",
    )(*(pltpu.with_memory_space_constraint(a, pltpu.HBM) for a in (background, scale_x, scale_y)))
    weights = jnp.transpose(filter_bands, (1, 0, 2))
    near = [[g * groups + i for i in range(groups)] for g in range(count // groups)]
    mine = lax.all_to_all(
        parted, "band", split_axis=0, concat_axis=0, tiled=True, axis_index_groups=near
    )

    def shifted(by):
        total = count * blocks
        pairs = []
        for source in range(total):
            target = (source + by) % total
            pairs.append(
                (
                    source % count * blocks + source // count,
                    target % count * blocks + target // count,
                )
            )
        return pairs

    axes = ("band", "lon")
    low = lax.ppermute(mine[groups - 1], axes, shifted(groups))
    high = lax.ppermute(mine[0], axes, shifted(-groups))
    span = groups * width
    inside = span - 2 * width
    halves = rows // LANES
    both = variables * part
    inner = pl.pallas_call(
        inner_kernel,
        out_shape=[struct(span, both, rows)] * 4
        + [
            struct(2, STEPS, both, rows),
            struct(halves, both, inside, LANES),
            struct(count, variables, inside, LANES),
        ],
        in_specs=[SMEM, VMEM],
        out_specs=[VMEM] * 7,
        compiler_params=ROOM,
        cost_estimate=pl.CostEstimate(
            flops=20 * STEPS * span * both * rows, bytes_accessed=2**20, transcendentals=0
        ),
        name="inner",
    )(band_rows, mine)
    outs = pl.pallas_call(
        functools.partial(outer_kernel, groups),
        out_shape=[struct(count, variables, span, LANES)] + [struct(both, width, rows)] * groups,
        in_specs=[SMEM] + [VMEM] * 9,
        out_specs=[VMEM] * (groups + 1),
        scratch_shapes=[pltpu.VMEM((2, 2 * width, both, rows), f32)] * 4
        + [
            pltpu.VMEM((halves, both, 2 * width, LANES), f32),
            pltpu.VMEM((halves, both, span, LANES), f32),
        ],
        compiler_params=ROOM,
        name="outer",
    )(band_rows, low, high, *inner)
    bands, strips = outs[0], outs[1:]
    arrived = lax.all_to_all(bands, "band", split_axis=0, concat_axis=0, tiled=True)
    pieces = [strips[0]] + [
        lax.ppermute(strips[k], "band", [(i, i ^ k) for i in range(count)])
        for k in range(1, groups)
    ]
    increment = pl.pallas_call(
        functools.partial(increment_kernel, groups),
        out_shape=struct(*background.shape),
        in_specs=[SMEM] + [VMEM] * groups,
        out_specs=VMEM,
        scratch_shapes=[pltpu.VMEM((variables, levels, width, rows), f32)],
        compiler_params=ROOM,
        name="increment",
    )(weights, *pieces)
    band_field = pl.pallas_call(
        functools.partial(band_kernel, groups),
        out_shape=struct(variables, levels, CAP, count * width),
        in_specs=[SMEM, SMEM, VMEM],
        out_specs=HBM,
        scratch_shapes=[pltpu.VMEM((variables, levels, CAP, count * width), f32)] * 2
        + [pltpu.SemaphoreType.DMA((variables,))],
        compiler_params=ROOM,
        name="bands",
    )(band_rows, weights, arrived)
    return increment, band_field


def solution(mesh):
    in_specs = (
        P(None, None, ("lon", "band"), None),
        P(None, ("lon", "band"), None),
        P(None, ("lon", "band"), None),
        P(),
        P(),
    )
    out_specs = (P(None, None, ("lon", "band"), None), P(None, None, "band", "lon"))
    return jax.shard_map(
        functools.partial(shards, dict(mesh.shape)),
        mesh=mesh,
        in_specs=in_specs,
        out_specs=out_specs,
        check_vma=False,
    )
```

time: 53.2 us -> 48.9 us (0.919)
  local copies, waits for them, and re-layouts: 2.7 us -> 0.03 us
  starting transfers between devices: 12.1 us -> 10.4 us
  waiting for transfers between devices: 13.4 us -> 14.3 us
  Pallas kernels: 10.3 us -> 9.65 us
    unnamed x23 -> x4, local copies, waits for them, and re-layouts: 2.68 us -> 0.01 us
    all_to_all x1, waiting for transfers between devices: 2.85 us -> 4.23 us  [shards(): lax.all_to_all(bands, 'band', split_axis=0, concat_axis=0, tiled=True)]
    ppermute x3, waiting for transfers between devices: 5.05 us -> 6.2 us  [shards(): lax.ppermute(strips[k], 'band', [(i, i ^ k) for i in range(count)])]
    ppermute x1, starting transfers between devices: 1.64 us -> 0.53 us  [shards(): low = lax.ppermute(mine[groups - 1], axes, shifted(groups))]
    ppermute x1, waiting for transfers between devices: 1.52 us -> 0.45 us  [shards(): high = lax.ppermute(mine[0], axes, shifted(-groups))]
    pallas_call x1 -> x2, Pallas kernels: 4.51 us -> 5.42 us  [the longest x1 2.94 us: shards(): pl.pallas_call(functools.partial(outer_kernel, groups), out_shape=[struct...]
    pallas_call x1, Pallas kernels: 1.93 us -> 1.17 us  [shards(): pl.pallas_call(regroup_kernel, out_shape=struct(groups, width, channels,...]
  transfers between devices with their start and end apart: 6 -> 6, of which waited for: 6 -> 5; matrix products, arithmetic and copies ran while one was open for 1% -> 0% of each run, Pallas kernels for 3% -> 8%
where the time goes in v3:
time: 48.9 us; the launch traced here: 48.6 us
  waiting for transfers between devices  14.3 us (29%)
  blocking collectives  13.5 us (28%)
  starting transfers between devices  10.4 us (21%)
  Pallas kernels  9.65 us (20%)
  between operations  0.68 us (1%)
    all_to_all x1, blocking collectives, shards(): lax.all_to_all(parted, 'band', split_axis=0, concat_axis=0, tiled=True, a...  13.5 us
    ppermute x3, waiting for transfers between devices, shards(): lax.ppermute(strips[k], 'band', [(i, i ^ k) for i in range(count)])  6.2 us
    all_to_all x1, starting transfers between devices, shards(): lax.all_to_all(bands, 'band', split_axis=0, concat_axis=0, tiled=True)  4.77 us
    all_to_all x1, waiting for transfers between devices, shards(): lax.all_to_all(bands, 'band', split_axis=0, concat_axis=0, tiled=True)  4.23 us
    ppermute x3, starting transfers between devices, shards(): lax.ppermute(strips[k], 'band', [(i, i ^ k) for i in range(count)])  3.55 us
    ppermute x1, waiting for transfers between devices, shards(): low = lax.ppermute(mine[groups - 1], axes, shifted(groups))  3.43 us
    pallas_call x1, Pallas kernels, shards(): pl.pallas_call(functools.partial(outer_kernel, groups), out_shape=[struct...  2.94 us
    pallas_call x1, Pallas kernels, shards(): pl.pallas_call(inner_kernel, out_shape=[struct(span, both, rows)] * 4 + [...  2.48 us
  transfers between devices with their start and end apart: 6, of which 5 were waited for; matrix products, arithmetic and copies ran while one was open for 0% of the time, Pallas kernels for 8%

profile of v3, /device:TPU:0, one launch (start us, length us, event | category | flops | bytes accessed | tf_op | source)
XLA Modules:
  0.0 48.6 jit_solution(6841226655443881020)
XLA Ops:
  0.6 1.2 %regroup.1 = f32[4,8,16,256]{3,2,1,0:T(8,128)S(1)} custom-call(f32[2,16,8,256]{3,2,1,0:T(8,128)} %background.1, f32[16,8,256]{2,1,0:T(8,128)} %scale_x.1, f32[16,8,256]{2,1,0:T(8,128)} %scale_y.1), custom_call_target="tpu_custom_call" | custom-call | tf_op jit(solution)/shard_map/regroup/pallas_call | solution.py:231
  1.8 13.5 %all_to_all.10.mine = f32[4,8,16,256]{3,2,1,0:T(8,128)S(1)} all-to-all(f32[4,8,16,256]{3,2,1,0:T(8,128)S(1)} %regroup.1), channel_id=1, replica_groups={{0,2,4,6},{8,10,12,14},{16,18,20,22},{24,26,28,30},{1,3,5,7},{9,11,13,1..., dimensions={0} | all-to-all | bytes 1048576 | tf_op jit(solution)/shard_map/all_to_all | solution.py:243
  15.3 0.0 copy-start.1
  15.3 1.6 %collective-permute-start.1 = (f32[8,16,256]{2,1,0:T(8,128)S(1)}, f32[8,16,256]{2,1,0:T(8,128)S(1)}, u32[]{:S(2)}, u32[]{:S(2)}) collective-permute-start(f32[8,16,256]{2,1,0:T(8,128)S(1)} %get-tuple-element.26), channel_id=1, source_target_pairs={{0,25},{2,27},{4,29},{6,31},{8,0},{10,2},{12,4},{14,6},{16,8},{18,... | collective-permute-start | bytes 393224 | tf_op jit(solution)/shard_map/ppermute | solution.py:262
  16.9 0.5 %collective-permute-start = (f32[8,16,256]{2,1,0:T(8,128)S(1)}, f32[8,16,256]{2,1,0:T(8,128)S(1)}, u32[]{:S(2)}, u32[]{:S(2)}) collective-permute-start(f32[8,16,256]{2,1,0:T(8,128)S(1)} %get-tuple-element.27), channel_id=1, source_target_pairs={{0,8},{2,10},{4,12},{6,14},{8,16},{10,18},{12,20},{14,22},{16,24},... | collective-permute-start | bytes 393224 | tf_op jit(solution)/shard_map/ppermute | solution.py:261
  17.4 0.0 copy-done.1
  17.4 2.5 %inner.1 = (f32[32,8,256]{2,1,0:T(8,128)S(1)}, f32[32,8,256]{2,1,0:T(8,128)S(1)}, f32[32,8,256]{2,1,0:T(8,128)S(1)}, f32[32,8,256]{2,1,0:T(8,128)S(1)}, f32[2,8,...) custom-call(s32[16]{0:T(128)S(1)} %copy-done.1, ...), custom_call_target="tpu_custom_call" | custom-call | flops 10485760 | bytes 1048576 | tf_op jit(solution)/shard_map/inner/pallas_call | solution.py:267
  19.9 0.5 collective-permute-done.1.high
  20.4 3.4 %collective-permute-done.low = f32[8,16,256]{2,1,0:T(8,128)S(1)} collective-permute-done((f32[8,16,256]{2,1,0:T(8,128)S(1)}, f32[8,16,256]{2,1,0:T(8,128)S(1)}, u32[]{:S(2)}, u32[]{:S(2)}) %collective-permute-start) | collective-permute-done | bytes 131104 | tf_op jit(solution)/shard_map/ppermute | solution.py:261
  23.8 2.9 %outer.1 = (f32[16,2,32,128]{3,2,1,0:T(8,128)}, f32[8,8,256]{2,1,0:T(8,128)S(1)}, f32[8,8,256]{2,1,0:T(8,128)S(1)}, f32[8,8,256]{2,1,0:T(8,128)S(1)}, f32[8,8,256]{2,1,0:T(8,128)S(1)}) custom-call(s32[16]{0:T(128)S(1)} %copy-done.1, f32[8,16,256]{2,1,0:T(8,128)S(1)} %collective-permute-done.low, f32[8,16,256]{2,1,0:T(8,128)S(1)} %collective-permute-done.1.high, ...), custom_call_target="tpu_custom_call" | custom-call | tf_op jit(solution)/shard_map/outer/pallas_call | solution.py:283
  26.7 4.8 %all-to-all-start.1 = ((f32[16,2,32,128]{3,2,1,0:T(8,128)}), f32[16,2,32,128]{3,2,1,0:T(8,128)S(1)}, u32[]{:S(2)}, u32[]{:S(2)}) async-start(f32[16,2,32,128]{3,2,1,0:T(8,128)} %get-tuple-element.25), calls=%async_computation.1 | async-start | bytes 1048576 | tf_op jit(solution)/shard_map/all_to_all | solution.py:297
  31.5 0.0 copy-start
  31.5 2.0 %collective-permute-start.2 = (f32[8,8,256]{2,1,0:T(8,128)S(1)}, f32[8,8,256]{2,1,0:T(8,128)S(1)}, u32[]{:S(2)}, u32[]{:S(2)}) collective-permute-start(f32[8,8,256]{2,1,0:T(8,128)S(1)} %get-tuple-element.22), channel_id=1, source_target_pairs={{0,2},{2,0},{4,6},{6,4},{8,10},{10,8},{12,14},{14,12},{16,18},{18,... | collective-permute-start | bytes 196616 | tf_op jit(solution)/shard_map/ppermute | solution.py:299
  33.5 1.5 %collective-permute-start.3 = (f32[8,8,256]{2,1,0:T(8,128)S(1)}, f32[8,8,256]{2,1,0:T(8,128)S(1)}, u32[]{:S(2)}, u32[]{:S(2)}) collective-permute-start(f32[8,8,256]{2,1,0:T(8,128)S(1)} %get-tuple-element.23), channel_id=1, source_target_pairs={{0,4},{2,6},{4,0},{6,2},{8,12},{10,14},{12,8},{14,10},{16,20},{18,... | collective-permute-start | bytes 196616 | tf_op jit(solution)/shard_map/ppermute | solution.py:299
  35.0 0.1 collective-permute-start.4
  35.1 2.7 %collective-permute-done.2.refs_1_ = f32[8,8,256]{2,1,0:T(8,128)S(1)} collective-permute-done((f32[8,8,256]{2,1,0:T(8,128)S(1)}, f32[8,8,256]{2,1,0:T(8,128)S(1)}, u32[]{:S(2)}, u32[]{:S(2)}) %collective-permute-start.2) | collective-permute-done | bytes 65568 | tf_op jit(solution)/shard_map/ppermute | solution.py:299
  37.8 3.5 %collective-permute-done.3.refs_2_ = f32[8,8,256]{2,1,0:T(8,128)S(1)} collective-permute-done((f32[8,8,256]{2,1,0:T(8,128)S(1)}, f32[8,8,256]{2,1,0:T(8,128)S(1)}, u32[]{:S(2)}, u32[]{:S(2)}) %collective-permute-start.3) | collective-permute-done | bytes 65568 | tf_op jit(solution)/shard_map/ppermute | solution.py:299
  41.3 0.0 collective-permute-done.4.refs_3_
  41.3 0.0 copy-done
  41.3 1.4 %increment.1 = f32[2,16,8,256]{3,2,1,0:T(8,128)} custom-call(f32[5,2,16]{2,1,0:T(2,128)S(1)} %bitcast.5, f32[8,8,256]{2,1,0:T(8,128)S(1)} %get-tuple-element.21.refs_0_, f32[8,8,256]{2,1,0:T(8,128)S(1)} %collective-permute-done.2.refs_1_, f32[8,8,256]{2,1,0:T(8,128)S(1)} %collective-permute-done.3.refs_2_, f32[8,8,256]{2,1,0:T(8,128)S(1)} %collective-permute-done.4.refs_3_), custom_call_target="tpu_custom_call" | custom-call | tf_op jit(solution)/shard_map/increment/pallas_call | solution.py:302
  42.7 4.2 %all-to-all-done.1.arrived = f32[16,2,32,128]{3,2,1,0:T(8,128)S(1)} async-done(((f32[16,2,32,128]{3,2,1,0:T(8,128)}), f32[16,2,32,128]{3,2,1,0:T(8,128)S(1)}, u32[]{:S(2)}, u32[]{:S(2)}) %all-to-all-start.1) | async-done | bytes 524320 | tf_op jit(solution)/shard_map/all_to_all | solution.py:297
  47.0 1.6 %bands.1 = f32[2,16,32,128]{3,2,1,0:T(8,128)} custom-call(s32[16]{0:T(128)S(1)} %copy-done.1, f32[5,2,16]{2,1,0:T(2,128)S(1)} %bitcast.6, f32[16,2,32,128]{3,2,1,0:T(8,128)S(1)} %all-to-all-done.1.arrived), custom_call_target="tpu_custom_call" | custom-call | tf_op jit(solution)/shard_map/bands/pallas_call | solution.py:311
  (1 shorter events, 0.0 us)
Async XLA Ops:
  15.3 2.1 %copy-start.1 = (s32[16]{0:T(128)S(1)}, s32[16]{0:T(128)}, u32[]{:S(2)}) copy-start(s32[16]{0:T(128)} %band_rows.5) | copy-start | bytes 196
  15.3 5.0 %collective-permute-start.1 = (f32[8,16,256]{2,1,0:T(8,128)S(1)}, f32[8,16,256]{2,1,0:T(8,128)S(1)}, u32[]{:S(2)}, u32[]{:S(2)}) collective-permute-start(f32[8,16,256]{2,1,0:T(8,128)S(1)} %get-tuple-element.26), channel_id=1, source_target_pairs={{0,25},{2,27},{4,29},{6,31},{8,0},{10,2},{12,4},{14,6},{16,8},{18,... | collective-permute-start | bytes 393224 | tf_op jit(solution)/shard_map/ppermute | solution.py:262
  16.9 6.9 %collective-permute-start = (f32[8,16,256]{2,1,0:T(8,128)S(1)}, f32[8,16,256]{2,1,0:T(8,128)S(1)}, u32[]{:S(2)}, u32[]{:S(2)}) collective-permute-start(f32[8,16,256]{2,1,0:T(8,128)S(1)} %get-tuple-element.27), channel_id=1, source_target_pairs={{0,8},{2,10},{4,12},{6,14},{8,16},{10,18},{12,20},{14,22},{16,24},... | collective-permute-start | bytes 393224 | tf_op jit(solution)/shard_map/ppermute | solution.py:261
  26.7 20.2 %all-to-all-start.1 = ((f32[16,2,32,128]{3,2,1,0:T(8,128)}), f32[16,2,32,128]{3,2,1,0:T(8,128)S(1)}, u32[]{:S(2)}, u32[]{:S(2)}) async-start(f32[16,2,32,128]{3,2,1,0:T(8,128)} %get-tuple-element.25), calls=%async_computation.1 | async-start | bytes 1048576 | tf_op jit(solution)/shard_map/all_to_all | solution.py:297
  31.5 9.8 %copy-start = (f32[2,5,16]{2,0,1:T(2,128)S(1)}, f32[2,5,16]{2,0,1:T(2,128)}, u32[]{:S(2)}) copy-start(f32[2,5,16]{2,0,1:T(2,128)} %param.8) | copy-start | bytes 1924
  31.5 6.3 %collective-permute-start.2 = (f32[8,8,256]{2,1,0:T(8,128)S(1)}, f32[8,8,256]{2,1,0:T(8,128)S(1)}, u32[]{:S(2)}, u32[]{:S(2)}) collective-permute-start(f32[8,8,256]{2,1,0:T(8,128)S(1)} %get-tuple-element.22), channel_id=1, source_target_pairs={{0,2},{2,0},{4,6},{6,4},{8,10},{10,8},{12,14},{14,12},{16,18},{18,... | collective-permute-start | bytes 196616 | tf_op jit(solution)/shard_map/ppermute | solution.py:299
  33.5 7.8 %collective-permute-start.3 = (f32[8,8,256]{2,1,0:T(8,128)S(1)}, f32[8,8,256]{2,1,0:T(8,128)S(1)}, u32[]{:S(2)}, u32[]{:S(2)}) collective-permute-start(f32[8,8,256]{2,1,0:T(8,128)S(1)} %get-tuple-element.23), channel_id=1, source_target_pairs={{0,4},{2,6},{4,0},{6,2},{8,12},{10,14},{12,8},{14,10},{16,20},{18,... | collective-permute-start | bytes 196616 | tf_op jit(solution)/shard_map/ppermute | solution.py:299
  35.0 6.3 %collective-permute-start.4 = (f32[8,8,256]{2,1,0:T(8,128)S(1)}, f32[8,8,256]{2,1,0:T(8,128)S(1)}, u32[]{:S(2)}, u32[]{:S(2)}) collective-permute-start(f32[8,8,256]{2,1,0:T(8,128)S(1)} %get-tuple-element.24), channel_id=1, source_target_pairs={{0,6},{2,4},{4,2},{6,0},{8,14},{10,12},{12,10},{14,8},{16,22},{18,... | collective-permute-start | bytes 196616 | tf_op jit(solution)/shard_map/ppermute | solution.py:299

commit v4 on v3

--- a/solution.py
+++ b/solution.py
@@ -13,7 +13,6 @@
 LANES = 128
 TAPS = 5
 BLOCK = 16
-UNROLL = 4
 VMEM = pl.BlockSpec(memory_space=pltpu.VMEM)
 SMEM = pl.BlockSpec(memory_space=pltpu.SMEM)
 HBM = pl.BlockSpec(memory_space=pltpu.HBM)
@@ -60,29 +59,29 @@
     down_y[near] = pltpu.roll(flow_y, 1, 2)
 
 
-def advance(field, along_x, along_y, down_y, first, last, before, behind):
-    rows = field.shape[-1]
-    if before is None:
-        before = along_x[first - 1] * (field[first] - field[first - 1])
-    entry = before
-    for c in range(first, last, BLOCK):
-        m = min(BLOCK, last - c)
-        near = pl.ds(c, m)
-        if c + m == last and behind is not None:
-            here = field[near]
-            after = here[1:]
-            ahead = [along_x[pl.ds(c, m - 1)] * (after - here[:-1]), behind[None]]
-            flux_x = jnp.concatenate(ahead, 0)
-        else:
-            both = field[pl.ds(c, m + 1)]
-            here, after = both[:m], both[1:]
-            flux_x = along_x[near] * (after - here)
-        left = jnp.concatenate([before[None], flux_x[:-1]], 0)
-        flux_y = along_y[near] * (pltpu.roll(here, rows - 1, 2) - here)
-        under = down_y[near] * (here - pltpu.roll(here, 1, 2))
-        field[near] = here + flux_x - left + flux_y - under
-        before = flux_x[m - 1]
-    return entry, before
+def advance(parts):
+    joined, fluxes, ends = [], [], []
+    for field, along_x, along_y, down_y, first, last, before, behind in parts:
+        near = pl.ds(first, last - first)
+        here = field[near]
+        inner = along_x[pl.ds(first, last - first - 1)] * (here[1:] - here[:-1])
+        if before is None:
+            before = along_x[first - 1] * (here[0] - field[first - 1])
+        if behind is None:
+            behind = along_x[last - 1] * (field[last] - here[-1])
+        fluxes.append((before, behind))
+        entering = jnp.concatenate([before[None], inner], 0)
+        leaving = jnp.concatenate([inner, behind[None]], 0)
+        joined.append((here, leaving, entering, along_y[near], down_y[near]))
+        ends.append(sum(ends[-1:]) + last - first)
+    here, leaving, entering, up, down = (jnp.concatenate(each, 0) for each in zip(*joined))
+    rows = here.shape[-1]
+    flux_y = up * (pltpu.roll(here, rows - 1, 2) - here)
+    under = down * (here - pltpu.roll(here, 1, 2))
+    result = here + leaving - entering + flux_y - under
+    for (field, _, _, _, first, last, _, _), end in zip(parts, ends):
+        field[pl.ds(first, last - first)] = result[end - last + first : end]
+    return fluxes
 
 
 def turn(columns, result, at):
@@ -91,12 +90,13 @@
         result[half, :, at] = block[:, :, half * LANES : (half + 1) * LANES]
 
 
-def pack(result, band_rows, bands, at):
+def pack(result, band_rows, bands, copies):
     halves, channels, count, _ = result.shape
     part = channels // 2
+    total = bands.shape[0]
     lane = lax.broadcasted_iota(jnp.int32, (count, LANES), 1)
-
-    def one_band(b, start):
+    start = jnp.int32(0)
+    for b in range(total):
         half = start // LANES
         offset = start - half * LANES
         beyond = lax.rem(half + 1, halves)
@@ -108,33 +108,40 @@
                 shift = lax.rem(LANES + l * CAP - offset, LANES)
                 turned = pltpu.roll(window, shift, 1)
                 packed = turned if l == 0 else jnp.where(lane >= l * CAP, turned, packed)
-            for source, target in at:
-                bands[b, v, target] = packed[source]
-        return start + band_rows[b]
-
-    lax.fori_loop(0, bands.shape[0], one_band, jnp.int32(0), unroll=UNROLL)
-
-
-def inner_kernel(band_rows, mine, field, along_x, along_y, down_y, sides, result, bands):
+            bands[b, v] = packed
+        start = start + band_rows[b]
+        if (b + 1) * len(copies) % total == 0:
+            copies[(b + 1) * len(copies) // total - 1].start()
+
+
+def inner_kernel(band_rows, mine, field, along_x, along_y, down_y, sides, result, bands, ready, sems):
     groups, width, channels, rows = mine.shape
     for s in range(groups):
         spread_out(mine.at[s], pl.ds(s * width, width), field, along_x, along_y, down_y)
     span = groups * width
     for step in range(STEPS):
-        entry, leave = advance(
-            field, along_x, along_y, down_y, step + 1, span - 1 - step, None, None
-        )
-        sides[0, step] = entry
-        sides[1, step] = leave
+        last = step + 1
+        behind = None
+        for first in range(step + 1, span - 1 - step, BLOCK):
+            last = min(first + BLOCK, span - 1 - step)
+            piece = (field, along_x, along_y, down_y, first, last, behind, None)
+            before, behind = advance([piece])[0]
+            if first == step + 1:
+                sides[0, step] = before
+        sides[1, step] = behind
     for s in range(1, groups - 1):
         turn(field[pl.ds(s * width, width)], result, pl.ds((s - 1) * width, width))
-    pack(result, band_rows, bands, [(slice(None), slice(None))])
-
-
-def outer_kernel(groups, band_rows, low, high, *refs):
-    inner, sides, inner_result, inner_bands, bands = refs[:4], *refs[4:8]
+    copy = pltpu.make_async_copy(ready, bands.at[:, :, pl.ds(0, span - 2 * width)], sems.at[0])
+    pack(result, band_rows, ready, [copy])
+    copy.wait()
+
+
+def outer_kernel(groups, rows_far, low, high, *refs):
+    inner, sides, inner_result, _, bands = refs[:4], *refs[4:8]
     strips = refs[8 : 8 + groups]
-    ends, result, whole = refs[8 + groups : 12 + groups], *refs[12 + groups :]
+    ends, result, whole, ready, band_rows, sems = refs[8 + groups : 12 + groups], *refs[12 + groups :]
+    rows_copy = pltpu.make_async_copy(rows_far, band_rows, sems.at[groups])
+    rows_copy.start()
     width, _, rows = low.shape
     span = groups * width
     for side, (halo, own) in enumerate(((low, 0), (high, span - width))):
@@ -143,15 +150,24 @@
         for end, array in zip(arrays, inner):
             end[pl.ds((1 - side) * width, width)] = array[pl.ds(own, width)]
     for step in range(STEPS):
-        first = step + 1
-        arrays = [end.at[0] for end in ends]
-        advance(*arrays, first, first + width, None, sides[0, step])
-        first = width - 1 - step
-        arrays = [end.at[1] for end in ends]
-        advance(*arrays, first, first + width, sides[1, step], None)
+        pieces = []
+        for side, first in enumerate((step + 1, width - 1 - step)):
+            arrays = [end.at[side] for end in ends]
+            faces = (sides[1, step], None) if side else (None, sides[0, step])
+            pieces.append((*arrays, first, first + width, *faces))
+        advance(pieces)
     field = ends[0]
     turn(field[0, pl.ds(width, width)], result, pl.ds(0, width))
     turn(field[1, pl.ds(0, width)], result, pl.ds(width, width))
+
+    copies = []
+    each = bands.shape[0] // groups
+    for i in range(groups):
+        near = pl.ds(i * each, each)
+        target = bands.at[near, :, pl.ds(span - 2 * width, 2 * width)]
+        copies.append(pltpu.make_async_copy(ready.at[near], target, sems.at[i]))
+    rows_copy.wait()
+    pack(result, band_rows, ready, copies)
 
     me = lax.rem(lax.axis_index("band"), groups)
     whole[:, :, pl.ds(width, span - 2 * width)] = inner_result[...]
@@ -163,26 +179,21 @@
             strips[k][:, :, half * LANES : (half + 1) * LANES] = whole[
                 half, :, pl.ds(pl.multiple_of(s * width, width), width)
             ]
-
-    bands[:, :, pl.ds(width, span - 2 * width)] = inner_bands[...]
-    edges = [
-        (slice(0, width), pl.ds(0, width)),
-        (slice(width, 2 * width), pl.ds(span - width, width)),
-    ]
-    pack(result, band_rows, bands, edges)
-
-
-def filtered(weights, v, l, levels, at):
-    total = at(v, l)
+    for copy in copies:
+        copy.wait()
+
+
+def filtered(taps, v, l, levels, whole):
+    total = whole[v, l]
     for tap in range(TAPS):
         other = l + tap - TAPS // 2
         if 0 <= other < levels:
-            total = total + weights[tap, v, l] * at(v, other)
+            total = total + taps(tap, v, l) * whole[v, other]
     return total
 
 
-def increment_kernel(groups, weights, *refs):
-    pieces, out, whole = refs[:groups], refs[groups], refs[groups + 1]
+def increment_kernel(groups, band_rows, weights, *refs):
+    pieces, out, taps, keep, whole = refs[:groups], *refs[groups:]
     variables, levels = out.shape[:2]
     part = levels // groups
     me = lax.rem(lax.axis_index("band"), groups)
@@ -192,27 +203,40 @@
             whole[v, near] = pieces[k][pl.ds(v * part, part)]
     for v in range(variables):
         for l in range(levels):
-            out[v, l] = filtered(weights, v, l, levels, lambda a, b: whole[a, b])
-
-
-def band_kernel(groups, band_rows, weights, arrived, out, whole, ready, sems):
-    variables, levels, height, columns = out.shape
+            out[v, l] = filtered(lambda a, b, c: weights[a, b, c], v, l, levels, whole)
+            for tap in range(TAPS):
+                taps[tap, v, l] = jnp.full(taps.shape[3:], weights[tap, v, l])
+    row = lax.broadcasted_iota(jnp.int32, keep.shape, 0)
+    keep[...] = (row < band_rows[lax.axis_index("band")]).astype(jnp.int32)
+
+
+def band_kernel(groups, width, taps, keep, arrived, out, whole, ready, sems):
+    variables, levels, height, _ = out.shape
     part = levels // groups
-    count = arrived.shape[0]
-    here = band_rows[lax.axis_index("band")]
-    keep = lax.broadcasted_iota(jnp.int32, (height, columns), 0) < here
+    count, _, span, _ = arrived.shape
+    inside = span - 2 * width
+    mine = keep[...] > 0
     copies = []
     for v in range(variables):
         for q in range(groups):
-            tall = jnp.concatenate([arrived[s, v] for s in range(q, count, groups)], 0)
-            flat = jnp.transpose(tall)
+            blocks = []
+            for s in range(q, count, groups):
+                blocks += [arrived[s, v, inside : inside + width], arrived[s, v, :inside]]
+                blocks += [arrived[s, v, inside + width :]]
+            flat = jnp.transpose(jnp.concatenate(blocks, 0))
             for l in range(part):
                 whole[v, q * part + l] = flat[l * height : (l + 1) * height]
+    for v in range(variables):
         for l in range(levels):
-            total = filtered(weights, v, l, levels, lambda a, b: whole[a, b])
-            ready[v, l] = jnp.where(keep, total, 0.0)
-        copies.append(pltpu.make_async_copy(ready.at[v], out.at[v], sems.at[v]))
-        copies[v].start()
+            total = filtered(lambda a, b, c: taps[a, b, c], v, l, levels, whole)
+            ready[v, l] = jnp.where(mine, total, 0.0)
+            if (l + 1) % part == 0:
+                near = pl.ds(l + 1 - part, part)
+                i = len(copies)
+                copies.append(
+                    pltpu.make_async_copy(ready.at[v, near], out.at[v, near], sems.at[i])
+                )
+                copies[i].start()
     for copy in copies:
         copy.wait()
 
@@ -270,10 +294,14 @@
         + [
             struct(2, STEPS, both, rows),
             struct(halves, both, inside, LANES),
-            struct(count, variables, inside, LANES),
+            struct(count, variables, span, LANES),
         ],
         in_specs=[SMEM, VMEM],
-        out_specs=[VMEM] * 7,
+        out_specs=[VMEM] * 6 + [HBM],
+        scratch_shapes=[
+            pltpu.VMEM((count, variables, inside, LANES), f32),
+            pltpu.SemaphoreType.DMA((1,)),
+        ],
         compiler_params=ROOM,
         cost_estimate=pl.CostEstimate(
             flops=20 * STEPS * span * both * rows, bytes_accessed=2**20, transcendentals=0
@@ -283,12 +311,16 @@
     outs = pl.pallas_call(
         functools.partial(outer_kernel, groups),
         out_shape=[struct(count, variables, span, LANES)] + [struct(both, width, rows)] * groups,
-        in_specs=[SMEM] + [VMEM] * 9,
-        out_specs=[VMEM] * (groups + 1),
+        in_specs=[HBM] + [VMEM] * 8 + [HBM],
+        out_specs=[HBM] + [VMEM] * groups,
+        input_output_aliases={9: 0},
         scratch_shapes=[pltpu.VMEM((2, 2 * width, both, rows), f32)] * 4
         + [
             pltpu.VMEM((halves, both, 2 * width, LANES), f32),
             pltpu.VMEM((halves, both, span, LANES), f32),
+            pltpu.VMEM((count, variables, 2 * width, LANES), f32),
+            pltpu.SMEM(band_rows.shape, band_rows.dtype),
+            pltpu.SemaphoreType.DMA((groups + 1,)),
         ],
         compiler_params=ROOM,
         name="outer",
@@ -299,25 +331,29 @@
         lax.ppermute(strips[k], "band", [(i, i ^ k) for i in range(count)])
         for k in range(1, groups)
     ]
-    increment = pl.pallas_call(
+    increment, taps, keep = pl.pallas_call(
         functools.partial(increment_kernel, groups),
-        out_shape=struct(*background.shape),
-        in_specs=[SMEM] + [VMEM] * groups,
-        out_specs=VMEM,
+        out_shape=[
+            struct(*background.shape),
+            struct(TAPS, variables, levels, 1, count * width),
+            jax.ShapeDtypeStruct((CAP, count * width), jnp.int32),
+        ],
+        in_specs=[SMEM, SMEM] + [VMEM] * groups,
+        out_specs=[VMEM] * 3,
         scratch_shapes=[pltpu.VMEM((variables, levels, width, rows), f32)],
         compiler_params=ROOM,
         name="increment",
-    )(weights, *pieces)
+    )(band_rows, weights, *pieces)
     band_field = pl.pallas_call(
-        functools.partial(band_kernel, groups),
+        functools.partial(band_kernel, groups, width),
         out_shape=struct(variables, levels, CAP, count * width),
-        in_specs=[SMEM, SMEM, VMEM],
+        in_specs=[VMEM] * 3,
         out_specs=HBM,
         scratch_shapes=[pltpu.VMEM((variables, levels, CAP, count * width), f32)] * 2
-        + [pltpu.SemaphoreType.DMA((variables,))],
+        + [pltpu.SemaphoreType.DMA((variables * groups,))],
         compiler_params=ROOM,
         name="bands",
-    )(band_rows, weights, arrived)
+    )(taps, keep, arrived)
     return increment, band_field
 
 

time: 48.9 us -> 47.5 us (0.971)
  Pallas kernels: 9.65 us -> 8.74 us
    pallas_call x1, Pallas kernels: 2.94 us -> 2.21 us  [shards(): pl.pallas_call(functools.partial(outer_kernel, groups), out_shape=[struct...]
    pallas_call x2, Pallas kernels: 3.06 us -> 2.43 us  [the longest x1 1.45 us: shards(): pl.pallas_call(functools.partial(increment_kernel, groups), out_shape=[st...]
  transfers between devices with their start and end apart: 6 -> 6, of which waited for: 5 -> 4; matrix products, arithmetic and copies ran while one was open for 0% -> 0% of each run, Pallas kernels for 8% -> 9%
where the time goes in v4:
time: 47.5 us; the launch traced here: 47.2 us
  waiting for transfers between devices  13.9 us (29%)
  blocking collectives  13.5 us (28%)
  starting transfers between devices  10.4 us (22%)
  Pallas kernels  8.74 us (18%)
  between operations  0.7 us (1%)
    all_to_all x1, blocking collectives, shards(): lax.all_to_all(parted, 'band', split_axis=0, concat_axis=0, tiled=True, a...  13.5 us
    ppermute x3, waiting for transfers between devices, shards(): lax.ppermute(strips[k], 'band', [(i, i ^ k) for i in range(count)])  6.2 us
    all_to_all x1, starting transfers between devices, shards(): lax.all_to_all(bands, 'band', split_axis=0, concat_axis=0, tiled=True)  4.78 us
    all_to_all x1, waiting for transfers between devices, shards(): lax.all_to_all(bands, 'band', split_axis=0, concat_axis=0, tiled=True)  4.22 us
    ppermute x3, starting transfers between devices, shards(): lax.ppermute(strips[k], 'band', [(i, i ^ k) for i in range(count)])  3.55 us
    ppermute x1, waiting for transfers between devices, shards(): low = lax.ppermute(mine[groups - 1], axes, shifted(groups))  3.42 us
    pallas_call x1, Pallas kernels, shards(): pl.pallas_call(inner_kernel, out_shape=[struct(span, both, rows)] * 4 + [...  2.93 us
    pallas_call x1, Pallas kernels, shards(): pl.pallas_call(functools.partial(outer_kernel, groups), out_shape=[struct...  2.21 us
  transfers between devices with their start and end apart: 6, of which 4 were waited for; matrix products, arithmetic and copies ran while one was open for 0% of the time, Pallas kernels for 9%

profile of v4, /device:TPU:0, one launch (start us, length us, event | category | flops | bytes accessed | tf_op | source)
XLA Modules:
  0.0 47.2 jit_solution(4860075370773983209)
XLA Ops:
  0.6 1.2 %regroup.1 = f32[4,8,16,256]{3,2,1,0:T(8,128)S(1)} custom-call(f32[2,16,8,256]{3,2,1,0:T(8,128)} %background.1, f32[16,8,256]{2,1,0:T(8,128)} %scale_x.1, f32[16,8,256]{2,1,0:T(8,128)} %scale_y.1), custom_call_target="tpu_custom_call" | custom-call | tf_op jit(solution)/shard_map/regroup/pallas_call | solution.py:255
  1.8 13.5 %all_to_all.10.mine = f32[4,8,16,256]{3,2,1,0:T(8,128)S(1)} all-to-all(f32[4,8,16,256]{3,2,1,0:T(8,128)S(1)} %regroup.1), channel_id=1, replica_groups={{0,2,4,6},{8,10,12,14},{16,18,20,22},{24,26,28,30},{1,3,5,7},{9,11,13,1..., dimensions={0} | all-to-all | bytes 1048576 | tf_op jit(solution)/shard_map/all_to_all | solution.py:267
  15.3 0.0 copy-start.1
  15.3 1.6 %collective-permute-start.1 = (f32[8,16,256]{2,1,0:T(8,128)S(1)}, f32[8,16,256]{2,1,0:T(8,128)S(1)}, u32[]{:S(2)}, u32[]{:S(2)}) collective-permute-start(f32[8,16,256]{2,1,0:T(8,128)S(1)} %get-tuple-element.32), channel_id=1, source_target_pairs={{0,25},{2,27},{4,29},{6,31},{8,0},{10,2},{12,4},{14,6},{16,8},{18,... | collective-permute-start | bytes 393224 | tf_op jit(solution)/shard_map/ppermute | solution.py:286
  16.9 0.5 %collective-permute-start = (f32[8,16,256]{2,1,0:T(8,128)S(1)}, f32[8,16,256]{2,1,0:T(8,128)S(1)}, u32[]{:S(2)}, u32[]{:S(2)}) collective-permute-start(f32[8,16,256]{2,1,0:T(8,128)S(1)} %get-tuple-element.33), channel_id=1, source_target_pairs={{0,8},{2,10},{4,12},{6,14},{8,16},{10,18},{12,20},{14,22},{16,24},... | collective-permute-start | bytes 393224 | tf_op jit(solution)/shard_map/ppermute | solution.py:285
  17.4 0.0 copy-done.1
  17.4 2.9 %inner.1 = (f32[32,8,256]{2,1,0:T(8,128)S(1)}, f32[32,8,256]{2,1,0:T(8,128)S(1)}, f32[32,8,256]{2,1,0:T(8,128)S(1)}, f32[32,8,256]{2,1,0:T(8,128)S(1)}, f32[2,8,...) custom-call(s32[16]{0:T(128)S(1)} %copy-done.1, f32[4,8,16,256]{3,2,1,0:T(8,128)S(1)} %all_to_all.10.mine), custom_call_target="tpu_custom_call" | custom-call | flops 10485760 | bytes 1048576 | tf_op jit(solution)/shard_map/inner/pallas_call | solution.py:291
  20.4 0.0 collective-permute-done.1.high
  20.4 3.4 %collective-permute-done.low = f32[8,16,256]{2,1,0:T(8,128)S(1)} collective-permute-done((f32[8,16,256]{2,1,0:T(8,128)S(1)}, f32[8,16,256]{2,1,0:T(8,128)S(1)}, u32[]{:S(2)}, u32[]{:S(2)}) %collective-permute-start) | collective-permute-done | bytes 131104 | tf_op jit(solution)/shard_map/ppermute | solution.py:285
  23.8 2.2 %outer.1 = (f32[16,2,32,128]{3,2,1,0:T(8,128)}, f32[8,8,256]{2,1,0:T(8,128)S(1)}, f32[8,8,256]{2,1,0:T(8,128)S(1)}, f32[8,8,256]{2,1,0:T(8,128)S(1)}, f32[8,8,256]{2,1,0:T(8,128)S(1)}) custom-call(s32[16]{0:T(128)S(1)} %copy-done.1, f32[8,16,256]{2,1,0:T(8,128)S(1)} %collective-permute-done.low, ...), custom_call_target="tpu_custom_call", output_to_operand_aliasing={{0}: (9, {})} | custom-call | tf_op jit(solution)/shard_map/outer/pallas_call | solution.py:311
  26.0 4.8 %all-to-all-start.1 = ((f32[16,2,32,128]{3,2,1,0:T(8,128)}), f32[16,2,32,128]{3,2,1,0:T(8,128)S(1)}, u32[]{:S(2)}, u32[]{:S(2)}) async-start(f32[16,2,32,128]{3,2,1,0:T(8,128)} %get-tuple-element.31), calls=%async_computation.1 | async-start | bytes 1048576 | tf_op jit(solution)/shard_map/all_to_all | solution.py:329
  30.8 0.0 copy-start
  30.8 2.0 %collective-permute-start.2 = (f32[8,8,256]{2,1,0:T(8,128)S(1)}, f32[8,8,256]{2,1,0:T(8,128)S(1)}, u32[]{:S(2)}, u32[]{:S(2)}) collective-permute-start(f32[8,8,256]{2,1,0:T(8,128)S(1)} %get-tuple-element.25), channel_id=1, source_target_pairs={{0,2},{2,0},{4,6},{6,4},{8,10},{10,8},{12,14},{14,12},{16,18},{18,... | collective-permute-start | bytes 196616 | tf_op jit(solution)/shard_map/ppermute | solution.py:331
  32.8 1.5 %collective-permute-start.3 = (f32[8,8,256]{2,1,0:T(8,128)S(1)}, f32[8,8,256]{2,1,0:T(8,128)S(1)}, u32[]{:S(2)}, u32[]{:S(2)}) collective-permute-start(f32[8,8,256]{2,1,0:T(8,128)S(1)} %get-tuple-element.26), channel_id=1, source_target_pairs={{0,4},{2,6},{4,0},{6,2},{8,12},{10,14},{12,8},{14,10},{16,20},{18,... | collective-permute-start | bytes 196616 | tf_op jit(solution)/shard_map/ppermute | solution.py:331
  34.3 0.1 collective-permute-start.4
  34.4 2.7 %collective-permute-done.2.refs_1_ = f32[8,8,256]{2,1,0:T(8,128)S(1)} collective-permute-done((f32[8,8,256]{2,1,0:T(8,128)S(1)}, f32[8,8,256]{2,1,0:T(8,128)S(1)}, u32[]{:S(2)}, u32[]{:S(2)}) %collective-permute-start.2) | collective-permute-done | bytes 65568 | tf_op jit(solution)/shard_map/ppermute | solution.py:331
  37.1 3.5 %collective-permute-done.3.refs_2_ = f32[8,8,256]{2,1,0:T(8,128)S(1)} collective-permute-done((f32[8,8,256]{2,1,0:T(8,128)S(1)}, f32[8,8,256]{2,1,0:T(8,128)S(1)}, u32[]{:S(2)}, u32[]{:S(2)}) %collective-permute-start.3) | collective-permute-done | bytes 65568 | tf_op jit(solution)/shard_map/ppermute | solution.py:331
  40.6 0.0 collective-permute-done.4.refs_3_
  40.6 0.0 copy-done
  40.6 1.5 %increment.1 = (f32[2,16,8,256]{3,2,1,0:T(8,128)}, f32[5,2,16,1,128]{4,3,2,1,0:T(1,128)S(1)}, s32[32,128]{1,0:T(8,128)S(1)}) custom-call(s32[16]{0:T(128)S(1)} %copy-done.1, f32[5,2,16]{2,1,0:T(2,128)S(1)} %bitcast.5, f32[8,8,256]{2,1,0:T(8,128)S(1)} %get-tuple-element.24.refs_0_, f32[8,8,256]{2,1,0:T(8,128)S(1)} %collective-permute-done.2.refs_1_, ...), custom_call_target="tpu_custom_call" | custom-call | tf_op jit(solution)/shard_map/increment/pallas_call | solution.py:334
  42.0 4.2 %all-to-all-done.1.arrived = f32[16,2,32,128]{3,2,1,0:T(8,128)S(1)} async-done(((f32[16,2,32,128]{3,2,1,0:T(8,128)}), f32[16,2,32,128]{3,2,1,0:T(8,128)S(1)}, u32[]{:S(2)}, u32[]{:S(2)}) %all-to-all-start.1) | async-done | bytes 524320 | tf_op jit(solution)/shard_map/all_to_all | solution.py:329
  46.2 1.0 %bands.1 = f32[2,16,32,128]{3,2,1,0:T(8,128)} custom-call(f32[5,2,16,1,128]{4,3,2,1,0:T(1,128)S(1)} %get-tuple-element.29.taps, s32[32,128]{1,0:T(8,128)S(1)} %get-tuple-element.30.keep, f32[16,2,32,128]{3,2,1,0:T(8,128)S(1)} %all-to-all-done.1.arrived), custom_call_target="tpu_custom_call" | custom-call | tf_op jit(solution)/shard_map/bands/pallas_call | solution.py:347
  (1 shorter events, 0.0 us)
Async XLA Ops:
  15.3 2.1 %copy-start.1 = (s32[16]{0:T(128)S(1)}, s32[16]{0:T(128)}, u32[]{:S(2)}) copy-start(s32[16]{0:T(128)} %band_rows.3) | copy-start | bytes 196
  15.3 5.0 %collective-permute-start.1 = (f32[8,16,256]{2,1,0:T(8,128)S(1)}, f32[8,16,256]{2,1,0:T(8,128)S(1)}, u32[]{:S(2)}, u32[]{:S(2)}) collective-permute-start(f32[8,16,256]{2,1,0:T(8,128)S(1)} %get-tuple-element.32), channel_id=1, source_target_pairs={{0,25},{2,27},{4,29},{6,31},{8,0},{10,2},{12,4},{14,6},{16,8},{18,... | collective-permute-start | bytes 393224 | tf_op jit(solution)/shard_map/ppermute | solution.py:286
  16.9 6.9 %collective-permute-start = (f32[8,16,256]{2,1,0:T(8,128)S(1)}, f32[8,16,256]{2,1,0:T(8,128)S(1)}, u32[]{:S(2)}, u32[]{:S(2)}) collective-permute-start(f32[8,16,256]{2,1,0:T(8,128)S(1)} %get-tuple-element.33), channel_id=1, source_target_pairs={{0,8},{2,10},{4,12},{6,14},{8,16},{10,18},{12,20},{14,22},{16,24},... | collective-permute-start | bytes 393224 | tf_op jit(solution)/shard_map/ppermute | solution.py:285
  26.0 20.2 %all-to-all-start.1 = ((f32[16,2,32,128]{3,2,1,0:T(8,128)}), f32[16,2,32,128]{3,2,1,0:T(8,128)S(1)}, u32[]{:S(2)}, u32[]{:S(2)}) async-start(f32[16,2,32,128]{3,2,1,0:T(8,128)} %get-tuple-element.31), calls=%async_computation.1 | async-start | bytes 1048576 | tf_op jit(solution)/shard_map/all_to_all | solution.py:329
  30.8 9.8 %copy-start = (f32[2,5,16]{2,0,1:T(2,128)S(1)}, f32[2,5,16]{2,0,1:T(2,128)}, u32[]{:S(2)}) copy-start(f32[2,5,16]{2,0,1:T(2,128)} %param.8) | copy-start | bytes 1924
  30.8 6.3 %collective-permute-start.2 = (f32[8,8,256]{2,1,0:T(8,128)S(1)}, f32[8,8,256]{2,1,0:T(8,128)S(1)}, u32[]{:S(2)}, u32[]{:S(2)}) collective-permute-start(f32[8,8,256]{2,1,0:T(8,128)S(1)} %get-tuple-element.25), channel_id=1, source_target_pairs={{0,2},{2,0},{4,6},{6,4},{8,10},{10,8},{12,14},{14,12},{16,18},{18,... | collective-permute-start | bytes 196616 | tf_op jit(solution)/shard_map/ppermute | solution.py:331
  32.8 7.8 %collective-permute-start.3 = (f32[8,8,256]{2,1,0:T(8,128)S(1)}, f32[8,8,256]{2,1,0:T(8,128)S(1)}, u32[]{:S(2)}, u32[]{:S(2)}) collective-permute-start(f32[8,8,256]{2,1,0:T(8,128)S(1)} %get-tuple-element.26), channel_id=1, source_target_pairs={{0,4},{2,6},{4,0},{6,2},{8,12},{10,14},{12,8},{14,10},{16,20},{18,... | collective-permute-start | bytes 196616 | tf_op jit(solution)/shard_map/ppermute | solution.py:331
  34.3 6.3 %collective-permute-start.4 = (f32[8,8,256]{2,1,0:T(8,128)S(1)}, f32[8,8,256]{2,1,0:T(8,128)S(1)}, u32[]{:S(2)}, u32[]{:S(2)}) collective-permute-start(f32[8,8,256]{2,1,0:T(8,128)S(1)} %get-tuple-element.27), channel_id=1, source_target_pairs={{0,6},{2,4},{4,2},{6,0},{8,14},{10,12},{12,10},{14,8},{16,22},{18,... | collective-permute-start | bytes 196616 | tf_op jit(solution)/shard_map/ppermute | solution.py:331

commit v5 on v4

--- a/solution.py
+++ b/solution.py
@@ -19,29 +19,49 @@
 ROOM = pltpu.CompilerParams(vmem_limit_bytes=8 * 2**20)
 
 
-def regroup_kernel(background, scale_x, scale_y, out, field, along_x, along_y, sems):
+def member(groups):
+    return lax.rem(lax.axis_index("band"), groups)
+
+
+def regroup_kernel(background, scale_x, scale_y, *refs):
+    *pieces, field, along_x, along_y, sems = refs
     variables, levels = background.shape[:2]
-    groups = out.shape[0]
-    part = levels // groups
-    copies = []
-    for q in range(groups):
-        near = pl.ds(q * part, part)
+    part = levels // len(pieces)
+    me = member(len(pieces))
+    parts, copies = [], []
+    for k in range(len(pieces)):
+        near = pl.ds(jnp.bitwise_xor(me, k) * part, part)
+        parts.append(near)
         copies.append(
             [
-                pltpu.make_async_copy(background.at[:, near], field.at[:, near], sems.at[q, 0]),
-                pltpu.make_async_copy(scale_x.at[near], along_x.at[near], sems.at[q, 1]),
-                pltpu.make_async_copy(scale_y.at[near], along_y.at[near], sems.at[q, 2]),
+                pltpu.make_async_copy(background.at[:, near], field.at[:, near], sems.at[k, 0]),
+                pltpu.make_async_copy(scale_x.at[near], along_x.at[near], sems.at[k, 1]),
+                pltpu.make_async_copy(scale_y.at[near], along_y.at[near], sems.at[k, 2]),
             ]
         )
-        for copy in copies[q]:
+        for copy in copies[k]:
             copy.start()
-    for q in range(groups):
-        near = pl.ds(q * part, part)
-        for copy in copies[q]:
+    for near, piece, each in zip(parts, pieces, copies):
+        for copy in each:
             copy.wait()
         sources = [field[v, near] for v in range(variables)]
         sources += [along_x[near], along_y[near]]
-        out[q] = jnp.swapaxes(jnp.concatenate(sources, 0), 0, 1)
+        piece[...] = jnp.swapaxes(jnp.concatenate(sources, 0), 0, 1)
+
+
+def edges_kernel(*refs):
+    *pieces, first, last = refs
+    groups = len(pieces)
+    me = member(groups)
+    for k, piece in enumerate(pieces):
+
+        @pl.when(me == k)
+        def _(piece=piece):
+            first[...] = piece[...]
+
+        @pl.when(me == groups - 1 - k)
+        def _(piece=piece):
+            last[...] = piece[...]
 
 
 def spread_out(source, near, field, along_x, along_y, down_y):
@@ -114,10 +134,14 @@
             copies[(b + 1) * len(copies) // total - 1].start()
 
 
-def inner_kernel(band_rows, mine, field, along_x, along_y, down_y, sides, result, bands, ready, sems):
-    groups, width, channels, rows = mine.shape
-    for s in range(groups):
-        spread_out(mine.at[s], pl.ds(s * width, width), field, along_x, along_y, down_y)
+def inner_kernel(groups, band_rows, *refs):
+    pieces, field, along_x, along_y, down_y = refs[:groups], *refs[groups : groups + 4]
+    sides, result, bands, ready, sems = refs[groups + 4 :]
+    width = pieces[0].shape[0]
+    me = member(groups)
+    for k, piece in enumerate(pieces):
+        near = pl.ds(jnp.bitwise_xor(me, k) * width, width)
+        spread_out(piece, near, field, along_x, along_y, down_y)
     span = groups * width
     for step in range(STEPS):
         last = step + 1
@@ -169,7 +193,7 @@
     rows_copy.wait()
     pack(result, band_rows, ready, copies)
 
-    me = lax.rem(lax.axis_index("band"), groups)
+    me = member(groups)
     whole[:, :, pl.ds(width, span - 2 * width)] = inner_result[...]
     whole[:, :, pl.ds(0, width)] = result[:, :, pl.ds(0, width)]
     whole[:, :, pl.ds(span - width, width)] = result[:, :, pl.ds(width, width)]
@@ -196,7 +220,7 @@
     pieces, out, taps, keep, whole = refs[:groups], *refs[groups:]
     variables, levels = out.shape[:2]
     part = levels // groups
-    me = lax.rem(lax.axis_index("band"), groups)
+    me = member(groups)
     for k in range(groups):
         near = pl.ds(jnp.bitwise_xor(me, k) * part, part)
         for v in range(variables):
@@ -252,21 +276,34 @@
     def struct(*shape):
         return jax.ShapeDtypeStruct(shape, f32)
 
+    piece = struct(width, channels, rows)
     parted = pl.pallas_call(
         regroup_kernel,
-        out_shape=struct(groups, width, channels, rows),
+        out_shape=[piece] * groups,
         in_specs=[HBM] * 3,
-        out_specs=VMEM,
+        out_specs=[VMEM] * groups,
         scratch_shapes=[pltpu.VMEM(a.shape, f32) for a in (background, scale_x, scale_y)]
         + [pltpu.SemaphoreType.DMA((groups, 3))],
         compiler_params=ROOM,
         name="regroup",
     )(*(pltpu.with_memory_space_constraint(a, pltpu.HBM) for a in (background, scale_x, scale_y)))
     weights = jnp.transpose(filter_bands, (1, 0, 2))
-    near = [[g * groups + i for i in range(groups)] for g in range(count // groups)]
-    mine = lax.all_to_all(
-        parted, "band", split_axis=0, concat_axis=0, tiled=True, axis_index_groups=near
-    )
+
+    def exchanged(pieces):
+        return [pieces[0]] + [
+            lax.ppermute(pieces[k], "band", [(i, i ^ k) for i in range(count)])
+            for k in range(1, groups)
+        ]
+
+    mine = exchanged(parted)
+    first, last = pl.pallas_call(
+        edges_kernel,
+        out_shape=[piece] * 2,
+        in_specs=[VMEM] * groups,
+        out_specs=[VMEM] * 2,
+        compiler_params=ROOM,
+        name="edges",
+    )(*mine)
 
     def shifted(by):
         total = count * blocks
@@ -282,21 +319,21 @@
         return pairs
 
     axes = ("band", "lon")
-    low = lax.ppermute(mine[groups - 1], axes, shifted(groups))
-    high = lax.ppermute(mine[0], axes, shifted(-groups))
+    low = lax.ppermute(last, axes, shifted(groups))
+    high = lax.ppermute(first, axes, shifted(-groups))
     span = groups * width
     inside = span - 2 * width
     halves = rows // LANES
     both = variables * part
     inner = pl.pallas_call(
-        inner_kernel,
+        functools.partial(inner_kernel, groups),
         out_shape=[struct(span, both, rows)] * 4
         + [
             struct(2, STEPS, both, rows),
             struct(halves, both, inside, LANES),
             struct(count, variables, span, LANES),
         ],
-        in_specs=[SMEM, VMEM],
+        in_specs=[SMEM] + [VMEM] * groups,
         out_specs=[VMEM] * 6 + [HBM],
         scratch_shapes=[
             pltpu.VMEM((count, variables, inside, LANES), f32),
@@ -307,7 +344,7 @@
             flops=20 * STEPS * span * both * rows, bytes_accessed=2**20, transcendentals=0
         ),
         name="inner",
-    )(band_rows, mine)
+    )(band_rows, *mine)
     outs = pl.pallas_call(
         functools.partial(outer_kernel, groups),
         out_shape=[struct(count, variables, span, LANES)] + [struct(both, width, rows)] * groups,
@@ -327,10 +364,7 @@
     )(band_rows, low, high, *inner)
     bands, strips = outs[0], outs[1:]
     arrived = lax.all_to_all(bands, "band", split_axis=0, concat_axis=0, tiled=True)
-    pieces = [strips[0]] + [
-        lax.ppermute(strips[k], "band", [(i, i ^ k) for i in range(count)])
-        for k in range(1, groups)
-    ]
+    pieces = exchanged(strips)
     increment, taps, keep = pl.pallas_call(
         functools.partial(increment_kernel, groups),
         out_shape=[

time: 47.5 us -> 45 us (0.947)
  blocking collectives: 13.5 us -> 0 us
  starting transfers between devices: 10.4 us -> 16.3 us
  waiting for transfers between devices: 13.9 us -> 18.9 us
    all_to_all x1 -> x0, blocking collectives: 13.5 us -> none  [shards(): lax.all_to_all(parted, 'band', split_axis=0, concat_axis=0, tiled=True, a...]
    ppermute x5 -> x8, starting transfers between devices: 5.64 us -> 11.7 us  [the longest x6 8.1 us: exchanged(): lax.ppermute(pieces[k], 'band', [(i, i ^ k) for i in range(count)])]
    ppermute x5 -> x8, waiting for transfers between devices: 9.63 us -> 15.2 us  [the longest x6 12.6 us: exchanged(): lax.ppermute(pieces[k], 'band', [(i, i ^ k) for i in range(count)])]
    all_to_all x1, waiting for transfers between devices: 4.22 us -> 3.69 us  [shards(): lax.all_to_all(bands, 'band', split_axis=0, concat_axis=0, tiled=True)]
    pallas_call x2 -> x3, Pallas kernels: 4.1 us -> 4.17 us  [the longest x1 2.95 us: shards(): pl.pallas_call(functools.partial(inner_kernel, groups), out_shape=[struct...]
  transfers between devices with their start and end apart: 6 -> 9, of which waited for: 4 -> 8; matrix products, arithmetic and copies ran while one was open for 0% -> 0% of each run, Pallas kernels for 9% -> 10%
where the time goes in v5:
time: 45 us; the launch traced here: 44.7 us
  waiting for transfers between devices  18.9 us (42%)
  starting transfers between devices  16.3 us (36%)
  Pallas kernels  8.81 us (20%)
  between operations  0.7 us (2%)
    ppermute x6, waiting for transfers between devices, exchanged(): lax.ppermute(pieces[k], 'band', [(i, i ^ k) for i in range(count)])  12.6 us
    ppermute x6, starting transfers between devices, exchanged(): lax.ppermute(pieces[k], 'band', [(i, i ^ k) for i in range(count)])  8.1 us
    all_to_all x1, starting transfers between devices, shards(): lax.all_to_all(bands, 'band', split_axis=0, concat_axis=0, tiled=True)  4.65 us
    all_to_all x1, waiting for transfers between devices, shards(): lax.all_to_all(bands, 'band', split_axis=0, concat_axis=0, tiled=True)  3.69 us
    pallas_call x1, Pallas kernels, shards(): pl.pallas_call(functools.partial(inner_kernel, groups), out_shape=[struct...  2.95 us
    pallas_call x1, Pallas kernels, shards(): pl.pallas_call(functools.partial(outer_kernel, groups), out_shape=[struct...  2.21 us
    ppermute x1, starting transfers between devices, shards(): high = lax.ppermute(first, axes, shifted(-groups))  1.97 us
    ppermute x1, starting transfers between devices, shards(): low = lax.ppermute(last, axes, shifted(groups))  1.64 us
  transfers between devices with their start and end apart: 9, of which 8 were waited for; matrix products, arithmetic and copies ran while one was open for 0% of the time, Pallas kernels for 10%

profile of v5, /device:TPU:0, one launch (start us, length us, event | category | flops | bytes accessed | tf_op | source)
XLA Modules:
  0.0 44.7 jit_solution(6866595328572010588)
XLA Ops:
  0.6 1.2 %regroup.1 = (f32[8,16,256]{2,1,0:T(8,128)S(1)}, f32[8,16,256]{2,1,0:T(8,128)S(1)}, f32[8,16,256]{2,1,0:T(8,128)S(1)}, f32[8,16,256]{2,1,0:T(8,128)S(1)}) custom-call(f32[2,16,8,256]{3,2,1,0:T(8,128)} %background.1, f32[16,8,256]{2,1,0:T(8,128)} %scale_x.1, f32[16,8,256]{2,1,0:T(8,128)} %scale_y.1), custom_call_target="tpu_custom_call" | custom-call | tf_op jit(solution)/shard_map/regroup/pallas_call | solution.py:280
  1.8 3.0 %collective-permute-start = (f32[8,16,256]{2,1,0:T(8,128)S(1)}, f32[8,16,256]{2,1,0:T(8,128)S(1)}, u32[]{:S(2)}, u32[]{:S(2)}) collective-permute-start(f32[8,16,256]{2,1,0:T(8,128)S(1)} %get-tuple-element.24), channel_id=1, source_target_pairs={{0,2},{2,0},{4,6},{6,4},{8,10},{10,8},{12,14},{14,12},{16,18},{18,... | collective-permute-start | bytes 393224 | tf_op jit(solution)/shard_map/ppermute | solution.py:294
  4.8 1.5 %collective-permute-start.1 = (f32[8,16,256]{2,1,0:T(8,128)S(1)}, f32[8,16,256]{2,1,0:T(8,128)S(1)}, u32[]{:S(2)}, u32[]{:S(2)}) collective-permute-start(f32[8,16,256]{2,1,0:T(8,128)S(1)} %get-tuple-element.25), channel_id=1, source_target_pairs={{0,4},{2,6},{4,0},{6,2},{8,12},{10,14},{12,8},{14,10},{16,20},{18,... | collective-permute-start | bytes 393224 | tf_op jit(solution)/shard_map/ppermute | solution.py:294
  6.3 0.0 collective-permute-start.2
  6.4 2.4 %collective-permute-done.refs_1_ = f32[8,16,256]{2,1,0:T(8,128)S(1)} collective-permute-done((f32[8,16,256]{2,1,0:T(8,128)S(1)}, f32[8,16,256]{2,1,0:T(8,128)S(1)}, u32[]{:S(2)}, u32[]{:S(2)}) %collective-permute-start) | collective-permute-done | bytes 131104 | tf_op jit(solution)/shard_map/ppermute | solution.py:294
  8.7 3.9 %collective-permute-done.1.refs_2_ = f32[8,16,256]{2,1,0:T(8,128)S(1)} collective-permute-done((f32[8,16,256]{2,1,0:T(8,128)S(1)}, f32[8,16,256]{2,1,0:T(8,128)S(1)}, u32[]{:S(2)}, u32[]{:S(2)}) %collective-permute-start.1) | collective-permute-done | bytes 131104 | tf_op jit(solution)/shard_map/ppermute | solution.py:294
  12.6 0.0 collective-permute-done.2.refs_3_
  12.7 0.0 copy-start.1
  12.7 1.6 %collective-permute-start.3 = (f32[8,16,256]{2,1,0:T(8,128)S(1)}, f32[8,16,256]{2,1,0:T(8,128)S(1)}, u32[]{:S(2)}, u32[]{:S(2)}) collective-permute-start(f32[8,16,256]{2,1,0:T(8,128)S(1)} %get-tuple-element.27), channel_id=1, source_target_pairs={{0,8},{2,10},{4,12},{6,14},{8,16},{10,18},{12,20},{14,22},{16,24},... | collective-permute-start | bytes 393224 | tf_op jit(solution)/shard_map/ppermute | solution.py:322
  14.3 2.0 %collective-permute-start.4 = (f32[8,16,256]{2,1,0:T(8,128)S(1)}, f32[8,16,256]{2,1,0:T(8,128)S(1)}, u32[]{:S(2)}, u32[]{:S(2)}) collective-permute-start(f32[8,16,256]{2,1,0:T(8,128)S(1)} %get-tuple-element.28), channel_id=1, source_target_pairs={{0,25},{2,27},{4,29},{6,31},{8,0},{10,2},{12,4},{14,6},{16,8},{18,... | collective-permute-start | bytes 393224 | tf_op jit(solution)/shard_map/ppermute | solution.py:323
  16.3 0.0 copy-done.1
  16.3 2.9 %inner.1 = (f32[32,8,256]{2,1,0:T(8,128)S(1)}, f32[32,8,256]{2,1,0:T(8,128)S(1)}, f32[32,8,256]{2,1,0:T(8,128)S(1)}, f32[32,8,256]{2,1,0:T(8,128)S(1)}, f32[2,8,...) custom-call(s32[16]{0:T(128)S(1)} %copy-done.1, ...), custom_call_target="tpu_custom_call" | custom-call | flops 10485760 | bytes 1048576 | tf_op jit(solution)/shard_map/inner/pallas_call | solution.py:328
  19.2 1.0 %collective-permute-done.3.low = f32[8,16,256]{2,1,0:T(8,128)S(1)} collective-permute-done((f32[8,16,256]{2,1,0:T(8,128)S(1)}, f32[8,16,256]{2,1,0:T(8,128)S(1)}, u32[]{:S(2)}, u32[]{:S(2)}) %collective-permute-start.3) | collective-permute-done | bytes 131104 | tf_op jit(solution)/shard_map/ppermute | solution.py:322
  20.2 1.6 %collective-permute-done.4.high = f32[8,16,256]{2,1,0:T(8,128)S(1)} collective-permute-done((f32[8,16,256]{2,1,0:T(8,128)S(1)}, f32[8,16,256]{2,1,0:T(8,128)S(1)}, u32[]{:S(2)}, u32[]{:S(2)}) %collective-permute-start.4) | collective-permute-done | bytes 131104 | tf_op jit(solution)/shard_map/ppermute | solution.py:323
  21.8 2.2 %outer.1 = (f32[16,2,32,128]{3,2,1,0:T(8,128)}, f32[8,8,256]{2,1,0:T(8,128)S(1)}, f32[8,8,256]{2,1,0:T(8,128)S(1)}, f32[8,8,256]{2,1,0:T(8,128)S(1)}, f32[8,8,256]{2,1,0:T(8,128)S(1)}) custom-call(s32[16]{0:T(128)S(1)} %copy-done.1, f32[8,16,256]{2,1,0:T(8,128)S(1)} %collective-permute-done.3.low, ...), custom_call_target="tpu_custom_call", output_to_operand_aliasing={{0}: (9, {})} | custom-call | tf_op jit(solution)/shard_map/outer/pallas_call | solution.py:348
  24.0 4.6 %all-to-all-start = ((f32[16,2,32,128]{3,2,1,0:T(8,128)}), f32[16,2,32,128]{3,2,1,0:T(8,128)S(1)}, u32[]{:S(2)}, u32[]{:S(2)}) async-start(f32[16,2,32,128]{3,2,1,0:T(8,128)} %get-tuple-element.43), calls=%async_computation | async-start | bytes 1048576 | tf_op jit(solution)/shard_map/all_to_all | solution.py:366
  28.7 0.0 copy-start
  28.7 2.0 %collective-permute-start.5 = (f32[8,8,256]{2,1,0:T(8,128)S(1)}, f32[8,8,256]{2,1,0:T(8,128)S(1)}, u32[]{:S(2)}, u32[]{:S(2)}) collective-permute-start(f32[8,8,256]{2,1,0:T(8,128)S(1)} %get-tuple-element.37), channel_id=1, source_target_pairs={{0,2},{2,0},{4,6},{6,4},{8,10},{10,8},{12,14},{14,12},{16,18},{18,... | collective-permute-start | bytes 196616 | tf_op jit(solution)/shard_map/ppermute | solution.py:294
  30.7 1.5 %collective-permute-start.6 = (f32[8,8,256]{2,1,0:T(8,128)S(1)}, f32[8,8,256]{2,1,0:T(8,128)S(1)}, u32[]{:S(2)}, u32[]{:S(2)}) collective-permute-start(f32[8,8,256]{2,1,0:T(8,128)S(1)} %get-tuple-element.38), channel_id=1, source_target_pairs={{0,4},{2,6},{4,0},{6,2},{8,12},{10,14},{12,8},{14,10},{16,20},{18,... | collective-permute-start | bytes 196616 | tf_op jit(solution)/shard_map/ppermute | solution.py:294
  32.1 0.1 collective-permute-start.7
  32.2 2.8 %collective-permute-done.5.refs_1_ = f32[8,8,256]{2,1,0:T(8,128)S(1)} collective-permute-done((f32[8,8,256]{2,1,0:T(8,128)S(1)}, f32[8,8,256]{2,1,0:T(8,128)S(1)}, u32[]{:S(2)}, u32[]{:S(2)}) %collective-permute-start.5) | collective-permute-done | bytes 65568 | tf_op jit(solution)/shard_map/ppermute | solution.py:294
  35.0 2.4 %collective-permute-done.6.refs_2_ = f32[8,8,256]{2,1,0:T(8,128)S(1)} collective-permute-done((f32[8,8,256]{2,1,0:T(8,128)S(1)}, f32[8,8,256]{2,1,0:T(8,128)S(1)}, u32[]{:S(2)}, u32[]{:S(2)}) %collective-permute-start.6) | collective-permute-done | bytes 65568 | tf_op jit(solution)/shard_map/ppermute | solution.py:294
  37.5 1.2 %collective-permute-done.7.refs_3_ = f32[8,8,256]{2,1,0:T(8,128)S(1)} collective-permute-done((f32[8,8,256]{2,1,0:T(8,128)S(1)}, f32[8,8,256]{2,1,0:T(8,128)S(1)}, u32[]{:S(2)}, u32[]{:S(2)}) %collective-permute-start.7) | collective-permute-done | bytes 65568 | tf_op jit(solution)/shard_map/ppermute | solution.py:294
  38.6 0.0 copy-done
  38.6 1.5 %increment.1 = (f32[2,16,8,256]{3,2,1,0:T(8,128)}, f32[5,2,16,1,128]{4,3,2,1,0:T(1,128)S(1)}, s32[32,128]{1,0:T(8,128)S(1)}) custom-call(s32[16]{0:T(128)S(1)} %copy-done.1, f32[5,2,16]{2,1,0:T(2,128)S(1)} %bitcast.1, f32[8,8,256]{2,1,0:T(8,128)S(1)} %get-tuple-element.36.refs_0_, f32[8,8,256]{2,1,0:T(8,128)S(1)} %collective-permute-done.5.refs_1_, ...), custom_call_target="tpu_custom_call" | custom-call | tf_op jit(solution)/shard_map/increment/pallas_call | solution.py:368
  40.1 3.7 %all-to-all-done.arrived = f32[16,2,32,128]{3,2,1,0:T(8,128)S(1)} async-done(((f32[16,2,32,128]{3,2,1,0:T(8,128)}), f32[16,2,32,128]{3,2,1,0:T(8,128)S(1)}, u32[]{:S(2)}, u32[]{:S(2)}) %all-to-all-start) | async-done | bytes 524320 | tf_op jit(solution)/shard_map/all_to_all | solution.py:366
  43.8 1.0 %bands.1 = f32[2,16,32,128]{3,2,1,0:T(8,128)} custom-call(f32[5,2,16,1,128]{4,3,2,1,0:T(1,128)S(1)} %get-tuple-element.41.taps, s32[32,128]{1,0:T(8,128)S(1)} %get-tuple-element.42.keep, f32[16,2,32,128]{3,2,1,0:T(8,128)S(1)} %all-to-all-done.arrived), custom_call_target="tpu_custom_call" | custom-call | tf_op jit(solution)/shard_map/bands/pallas_call | solution.py:381
  (1 shorter events, 0.0 us)
Async XLA Ops:
  1.8 6.9 %collective-permute-start = (f32[8,16,256]{2,1,0:T(8,128)S(1)}, f32[8,16,256]{2,1,0:T(8,128)S(1)}, u32[]{:S(2)}, u32[]{:S(2)}) collective-permute-start(f32[8,16,256]{2,1,0:T(8,128)S(1)} %get-tuple-element.24), channel_id=1, source_target_pairs={{0,2},{2,0},{4,6},{6,4},{8,10},{10,8},{12,14},{14,12},{16,18},{18,... | collective-permute-start | bytes 393224 | tf_op jit(solution)/shard_map/ppermute | solution.py:294
  4.8 7.8 %collective-permute-start.1 = (f32[8,16,256]{2,1,0:T(8,128)S(1)}, f32[8,16,256]{2,1,0:T(8,128)S(1)}, u32[]{:S(2)}, u32[]{:S(2)}) collective-permute-start(f32[8,16,256]{2,1,0:T(8,128)S(1)} %get-tuple-element.25), channel_id=1, source_target_pairs={{0,4},{2,6},{4,0},{6,2},{8,12},{10,14},{12,8},{14,10},{16,20},{18,... | collective-permute-start | bytes 393224 | tf_op jit(solution)/shard_map/ppermute | solution.py:294
  6.3 6.3 %collective-permute-start.2 = (f32[8,16,256]{2,1,0:T(8,128)S(1)}, f32[8,16,256]{2,1,0:T(8,128)S(1)}, u32[]{:S(2)}, u32[]{:S(2)}) collective-permute-start(f32[8,16,256]{2,1,0:T(8,128)S(1)} %get-tuple-element.26), channel_id=1, source_target_pairs={{0,6},{2,4},{4,2},{6,0},{8,14},{10,12},{12,10},{14,8},{16,22},{18,... | collective-permute-start | bytes 393224 | tf_op jit(solution)/shard_map/ppermute | solution.py:294
  12.7 3.6 %copy-start.1 = (s32[16]{0:T(128)S(1)}, s32[16]{0:T(128)}, u32[]{:S(2)}) copy-start(s32[16]{0:T(128)} %band_rows.3) | copy-start | bytes 196
  12.7 7.5 %collective-permute-start.3 = (f32[8,16,256]{2,1,0:T(8,128)S(1)}, f32[8,16,256]{2,1,0:T(8,128)S(1)}, u32[]{:S(2)}, u32[]{:S(2)}) collective-permute-start(f32[8,16,256]{2,1,0:T(8,128)S(1)} %get-tuple-element.27), channel_id=1, source_target_pairs={{0,8},{2,10},{4,12},{6,14},{8,16},{10,18},{12,20},{14,22},{16,24},... | collective-permute-start | bytes 393224 | tf_op jit(solution)/shard_map/ppermute | solution.py:322
  14.3 7.5 %collective-permute-start.4 = (f32[8,16,256]{2,1,0:T(8,128)S(1)}, f32[8,16,256]{2,1,0:T(8,128)S(1)}, u32[]{:S(2)}, u32[]{:S(2)}) collective-permute-start(f32[8,16,256]{2,1,0:T(8,128)S(1)} %get-tuple-element.28), channel_id=1, source_target_pairs={{0,25},{2,27},{4,29},{6,31},{8,0},{10,2},{12,4},{14,6},{16,8},{18,... | collective-permute-start | bytes 393224 | tf_op jit(solution)/shard_map/ppermute | solution.py:323
  24.0 19.8 %all-to-all-start = ((f32[16,2,32,128]{3,2,1,0:T(8,128)}), f32[16,2,32,128]{3,2,1,0:T(8,128)S(1)}, u32[]{:S(2)}, u32[]{:S(2)}) async-start(f32[16,2,32,128]{3,2,1,0:T(8,128)} %get-tuple-element.43), calls=%async_computation | async-start | bytes 1048576 | tf_op jit(solution)/shard_map/all_to_all | solution.py:366
  28.7 10.0 %copy-start = (f32[2,5,16]{2,0,1:T(2,128)S(1)}, f32[2,5,16]{2,0,1:T(2,128)}, u32[]{:S(2)}) copy-start(f32[2,5,16]{2,0,1:T(2,128)} %param.8) | copy-start | bytes 1924
  28.7 6.4 %collective-permute-start.5 = (f32[8,8,256]{2,1,0:T(8,128)S(1)}, f32[8,8,256]{2,1,0:T(8,128)S(1)}, u32[]{:S(2)}, u32[]{:S(2)}) collective-permute-start(f32[8,8,256]{2,1,0:T(8,128)S(1)} %get-tuple-element.37), channel_id=1, source_target_pairs={{0,2},{2,0},{4,6},{6,4},{8,10},{10,8},{12,14},{14,12},{16,18},{18,... | collective-permute-start | bytes 196616 | tf_op jit(solution)/shard_map/ppermute | solution.py:294
  30.7 6.8 %collective-permute-start.6 = (f32[8,8,256]{2,1,0:T(8,128)S(1)}, f32[8,8,256]{2,1,0:T(8,128)S(1)}, u32[]{:S(2)}, u32[]{:S(2)}) collective-permute-start(f32[8,8,256]{2,1,0:T(8,128)S(1)} %get-tuple-element.38), channel_id=1, source_target_pairs={{0,4},{2,6},{4,0},{6,2},{8,12},{10,14},{12,8},{14,10},{16,20},{18,... | collective-permute-start | bytes 196616 | tf_op jit(solution)/shard_map/ppermute | solution.py:294
  32.1 6.5 %collective-permute-start.7 = (f32[8,8,256]{2,1,0:T(8,128)S(1)}, f32[8,8,256]{2,1,0:T(8,128)S(1)}, u32[]{:S(2)}, u32[]{:S(2)}) collective-permute-start(f32[8,8,256]{2,1,0:T(8,128)S(1)} %get-tuple-element.39), channel_id=1, source_target_pairs={{0,6},{2,4},{4,2},{6,0},{8,14},{10,12},{12,10},{14,8},{16,22},{18,... | collective-permute-start | bytes 196616 | tf_op jit(solution)/shard_map/ppermute | solution.py:294

commit v6 on v5

--- a/solution.py
+++ b/solution.py
@@ -160,51 +160,48 @@
     copy.wait()
 
 
-def outer_kernel(groups, rows_far, low, high, *refs):
-    inner, sides, inner_result, _, bands = refs[:4], *refs[4:8]
-    strips = refs[8 : 8 + groups]
-    ends, result, whole, ready, band_rows, sems = refs[8 + groups : 12 + groups], *refs[12 + groups :]
+def end_kernel(groups, side, rows_far, halo, *refs):
+    inner, sides, _, bands, result = refs[:4], *refs[4:8]
+    end, ready, band_rows, sems = refs[8:12], *refs[12:]
     rows_copy = pltpu.make_async_copy(rows_far, band_rows, sems.at[groups])
     rows_copy.start()
-    width, _, rows = low.shape
+    width = halo.shape[0]
     span = groups * width
-    for side, (halo, own) in enumerate(((low, 0), (high, span - width))):
-        arrays = [end.at[side] for end in ends]
-        spread_out(halo, pl.ds(side * width, width), *arrays)
-        for end, array in zip(arrays, inner):
-            end[pl.ds((1 - side) * width, width)] = array[pl.ds(own, width)]
+    spread_out(halo, pl.ds(side * width, width), *end)
+    for here, array in zip(end, inner):
+        here[pl.ds((1 - side) * width, width)] = array[pl.ds(side * (span - width), width)]
     for step in range(STEPS):
-        pieces = []
-        for side, first in enumerate((step + 1, width - 1 - step)):
-            arrays = [end.at[side] for end in ends]
-            faces = (sides[1, step], None) if side else (None, sides[0, step])
-            pieces.append((*arrays, first, first + width, *faces))
-        advance(pieces)
-    field = ends[0]
-    turn(field[0, pl.ds(width, width)], result, pl.ds(0, width))
-    turn(field[1, pl.ds(0, width)], result, pl.ds(width, width))
+        first = width - 1 - step if side else step + 1
+        faces = (sides[1, step], None) if side else (None, sides[0, step])
+        advance([(*end, first, first + width, *faces)])
+    turn(end[0][pl.ds((1 - side) * width, width)], result, pl.ds(0, width))
 
     copies = []
     each = bands.shape[0] // groups
     for i in range(groups):
         near = pl.ds(i * each, each)
-        target = bands.at[near, :, pl.ds(span - 2 * width, 2 * width)]
+        target = bands.at[near, :, pl.ds(span - (2 - side) * width, width)]
         copies.append(pltpu.make_async_copy(ready.at[near], target, sems.at[i]))
     rows_copy.wait()
     pack(result, band_rows, ready, copies)
-
+    for copy in copies:
+        copy.wait()
+
+
+def strips_kernel(groups, low, inner, high, *refs):
+    strips, whole = refs[:groups], refs[groups]
+    halves, _, width, _ = low.shape
+    span = groups * width
     me = member(groups)
-    whole[:, :, pl.ds(width, span - 2 * width)] = inner_result[...]
-    whole[:, :, pl.ds(0, width)] = result[:, :, pl.ds(0, width)]
-    whole[:, :, pl.ds(span - width, width)] = result[:, :, pl.ds(width, width)]
+    whole[:, :, pl.ds(0, width)] = low[...]
+    whole[:, :, pl.ds(width, span - 2 * width)] = inner[...]
+    whole[:, :, pl.ds(span - width, width)] = high[...]
     for k in range(groups):
         s = jnp.bitwise_xor(me, k)
-        for half in range(rows // LANES):
+        for half in range(halves):
             strips[k][:, :, half * LANES : (half + 1) * LANES] = whole[
                 half, :, pl.ds(pl.multiple_of(s * width, width), width)
             ]
-    for copy in copies:
-        copy.wait()
 
 
 def filtered(taps, v, l, levels, whole):
@@ -345,24 +342,39 @@
         ),
         name="inner",
     )(band_rows, *mine)
-    outs = pl.pallas_call(
-        functools.partial(outer_kernel, groups),
-        out_shape=[struct(count, variables, span, LANES)] + [struct(both, width, rows)] * groups,
-        in_specs=[HBM] + [VMEM] * 8 + [HBM],
-        out_specs=[HBM] + [VMEM] * groups,
-        input_output_aliases={9: 0},
-        scratch_shapes=[pltpu.VMEM((2, 2 * width, both, rows), f32)] * 4
-        + [
-            pltpu.VMEM((halves, both, 2 * width, LANES), f32),
-            pltpu.VMEM((halves, both, span, LANES), f32),
-            pltpu.VMEM((count, variables, 2 * width, LANES), f32),
-            pltpu.SMEM(band_rows.shape, band_rows.dtype),
-            pltpu.SemaphoreType.DMA((groups + 1,)),
-        ],
-        compiler_params=ROOM,
-        name="outer",
-    )(band_rows, low, high, *inner)
-    bands, strips = outs[0], outs[1:]
+    *arrays, inner_result, bands = inner
+
+    def finished(side, halo, bands):
+        return pl.pallas_call(
+            functools.partial(end_kernel, groups, side),
+            out_shape=[
+                struct(count, variables, span, LANES),
+                struct(halves, both, width, LANES),
+            ],
+            in_specs=[HBM] + [VMEM] * 6 + [HBM],
+            out_specs=[HBM, VMEM],
+            input_output_aliases={7: 0},
+            scratch_shapes=[pltpu.VMEM((2 * width, both, rows), f32)] * 4
+            + [
+                pltpu.VMEM((count, variables, width, LANES), f32),
+                pltpu.SMEM(band_rows.shape, band_rows.dtype),
+                pltpu.SemaphoreType.DMA((groups + 1,)),
+            ],
+            compiler_params=ROOM,
+            name="high_end" if side else "low_end",
+        )(band_rows, halo, *arrays, bands)
+
+    bands, low_result = finished(0, low, bands)
+    bands, high_result = finished(1, high, bands)
+    strips = pl.pallas_call(
+        functools.partial(strips_kernel, groups),
+        out_shape=[struct(both, width, rows)] * groups,
+        in_specs=[VMEM] * 3,
+        out_specs=[VMEM] * groups,
+        scratch_shapes=[pltpu.VMEM((halves, both, span, LANES), f32)],
+        compiler_params=ROOM,
+        name="strips",
+    )(low_result, inner_result, high_result)
     arrived = lax.all_to_all(bands, "band", split_axis=0, concat_axis=0, tiled=True)
     pieces = exchanged(strips)
     increment, taps, keep = pl.pallas_call(

time: 45 us -> 44.6 us (level)
  waiting for transfers between devices: 18.9 us -> 15.6 us
  starting transfers between devices: 16.3 us -> 17.9 us
  Pallas kernels: 8.81 us -> 10.1 us
    ppermute x1, waiting for transfers between devices: 1.57 us -> 0.01 us  [shards(): high = lax.ppermute(first, axes, shifted(-groups))]
    all_to_all x1, starting transfers between devices: 4.65 us -> 6.22 us  [shards(): lax.all_to_all(bands, 'band', split_axis=0, concat_axis=0, tiled=True)]
    pallas_call x1 -> x3, Pallas kernels: 2.21 us -> 3.46 us  [the longest x2 3.41 us: finished(): pl.pallas_call(functools.partial(end_kernel, groups, side), out_shape=[st...]
    all_to_all x1, waiting for transfers between devices: 3.69 us -> 2.68 us  [shards(): lax.all_to_all(bands, 'band', split_axis=0, concat_axis=0, tiled=True)]
    ppermute x6, waiting for transfers between devices: 12.6 us -> 11.9 us  [exchanged(): lax.ppermute(pieces[k], 'band', [(i, i ^ k) for i in range(count)])]
  transfers between devices with their start and end apart: 9 -> 9, of which waited for: 8 -> 6; matrix products, arithmetic and copies ran while one was open for 0% -> 0% of each run, Pallas kernels for 10% -> 14%
where the time goes in v6:
time: 44.6 us; the launch traced here: 44.3 us
  starting transfers between devices  17.9 us (40%)
  waiting for transfers between devices  15.6 us (35%)
  Pallas kernels  10.1 us (23%)
  between operations  0.72 us (2%)
    ppermute x6, waiting for transfers between devices, exchanged(): lax.ppermute(pieces[k], 'band', [(i, i ^ k) for i in range(count)])  11.9 us
    ppermute x6, starting transfers between devices, exchanged(): lax.ppermute(pieces[k], 'band', [(i, i ^ k) for i in range(count)])  8.1 us
    all_to_all x1, starting transfers between devices, shards(): lax.all_to_all(bands, 'band', split_axis=0, concat_axis=0, tiled=True)  6.22 us
    pallas_call x2, Pallas kernels, finished(): pl.pallas_call(functools.partial(end_kernel, groups, side), out_shape=[st...  3.41 us
    pallas_call x1, Pallas kernels, shards(): pl.pallas_call(functools.partial(inner_kernel, groups), out_shape=[struct...  2.95 us
    all_to_all x1, waiting for transfers between devices, shards(): lax.all_to_all(bands, 'band', split_axis=0, concat_axis=0, tiled=True)  2.68 us
    ppermute x1, starting transfers between devices, shards(): high = lax.ppermute(first, axes, shifted(-groups))  1.97 us
    ppermute x1, starting transfers between devices, shards(): low = lax.ppermute(last, axes, shifted(groups))  1.64 us
  transfers between devices with their start and end apart: 9, of which 6 were waited for; matrix products, arithmetic and copies ran while one was open for 0% of the time, Pallas kernels for 14%

profile of v6, /device:TPU:0, one launch (start us, length us, event | category | flops | bytes accessed | tf_op | source)
XLA Modules:
  0.0 44.3 jit_solution(10661627722493058856)
XLA Ops:
  0.6 1.2 %regroup.1 = (f32[8,16,256]{2,1,0:T(8,128)S(1)}, f32[8,16,256]{2,1,0:T(8,128)S(1)}, f32[8,16,256]{2,1,0:T(8,128)S(1)}, f32[8,16,256]{2,1,0:T(8,128)S(1)}) custom-call(f32[2,16,8,256]{3,2,1,0:T(8,128)} %background.1, f32[16,8,256]{2,1,0:T(8,128)} %scale_x.1, f32[16,8,256]{2,1,0:T(8,128)} %scale_y.1), custom_call_target="tpu_custom_call" | custom-call | tf_op jit(solution)/shard_map/regroup/pallas_call | solution.py:277
  1.8 3.0 %collective-permute-start = (f32[8,16,256]{2,1,0:T(8,128)S(1)}, f32[8,16,256]{2,1,0:T(8,128)S(1)}, u32[]{:S(2)}, u32[]{:S(2)}) collective-permute-start(f32[8,16,256]{2,1,0:T(8,128)S(1)} %get-tuple-element.27), channel_id=1, source_target_pairs={{0,2},{2,0},{4,6},{6,4},{8,10},{10,8},{12,14},{14,12},{16,18},{18,... | collective-permute-start | bytes 393224 | tf_op jit(solution)/shard_map/ppermute | solution.py:291
  4.8 1.5 %collective-permute-start.1 = (f32[8,16,256]{2,1,0:T(8,128)S(1)}, f32[8,16,256]{2,1,0:T(8,128)S(1)}, u32[]{:S(2)}, u32[]{:S(2)}) collective-permute-start(f32[8,16,256]{2,1,0:T(8,128)S(1)} %get-tuple-element.28), channel_id=1, source_target_pairs={{0,4},{2,6},{4,0},{6,2},{8,12},{10,14},{12,8},{14,10},{16,20},{18,... | collective-permute-start | bytes 393224 | tf_op jit(solution)/shard_map/ppermute | solution.py:291
  6.3 0.0 collective-permute-start.2
  6.4 2.4 %collective-permute-done.refs_1_ = f32[8,16,256]{2,1,0:T(8,128)S(1)} collective-permute-done((f32[8,16,256]{2,1,0:T(8,128)S(1)}, f32[8,16,256]{2,1,0:T(8,128)S(1)}, u32[]{:S(2)}, u32[]{:S(2)}) %collective-permute-start) | collective-permute-done | bytes 131104 | tf_op jit(solution)/shard_map/ppermute | solution.py:291
  8.7 3.9 %collective-permute-done.1.refs_2_ = f32[8,16,256]{2,1,0:T(8,128)S(1)} collective-permute-done((f32[8,16,256]{2,1,0:T(8,128)S(1)}, f32[8,16,256]{2,1,0:T(8,128)S(1)}, u32[]{:S(2)}, u32[]{:S(2)}) %collective-permute-start.1) | collective-permute-done | bytes 131104 | tf_op jit(solution)/shard_map/ppermute | solution.py:291
  12.6 0.0 collective-permute-done.2.refs_3_
  12.7 0.0 copy-start
  12.7 1.6 %collective-permute-start.3 = (f32[8,16,256]{2,1,0:T(8,128)S(1)}, f32[8,16,256]{2,1,0:T(8,128)S(1)}, u32[]{:S(2)}, u32[]{:S(2)}) collective-permute-start(f32[8,16,256]{2,1,0:T(8,128)S(1)} %get-tuple-element.30), channel_id=1, source_target_pairs={{0,8},{2,10},{4,12},{6,14},{8,16},{10,18},{12,20},{14,22},{16,24},... | collective-permute-start | bytes 393224 | tf_op jit(solution)/shard_map/ppermute | solution.py:319
  14.3 2.0 %collective-permute-start.4 = (f32[8,16,256]{2,1,0:T(8,128)S(1)}, f32[8,16,256]{2,1,0:T(8,128)S(1)}, u32[]{:S(2)}, u32[]{:S(2)}) collective-permute-start(f32[8,16,256]{2,1,0:T(8,128)S(1)} %get-tuple-element.39), channel_id=1, source_target_pairs={{0,25},{2,27},{4,29},{6,31},{8,0},{10,2},{12,4},{14,6},{16,8},{18,... | collective-permute-start | bytes 393224 | tf_op jit(solution)/shard_map/ppermute | solution.py:320
  16.3 0.0 copy-done
  16.3 2.9 %inner.1 = (f32[32,8,256]{2,1,0:T(8,128)S(1)}, f32[32,8,256]{2,1,0:T(8,128)S(1)}, f32[32,8,256]{2,1,0:T(8,128)S(1)}, f32[32,8,256]{2,1,0:T(8,128)S(1)}, f32[2,8,...) custom-call(s32[16]{0:T(128)S(1)} %copy-done, ...), custom_call_target="tpu_custom_call" | custom-call | flops 10485760 | bytes 1048576 | tf_op jit(solution)/shard_map/inner/pallas_call | solution.py:325
  19.2 1.0 %collective-permute-done.3.halo = f32[8,16,256]{2,1,0:T(8,128)S(1)} collective-permute-done((f32[8,16,256]{2,1,0:T(8,128)S(1)}, f32[8,16,256]{2,1,0:T(8,128)S(1)}, u32[]{:S(2)}, u32[]{:S(2)}) %collective-permute-start.3) | collective-permute-done | bytes 131104 | tf_op jit(solution)/shard_map/ppermute | solution.py:319
  20.2 1.7 %low_end.1 = (f32[16,2,32,128]{3,2,1,0:T(8,128)}, f32[2,8,8,128]{3,2,1,0:T(8,128)S(1)}) custom-call(s32[16]{0:T(128)S(1)} %copy-done, f32[8,16,256]{2,1,0:T(8,128)S(1)} %collective-permute-done.3.halo, f32[32,8,256]{2,1,0:T(8,128)S(1)} %get-tuple-element.31.refs_0_, f32[32,8,256]{2,1,0:T(8,128)S(1)} %get-tuple-element.32.refs_1_, ...), custom_call_target="tpu_custom_call", output_to_operand_aliasing={{0}: (7, {})} | custom-call | tf_op jit(solution)/shard_map/low_end/pallas_call | solution.py:348
  21.9 0.0 collective-permute-done.4.halo
  21.9 1.7 %high_end.1 = (f32[16,2,32,128]{3,2,1,0:T(8,128)}, f32[2,8,8,128]{3,2,1,0:T(8,128)S(1)}) custom-call(s32[16]{0:T(128)S(1)} %copy-done, f32[8,16,256]{2,1,0:T(8,128)S(1)} %collective-permute-done.4.halo, f32[32,8,256]{2,1,0:T(8,128)S(1)} %get-tuple-element.31.refs_0_, f32[32,8,256]{2,1,0:T(8,128)S(1)} %get-tuple-element.32.refs_1_, ...), custom_call_target="tpu_custom_call", output_to_operand_aliasing={{0}: (7, {})} | custom-call | tf_op jit(solution)/shard_map/high_end/pallas_call | solution.py:348
  23.6 6.2 %all-to-all-start = ((f32[16,2,32,128]{3,2,1,0:T(8,128)}), f32[16,2,32,128]{3,2,1,0:T(8,128)S(1)}, u32[]{:S(2)}, u32[]{:S(2)}) async-start(f32[16,2,32,128]{3,2,1,0:T(8,128)} %get-tuple-element.49), calls=%async_computation | async-start | bytes 1048576 | tf_op jit(solution)/shard_map/all_to_all | solution.py:378
  29.9 0.1 strips.1
  29.9 0.0 copy-start.1
  29.9 2.0 %collective-permute-start.5 = (f32[8,8,256]{2,1,0:T(8,128)S(1)}, f32[8,8,256]{2,1,0:T(8,128)S(1)}, u32[]{:S(2)}, u32[]{:S(2)}) collective-permute-start(f32[8,8,256]{2,1,0:T(8,128)S(1)} %get-tuple-element.43), channel_id=1, source_target_pairs={{0,2},{2,0},{4,6},{6,4},{8,10},{10,8},{12,14},{14,12},{16,18},{18,... | collective-permute-start | bytes 196616 | tf_op jit(solution)/shard_map/ppermute | solution.py:291
  31.9 1.5 %collective-permute-start.6 = (f32[8,8,256]{2,1,0:T(8,128)S(1)}, f32[8,8,256]{2,1,0:T(8,128)S(1)}, u32[]{:S(2)}, u32[]{:S(2)}) collective-permute-start(f32[8,8,256]{2,1,0:T(8,128)S(1)} %get-tuple-element.44), channel_id=1, source_target_pairs={{0,4},{2,6},{4,0},{6,2},{8,12},{10,14},{12,8},{14,10},{16,20},{18,... | collective-permute-start | bytes 196616 | tf_op jit(solution)/shard_map/ppermute | solution.py:291
  33.4 0.1 collective-permute-start.7
  33.5 3.6 %collective-permute-done.5.refs_1_ = f32[8,8,256]{2,1,0:T(8,128)S(1)} collective-permute-done((f32[8,8,256]{2,1,0:T(8,128)S(1)}, f32[8,8,256]{2,1,0:T(8,128)S(1)}, u32[]{:S(2)}, u32[]{:S(2)}) %collective-permute-start.5) | collective-permute-done | bytes 65568 | tf_op jit(solution)/shard_map/ppermute | solution.py:291
  37.1 0.0 collective-permute-done.6.refs_2_
  37.1 2.1 %collective-permute-done.7.refs_3_ = f32[8,8,256]{2,1,0:T(8,128)S(1)} collective-permute-done((f32[8,8,256]{2,1,0:T(8,128)S(1)}, f32[8,8,256]{2,1,0:T(8,128)S(1)}, u32[]{:S(2)}, u32[]{:S(2)}) %collective-permute-start.7) | collective-permute-done | bytes 65568 | tf_op jit(solution)/shard_map/ppermute | solution.py:291
  39.2 0.0 copy-done.1
  39.2 1.5 %increment.1 = (f32[2,16,8,256]{3,2,1,0:T(8,128)}, f32[5,2,16,1,128]{4,3,2,1,0:T(1,128)S(1)}, s32[32,128]{1,0:T(8,128)S(1)}) custom-call(s32[16]{0:T(128)S(1)} %copy-done, f32[5,2,16]{2,1,0:T(2,128)S(1)} %bitcast.1, f32[8,8,256]{2,1,0:T(8,128)S(1)} %get-tuple-element.42.refs_0_, f32[8,8,256]{2,1,0:T(8,128)S(1)} %collective-permute-done.5.refs_1_, ...), custom_call_target="tpu_custom_call" | custom-call | tf_op jit(solution)/shard_map/increment/pallas_call | solution.py:380
  40.6 2.7 %all-to-all-done.arrived = f32[16,2,32,128]{3,2,1,0:T(8,128)S(1)} async-done(((f32[16,2,32,128]{3,2,1,0:T(8,128)}), f32[16,2,32,128]{3,2,1,0:T(8,128)S(1)}, u32[]{:S(2)}, u32[]{:S(2)}) %all-to-all-start) | async-done | bytes 524320 | tf_op jit(solution)/shard_map/all_to_all | solution.py:378
  43.3 1.0 %bands.1 = f32[2,16,32,128]{3,2,1,0:T(8,128)} custom-call(f32[5,2,16,1,128]{4,3,2,1,0:T(1,128)S(1)} %get-tuple-element.47.taps, s32[32,128]{1,0:T(8,128)S(1)} %get-tuple-element.48.keep, f32[16,2,32,128]{3,2,1,0:T(8,128)S(1)} %all-to-all-done.arrived), custom_call_target="tpu_custom_call" | custom-call | tf_op jit(solution)/shard_map/bands/pallas_call | solution.py:393
  (1 shorter events, 0.0 us)
Async XLA Ops:
  1.8 6.9 %collective-permute-start = (f32[8,16,256]{2,1,0:T(8,128)S(1)}, f32[8,16,256]{2,1,0:T(8,128)S(1)}, u32[]{:S(2)}, u32[]{:S(2)}) collective-permute-start(f32[8,16,256]{2,1,0:T(8,128)S(1)} %get-tuple-element.27), channel_id=1, source_target_pairs={{0,2},{2,0},{4,6},{6,4},{8,10},{10,8},{12,14},{14,12},{16,18},{18,... | collective-permute-start | bytes 393224 | tf_op jit(solution)/shard_map/ppermute | solution.py:291
  4.8 7.8 %collective-permute-start.1 = (f32[8,16,256]{2,1,0:T(8,128)S(1)}, f32[8,16,256]{2,1,0:T(8,128)S(1)}, u32[]{:S(2)}, u32[]{:S(2)}) collective-permute-start(f32[8,16,256]{2,1,0:T(8,128)S(1)} %get-tuple-element.28), channel_id=1, source_target_pairs={{0,4},{2,6},{4,0},{6,2},{8,12},{10,14},{12,8},{14,10},{16,20},{18,... | collective-permute-start | bytes 393224 | tf_op jit(solution)/shard_map/ppermute | solution.py:291
  6.3 6.3 %collective-permute-start.2 = (f32[8,16,256]{2,1,0:T(8,128)S(1)}, f32[8,16,256]{2,1,0:T(8,128)S(1)}, u32[]{:S(2)}, u32[]{:S(2)}) collective-permute-start(f32[8,16,256]{2,1,0:T(8,128)S(1)} %get-tuple-element.29), channel_id=1, source_target_pairs={{0,6},{2,4},{4,2},{6,0},{8,14},{10,12},{12,10},{14,8},{16,22},{18,... | collective-permute-start | bytes 393224 | tf_op jit(solution)/shard_map/ppermute | solution.py:291
  12.7 3.6 %copy-start = (s32[16]{0:T(128)S(1)}, s32[16]{0:T(128)}, u32[]{:S(2)}) copy-start(s32[16]{0:T(128)} %band_rows.3) | copy-start | bytes 196
  12.7 7.5 %collective-permute-start.3 = (f32[8,16,256]{2,1,0:T(8,128)S(1)}, f32[8,16,256]{2,1,0:T(8,128)S(1)}, u32[]{:S(2)}, u32[]{:S(2)}) collective-permute-start(f32[8,16,256]{2,1,0:T(8,128)S(1)} %get-tuple-element.30), channel_id=1, source_target_pairs={{0,8},{2,10},{4,12},{6,14},{8,16},{10,18},{12,20},{14,22},{16,24},... | collective-permute-start | bytes 393224 | tf_op jit(solution)/shard_map/ppermute | solution.py:319
  14.3 7.6 %collective-permute-start.4 = (f32[8,16,256]{2,1,0:T(8,128)S(1)}, f32[8,16,256]{2,1,0:T(8,128)S(1)}, u32[]{:S(2)}, u32[]{:S(2)}) collective-permute-start(f32[8,16,256]{2,1,0:T(8,128)S(1)} %get-tuple-element.39), channel_id=1, source_target_pairs={{0,25},{2,27},{4,29},{6,31},{8,0},{10,2},{12,4},{14,6},{16,8},{18,... | collective-permute-start | bytes 393224 | tf_op jit(solution)/shard_map/ppermute | solution.py:320
  23.6 19.6 %all-to-all-start = ((f32[16,2,32,128]{3,2,1,0:T(8,128)}), f32[16,2,32,128]{3,2,1,0:T(8,128)S(1)}, u32[]{:S(2)}, u32[]{:S(2)}) async-start(f32[16,2,32,128]{3,2,1,0:T(8,128)} %get-tuple-element.49), calls=%async_computation | async-start | bytes 1048576 | tf_op jit(solution)/shard_map/all_to_all | solution.py:378
  29.9 9.2 %copy-start.1 = (f32[2,5,16]{2,0,1:T(2,128)S(1)}, f32[2,5,16]{2,0,1:T(2,128)}, u32[]{:S(2)}) copy-start(f32[2,5,16]{2,0,1:T(2,128)} %param.8) | copy-start | bytes 1924
  29.9 7.1 %collective-permute-start.5 = (f32[8,8,256]{2,1,0:T(8,128)S(1)}, f32[8,8,256]{2,1,0:T(8,128)S(1)}, u32[]{:S(2)}, u32[]{:S(2)}) collective-permute-start(f32[8,8,256]{2,1,0:T(8,128)S(1)} %get-tuple-element.43), channel_id=1, source_target_pairs={{0,2},{2,0},{4,6},{6,4},{8,10},{10,8},{12,14},{14,12},{16,18},{18,... | collective-permute-start | bytes 196616 | tf_op jit(solution)/shard_map/ppermute | solution.py:291
  31.9 5.1 %collective-permute-start.6 = (f32[8,8,256]{2,1,0:T(8,128)S(1)}, f32[8,8,256]{2,1,0:T(8,128)S(1)}, u32[]{:S(2)}, u32[]{:S(2)}) collective-permute-start(f32[8,8,256]{2,1,0:T(8,128)S(1)} %get-tuple-element.44), channel_id=1, source_target_pairs={{0,4},{2,6},{4,0},{6,2},{8,12},{10,14},{12,8},{14,10},{16,20},{18,... | collective-permute-start | bytes 196616 | tf_op jit(solution)/shard_map/ppermute | solution.py:291
  33.4 5.8 %collective-permute-start.7 = (f32[8,8,256]{2,1,0:T(8,128)S(1)}, f32[8,8,256]{2,1,0:T(8,128)S(1)}, u32[]{:S(2)}, u32[]{:S(2)}) collective-permute-start(f32[8,8,256]{2,1,0:T(8,128)S(1)} %get-tuple-element.45), channel_id=1, source_target_pairs={{0,6},{2,4},{4,2},{6,0},{8,14},{10,12},{12,10},{14,8},{16,22},{18,... | collective-permute-start | bytes 196616 | tf_op jit(solution)/shard_map/ppermute | solution.py:291

commit v7 on v6

--- a/solution.py
+++ b/solution.py
@@ -110,33 +110,37 @@
         result[half, :, at] = block[:, :, half * LANES : (half + 1) * LANES]
 
 
-def pack(result, band_rows, bands, copies):
+def pack(result, turned, band_rows, bands, copies):
     halves, channels, count, _ = result.shape
     part = channels // 2
     total = bands.shape[0]
+    for half in range(halves):
+        for i in range(channels):
+            turned[half, i] = pltpu.roll(result[half, i], i % part * CAP, 1)
     lane = lax.broadcasted_iota(jnp.int32, (count, LANES), 1)
     start = jnp.int32(0)
     for b in range(total):
         half = start // LANES
         offset = start - half * LANES
         beyond = lax.rem(half + 1, halves)
+        place = jnp.bitwise_and(lane + (LANES - offset), LANES - 1)
+        over = jnp.bitwise_and(place, CAP - 1) >= LANES - offset
         for v in range(2):
-            packed = None
-            for l in range(part):
-                i = v * part + l
-                window = jnp.where(lane >= offset, result[half, i], result[beyond, i])
-                shift = lax.rem(LANES + l * CAP - offset, LANES)
-                turned = pltpu.roll(window, shift, 1)
-                packed = turned if l == 0 else jnp.where(lane >= l * CAP, turned, packed)
-            bands[b, v] = packed
+            here, there = turned[half, v * part], turned[beyond, v * part]
+            for l in range(1, part):
+                chosen = place >= l * CAP
+                here = jnp.where(chosen, turned[half, v * part + l], here)
+                there = jnp.where(chosen, turned[beyond, v * part + l], there)
+            together = jnp.where(over, there, here)
+            bands[b, v] = pltpu.roll(together, lax.rem(LANES - offset, LANES), 1)
         start = start + band_rows[b]
-        if (b + 1) * len(copies) % total == 0:
+        if copies and (b + 1) * len(copies) % total == 0:
             copies[(b + 1) * len(copies) // total - 1].start()
 
 
 def inner_kernel(groups, band_rows, *refs):
     pieces, field, along_x, along_y, down_y = refs[:groups], *refs[groups : groups + 4]
-    sides, result, bands, ready, sems = refs[groups + 4 :]
+    sides, result, bands, ready, turned, sems = refs[groups + 4 :]
     width = pieces[0].shape[0]
     me = member(groups)
     for k, piece in enumerate(pieces):
@@ -156,17 +160,31 @@
     for s in range(1, groups - 1):
         turn(field[pl.ds(s * width, width)], result, pl.ds((s - 1) * width, width))
     copy = pltpu.make_async_copy(ready, bands.at[:, :, pl.ds(0, span - 2 * width)], sems.at[0])
-    pack(result, band_rows, ready, [copy])
+    pack(result, turned, band_rows, ready, [copy])
     copy.wait()
 
 
 def end_kernel(groups, side, rows_far, halo, *refs):
-    inner, sides, _, bands, result = refs[:4], *refs[4:8]
-    end, ready, band_rows, sems = refs[8:12], *refs[12:]
+    inner, sides, refs = refs[:4], refs[4], refs[5:]
+    if side:
+        other, _, bands, result, *end, ready, turned, band_rows, sems = refs
+    else:
+        ready, result, *end, turned, band_rows, sems = refs
     rows_copy = pltpu.make_async_copy(rows_far, band_rows, sems.at[groups])
     rows_copy.start()
     width = halo.shape[0]
     span = groups * width
+    copies = []
+    if side:
+        other_copy = pltpu.make_async_copy(
+            other, bands.at[:, :, pl.ds(span - 2 * width, width)], sems.at[groups + 1]
+        )
+        other_copy.start()
+        each = bands.shape[0] // groups
+        for i in range(groups):
+            near = pl.ds(i * each, each)
+            target = bands.at[near, :, pl.ds(span - width, width)]
+            copies.append(pltpu.make_async_copy(ready.at[near], target, sems.at[i]))
     spread_out(halo, pl.ds(side * width, width), *end)
     for here, array in zip(end, inner):
         here[pl.ds((1 - side) * width, width)] = array[pl.ds(side * (span - width), width)]
@@ -175,17 +193,11 @@
         faces = (sides[1, step], None) if side else (None, sides[0, step])
         advance([(*end, first, first + width, *faces)])
     turn(end[0][pl.ds((1 - side) * width, width)], result, pl.ds(0, width))
-
-    copies = []
-    each = bands.shape[0] // groups
-    for i in range(groups):
-        near = pl.ds(i * each, each)
-        target = bands.at[near, :, pl.ds(span - (2 - side) * width, width)]
-        copies.append(pltpu.make_async_copy(ready.at[near], target, sems.at[i]))
     rows_copy.wait()
-    pack(result, band_rows, ready, copies)
-    for copy in copies:
-        copy.wait()
+    pack(result, turned, band_rows, ready, copies)
+    if side:
+        for copy in copies + [other_copy]:
+            copy.wait()
 
 
 def strips_kernel(groups, low, inner, high, *refs):
@@ -334,6 +346,7 @@
         out_specs=[VMEM] * 6 + [HBM],
         scratch_shapes=[
             pltpu.VMEM((count, variables, inside, LANES), f32),
+            pltpu.VMEM((halves, both, inside, LANES), f32),
             pltpu.SemaphoreType.DMA((1,)),
         ],
         compiler_params=ROOM,
@@ -344,28 +357,33 @@
     )(band_rows, *mine)
     *arrays, inner_result, bands = inner
 
-    def finished(side, halo, bands):
-        return pl.pallas_call(
-            functools.partial(end_kernel, groups, side),
-            out_shape=[
-                struct(count, variables, span, LANES),
-                struct(halves, both, width, LANES),
-            ],
-            in_specs=[HBM] + [VMEM] * 6 + [HBM],
-            out_specs=[HBM, VMEM],
-            input_output_aliases={7: 0},
-            scratch_shapes=[pltpu.VMEM((2 * width, both, rows), f32)] * 4
-            + [
-                pltpu.VMEM((count, variables, width, LANES), f32),
-                pltpu.SMEM(band_rows.shape, band_rows.dtype),
-                pltpu.SemaphoreType.DMA((groups + 1,)),
-            ],
-            compiler_params=ROOM,
-            name="high_end" if side else "low_end",
-        )(band_rows, halo, *arrays, bands)
-
-    bands, low_result = finished(0, low, bands)
-    bands, high_result = finished(1, high, bands)
+    cut = struct(count, variables, width, LANES)
+    turned = struct(halves, both, width, LANES)
+    scratch = [pltpu.VMEM((2 * width, both, rows), f32)] * 4
+    small = [
+        pltpu.VMEM(turned.shape, f32),
+        pltpu.SMEM(band_rows.shape, band_rows.dtype),
+        pltpu.SemaphoreType.DMA((groups + 2,)),
+    ]
+    low_bands, low_result = pl.pallas_call(
+        functools.partial(end_kernel, groups, 0),
+        out_shape=[cut, turned],
+        in_specs=[HBM] + [VMEM] * 6,
+        out_specs=[VMEM] * 2,
+        scratch_shapes=scratch + small,
+        compiler_params=ROOM,
+        name="low_end",
+    )(band_rows, low, *arrays)
+    bands, high_result = pl.pallas_call(
+        functools.partial(end_kernel, groups, 1),
+        out_shape=[struct(count, variables, span, LANES), turned],
+        in_specs=[HBM] + [VMEM] * 7 + [HBM],
+        out_specs=[HBM, VMEM],
+        input_output_aliases={8: 0},
+        scratch_shapes=scratch + [pltpu.VMEM(cut.shape, f32)] + small,
+        compiler_params=ROOM,
+        name="high_end",
+    )(band_rows, high, *arrays, low_bands, bands)
     strips = pl.pallas_call(
         functools.partial(strips_kernel, groups),
         out_shape=[struct(both, width, rows)] * groups,

time: 44.6 us -> 44.5 us (level)
  waiting for transfers between devices: 15.6 us -> 16.9 us
  Pallas kernels: 10.1 us -> 9.21 us
  starting transfers between devices: 17.9 us -> 17.4 us
    pallas_call x2, Pallas kernels: 3.41 us -> 2.65 us  [the longest x1 1.62 us: shards(): pl.pallas_call(functools.partial(end_kernel, groups, 1), out_shape=[struc...]
    ppermute x1, waiting for transfers between devices: 0.01 us -> 0.54 us  [shards(): high = lax.ppermute(first, axes, shifted(-groups))]
    all_to_all x1, starting transfers between devices: 6.22 us -> 5.69 us  [shards(): lax.all_to_all(bands, 'band', split_axis=0, concat_axis=0, tiled=True)]
    ppermute x6, waiting for transfers between devices: 11.9 us -> 12.3 us  [exchanged(): lax.ppermute(pieces[k], 'band', [(i, i ^ k) for i in range(count)])]
  transfers between devices with their start and end apart: 9 -> 9, of which waited for: 6 -> 8; matrix products, arithmetic and copies ran while one was open for 0% -> 0% of each run, Pallas kernels for 14% -> 12%
where the time goes in v7:
time: 44.5 us; the launch traced here: 44.2 us
  starting transfers between devices  17.4 us (39%)
  waiting for transfers between devices  16.9 us (38%)
  Pallas kernels  9.21 us (21%)
  between operations  0.71 us (2%)
    ppermute x6, waiting for transfers between devices, exchanged(): lax.ppermute(pieces[k], 'band', [(i, i ^ k) for i in range(count)])  12.3 us
    ppermute x6, starting transfers between devices, exchanged(): lax.ppermute(pieces[k], 'band', [(i, i ^ k) for i in range(count)])  8.1 us
    all_to_all x1, starting transfers between devices, shards(): lax.all_to_all(bands, 'band', split_axis=0, concat_axis=0, tiled=True)  5.69 us
    all_to_all x1, waiting for transfers between devices, shards(): lax.all_to_all(bands, 'band', split_axis=0, concat_axis=0, tiled=True)  2.91 us
    pallas_call x1, Pallas kernels, shards(): pl.pallas_call(functools.partial(inner_kernel, groups), out_shape=[struct...  2.85 us
    ppermute x1, starting transfers between devices, shards(): high = lax.ppermute(first, axes, shifted(-groups))  1.97 us
    ppermute x1, starting transfers between devices, shards(): low = lax.ppermute(last, axes, shifted(groups))  1.64 us
    pallas_call x1, Pallas kernels, shards(): pl.pallas_call(functools.partial(end_kernel, groups, 1), out_shape=[struc...  1.62 us
  transfers between devices with their start and end apart: 9, of which 8 were waited for; matrix products, arithmetic and copies ran while one was open for 0% of the time, Pallas kernels for 12%

profile of v7, /device:TPU:0, one launch (start us, length us, event | category | flops | bytes accessed | tf_op | source)
XLA Modules:
  0.0 44.2 jit_solution(12350777563144831490)
XLA Ops:
  0.6 1.2 %regroup.1 = (f32[8,16,256]{2,1,0:T(8,128)S(1)}, f32[8,16,256]{2,1,0:T(8,128)S(1)}, f32[8,16,256]{2,1,0:T(8,128)S(1)}, f32[8,16,256]{2,1,0:T(8,128)S(1)}) custom-call(f32[2,16,8,256]{3,2,1,0:T(8,128)} %background.1, f32[16,8,256]{2,1,0:T(8,128)} %scale_x.1, f32[16,8,256]{2,1,0:T(8,128)} %scale_y.1), custom_call_target="tpu_custom_call" | custom-call | tf_op jit(solution)/shard_map/regroup/pallas_call | solution.py:289
  1.8 3.0 %collective-permute-start = (f32[8,16,256]{2,1,0:T(8,128)S(1)}, f32[8,16,256]{2,1,0:T(8,128)S(1)}, u32[]{:S(2)}, u32[]{:S(2)}) collective-permute-start(f32[8,16,256]{2,1,0:T(8,128)S(1)} %get-tuple-element.27), channel_id=1, source_target_pairs={{0,2},{2,0},{4,6},{6,4},{8,10},{10,8},{12,14},{14,12},{16,18},{18,... | collective-permute-start | bytes 393224 | tf_op jit(solution)/shard_map/ppermute | solution.py:303
  4.8 1.5 %collective-permute-start.1 = (f32[8,16,256]{2,1,0:T(8,128)S(1)}, f32[8,16,256]{2,1,0:T(8,128)S(1)}, u32[]{:S(2)}, u32[]{:S(2)}) collective-permute-start(f32[8,16,256]{2,1,0:T(8,128)S(1)} %get-tuple-element.28), channel_id=1, source_target_pairs={{0,4},{2,6},{4,0},{6,2},{8,12},{10,14},{12,8},{14,10},{16,20},{18,... | collective-permute-start | bytes 393224 | tf_op jit(solution)/shard_map/ppermute | solution.py:303
  6.3 0.0 collective-permute-start.2
  6.4 2.4 %collective-permute-done.refs_1_ = f32[8,16,256]{2,1,0:T(8,128)S(1)} collective-permute-done((f32[8,16,256]{2,1,0:T(8,128)S(1)}, f32[8,16,256]{2,1,0:T(8,128)S(1)}, u32[]{:S(2)}, u32[]{:S(2)}) %collective-permute-start) | collective-permute-done | bytes 131104 | tf_op jit(solution)/shard_map/ppermute | solution.py:303
  8.7 3.9 %collective-permute-done.1.refs_2_ = f32[8,16,256]{2,1,0:T(8,128)S(1)} collective-permute-done((f32[8,16,256]{2,1,0:T(8,128)S(1)}, f32[8,16,256]{2,1,0:T(8,128)S(1)}, u32[]{:S(2)}, u32[]{:S(2)}) %collective-permute-start.1) | collective-permute-done | bytes 131104 | tf_op jit(solution)/shard_map/ppermute | solution.py:303
  12.6 0.0 collective-permute-done.2.refs_3_
  12.7 0.0 copy-start
  12.7 1.6 %collective-permute-start.3 = (f32[8,16,256]{2,1,0:T(8,128)S(1)}, f32[8,16,256]{2,1,0:T(8,128)S(1)}, u32[]{:S(2)}, u32[]{:S(2)}) collective-permute-start(f32[8,16,256]{2,1,0:T(8,128)S(1)} %get-tuple-element.30), channel_id=1, source_target_pairs={{0,8},{2,10},{4,12},{6,14},{8,16},{10,18},{12,20},{14,22},{16,24},... | collective-permute-start | bytes 393224 | tf_op jit(solution)/shard_map/ppermute | solution.py:331
  14.3 2.0 %collective-permute-start.4 = (f32[8,16,256]{2,1,0:T(8,128)S(1)}, f32[8,16,256]{2,1,0:T(8,128)S(1)}, u32[]{:S(2)}, u32[]{:S(2)}) collective-permute-start(f32[8,16,256]{2,1,0:T(8,128)S(1)} %get-tuple-element.38), channel_id=1, source_target_pairs={{0,25},{2,27},{4,29},{6,31},{8,0},{10,2},{12,4},{14,6},{16,8},{18,... | collective-permute-start | bytes 393224 | tf_op jit(solution)/shard_map/ppermute | solution.py:332
  16.3 0.0 copy-done
  16.3 2.9 %inner.1 = (f32[32,8,256]{2,1,0:T(8,128)S(1)}, f32[32,8,256]{2,1,0:T(8,128)S(1)}, f32[32,8,256]{2,1,0:T(8,128)S(1)}, f32[32,8,256]{2,1,0:T(8,128)S(1)}, f32[2,8,...) custom-call(s32[16]{0:T(128)S(1)} %copy-done, ...), custom_call_target="tpu_custom_call" | custom-call | flops 10485760 | bytes 1048576 | tf_op jit(solution)/shard_map/inner/pallas_call | solution.py:337
  19.1 1.1 %collective-permute-done.3.halo = f32[8,16,256]{2,1,0:T(8,128)S(1)} collective-permute-done((f32[8,16,256]{2,1,0:T(8,128)S(1)}, f32[8,16,256]{2,1,0:T(8,128)S(1)}, u32[]{:S(2)}, u32[]{:S(2)}) %collective-permute-start.3) | collective-permute-done | bytes 131104 | tf_op jit(solution)/shard_map/ppermute | solution.py:331
  20.2 1.0 %low_end.1 = (f32[16,2,8,128]{3,2,1,0:T(8,128)S(1)}, f32[2,8,8,128]{3,2,1,0:T(8,128)S(1)}) custom-call(s32[16]{0:T(128)S(1)} %copy-done, f32[8,16,256]{2,1,0:T(8,128)S(1)} %collective-permute-done.3.halo, f32[32,8,256]{2,1,0:T(8,128)S(1)} %get-tuple-element.31.refs_0_, f32[32,8,256]{2,1,0:T(8,128)S(1)} %get-tuple-element.32.refs_1_, ...), custom_call_target="tpu_custom_call" | custom-call | tf_op jit(solution)/shard_map/low_end/pallas_call | solution.py:368
  21.2 0.5 %collective-permute-done.4.halo = f32[8,16,256]{2,1,0:T(8,128)S(1)} collective-permute-done((f32[8,16,256]{2,1,0:T(8,128)S(1)}, f32[8,16,256]{2,1,0:T(8,128)S(1)}, u32[]{:S(2)}, u32[]{:S(2)}) %collective-permute-start.4) | collective-permute-done | bytes 131104 | tf_op jit(solution)/shard_map/ppermute | solution.py:332
  21.8 1.6 %high_end.1 = (f32[16,2,32,128]{3,2,1,0:T(8,128)}, f32[2,8,8,128]{3,2,1,0:T(8,128)S(1)}) custom-call(s32[16]{0:T(128)S(1)} %copy-done, f32[8,16,256]{2,1,0:T(8,128)S(1)} %collective-permute-done.4.halo, f32[32,8,256]{2,1,0:T(8,128)S(1)} %get-tuple-element.31.refs_0_, f32[32,8,256]{2,1,0:T(8,128)S(1)} %get-tuple-element.32.refs_1_, ...), custom_call_target="tpu_custom_call", output_to_operand_aliasing={{0}: (8, {})} | custom-call | tf_op jit(solution)/shard_map/high_end/pallas_call | solution.py:377
  23.4 5.7 %all-to-all-start = ((f32[16,2,32,128]{3,2,1,0:T(8,128)}), f32[16,2,32,128]{3,2,1,0:T(8,128)S(1)}, u32[]{:S(2)}, u32[]{:S(2)}) async-start(f32[16,2,32,128]{3,2,1,0:T(8,128)} %get-tuple-element.49), calls=%async_computation | async-start | bytes 1048576 | tf_op jit(solution)/shard_map/all_to_all | solution.py:396
  29.1 0.1 strips.1
  29.2 0.0 copy-start.1
  29.2 2.0 %collective-permute-start.5 = (f32[8,8,256]{2,1,0:T(8,128)S(1)}, f32[8,8,256]{2,1,0:T(8,128)S(1)}, u32[]{:S(2)}, u32[]{:S(2)}) collective-permute-start(f32[8,8,256]{2,1,0:T(8,128)S(1)} %get-tuple-element.43), channel_id=1, source_target_pairs={{0,2},{2,0},{4,6},{6,4},{8,10},{10,8},{12,14},{14,12},{16,18},{18,... | collective-permute-start | bytes 196616 | tf_op jit(solution)/shard_map/ppermute | solution.py:303
  31.2 1.5 %collective-permute-start.6 = (f32[8,8,256]{2,1,0:T(8,128)S(1)}, f32[8,8,256]{2,1,0:T(8,128)S(1)}, u32[]{:S(2)}, u32[]{:S(2)}) collective-permute-start(f32[8,8,256]{2,1,0:T(8,128)S(1)} %get-tuple-element.44), channel_id=1, source_target_pairs={{0,4},{2,6},{4,0},{6,2},{8,12},{10,14},{12,8},{14,10},{16,20},{18,... | collective-permute-start | bytes 196616 | tf_op jit(solution)/shard_map/ppermute | solution.py:303
  32.6 0.1 collective-permute-start.7
  32.7 3.6 %collective-permute-done.5.refs_1_ = f32[8,8,256]{2,1,0:T(8,128)S(1)} collective-permute-done((f32[8,8,256]{2,1,0:T(8,128)S(1)}, f32[8,8,256]{2,1,0:T(8,128)S(1)}, u32[]{:S(2)}, u32[]{:S(2)}) %collective-permute-start.5) | collective-permute-done | bytes 65568 | tf_op jit(solution)/shard_map/ppermute | solution.py:303
  36.3 0.6 %collective-permute-done.6.refs_2_ = f32[8,8,256]{2,1,0:T(8,128)S(1)} collective-permute-done((f32[8,8,256]{2,1,0:T(8,128)S(1)}, f32[8,8,256]{2,1,0:T(8,128)S(1)}, u32[]{:S(2)}, u32[]{:S(2)}) %collective-permute-start.6) | collective-permute-done | bytes 65568 | tf_op jit(solution)/shard_map/ppermute | solution.py:303
  36.9 1.9 %collective-permute-done.7.refs_3_ = f32[8,8,256]{2,1,0:T(8,128)S(1)} collective-permute-done((f32[8,8,256]{2,1,0:T(8,128)S(1)}, f32[8,8,256]{2,1,0:T(8,128)S(1)}, u32[]{:S(2)}, u32[]{:S(2)}) %collective-permute-start.7) | collective-permute-done | bytes 65568 | tf_op jit(solution)/shard_map/ppermute | solution.py:303
  38.9 0.0 copy-done.1
  38.9 1.5 %increment.1 = (f32[2,16,8,256]{3,2,1,0:T(8,128)}, f32[5,2,16,1,128]{4,3,2,1,0:T(1,128)S(1)}, s32[32,128]{1,0:T(8,128)S(1)}) custom-call(s32[16]{0:T(128)S(1)} %copy-done, f32[5,2,16]{2,1,0:T(2,128)S(1)} %bitcast.1, f32[8,8,256]{2,1,0:T(8,128)S(1)} %get-tuple-element.42.refs_0_, f32[8,8,256]{2,1,0:T(8,128)S(1)} %collective-permute-done.5.refs_1_, ...), custom_call_target="tpu_custom_call" | custom-call | tf_op jit(solution)/shard_map/increment/pallas_call | solution.py:398
  40.3 2.9 %all-to-all-done.arrived = f32[16,2,32,128]{3,2,1,0:T(8,128)S(1)} async-done(((f32[16,2,32,128]{3,2,1,0:T(8,128)}), f32[16,2,32,128]{3,2,1,0:T(8,128)S(1)}, u32[]{:S(2)}, u32[]{:S(2)}) %all-to-all-start) | async-done | bytes 524320 | tf_op jit(solution)/shard_map/all_to_all | solution.py:396
  43.2 1.0 %bands.1 = f32[2,16,32,128]{3,2,1,0:T(8,128)} custom-call(f32[5,2,16,1,128]{4,3,2,1,0:T(1,128)S(1)} %get-tuple-element.47.taps, s32[32,128]{1,0:T(8,128)S(1)} %get-tuple-element.48.keep, f32[16,2,32,128]{3,2,1,0:T(8,128)S(1)} %all-to-all-done.arrived), custom_call_target="tpu_custom_call" | custom-call | tf_op jit(solution)/shard_map/bands/pallas_call | solution.py:411
  (1 shorter events, 0.0 us)
Async XLA Ops:
  1.8 6.9 %collective-permute-start = (f32[8,16,256]{2,1,0:T(8,128)S(1)}, f32[8,16,256]{2,1,0:T(8,128)S(1)}, u32[]{:S(2)}, u32[]{:S(2)}) collective-permute-start(f32[8,16,256]{2,1,0:T(8,128)S(1)} %get-tuple-element.27), channel_id=1, source_target_pairs={{0,2},{2,0},{4,6},{6,4},{8,10},{10,8},{12,14},{14,12},{16,18},{18,... | collective-permute-start | bytes 393224 | tf_op jit(solution)/shard_map/ppermute | solution.py:303
  4.8 7.8 %collective-permute-start.1 = (f32[8,16,256]{2,1,0:T(8,128)S(1)}, f32[8,16,256]{2,1,0:T(8,128)S(1)}, u32[]{:S(2)}, u32[]{:S(2)}) collective-permute-start(f32[8,16,256]{2,1,0:T(8,128)S(1)} %get-tuple-element.28), channel_id=1, source_target_pairs={{0,4},{2,6},{4,0},{6,2},{8,12},{10,14},{12,8},{14,10},{16,20},{18,... | collective-permute-start | bytes 393224 | tf_op jit(solution)/shard_map/ppermute | solution.py:303
  6.3 6.3 %collective-permute-start.2 = (f32[8,16,256]{2,1,0:T(8,128)S(1)}, f32[8,16,256]{2,1,0:T(8,128)S(1)}, u32[]{:S(2)}, u32[]{:S(2)}) collective-permute-start(f32[8,16,256]{2,1,0:T(8,128)S(1)} %get-tuple-element.29), channel_id=1, source_target_pairs={{0,6},{2,4},{4,2},{6,0},{8,14},{10,12},{12,10},{14,8},{16,22},{18,... | collective-permute-start | bytes 393224 | tf_op jit(solution)/shard_map/ppermute | solution.py:303
  12.7 3.6 %copy-start = (s32[16]{0:T(128)S(1)}, s32[16]{0:T(128)}, u32[]{:S(2)}) copy-start(s32[16]{0:T(128)} %band_rows.3) | copy-start | bytes 196
  12.7 7.5 %collective-permute-start.3 = (f32[8,16,256]{2,1,0:T(8,128)S(1)}, f32[8,16,256]{2,1,0:T(8,128)S(1)}, u32[]{:S(2)}, u32[]{:S(2)}) collective-permute-start(f32[8,16,256]{2,1,0:T(8,128)S(1)} %get-tuple-element.30), channel_id=1, source_target_pairs={{0,8},{2,10},{4,12},{6,14},{8,16},{10,18},{12,20},{14,22},{16,24},... | collective-permute-start | bytes 393224 | tf_op jit(solution)/shard_map/ppermute | solution.py:331
  14.3 7.5 %collective-permute-start.4 = (f32[8,16,256]{2,1,0:T(8,128)S(1)}, f32[8,16,256]{2,1,0:T(8,128)S(1)}, u32[]{:S(2)}, u32[]{:S(2)}) collective-permute-start(f32[8,16,256]{2,1,0:T(8,128)S(1)} %get-tuple-element.38), channel_id=1, source_target_pairs={{0,25},{2,27},{4,29},{6,31},{8,0},{10,2},{12,4},{14,6},{16,8},{18,... | collective-permute-start | bytes 393224 | tf_op jit(solution)/shard_map/ppermute | solution.py:332
  23.4 19.8 %all-to-all-start = ((f32[16,2,32,128]{3,2,1,0:T(8,128)}), f32[16,2,32,128]{3,2,1,0:T(8,128)S(1)}, u32[]{:S(2)}, u32[]{:S(2)}) async-start(f32[16,2,32,128]{3,2,1,0:T(8,128)} %get-tuple-element.49), calls=%async_computation | async-start | bytes 1048576 | tf_op jit(solution)/shard_map/all_to_all | solution.py:396
  29.2 9.7 %copy-start.1 = (f32[2,5,16]{2,0,1:T(2,128)S(1)}, f32[2,5,16]{2,0,1:T(2,128)}, u32[]{:S(2)}) copy-start(f32[2,5,16]{2,0,1:T(2,128)} %param.8) | copy-start | bytes 1924
  29.2 7.1 %collective-permute-start.5 = (f32[8,8,256]{2,1,0:T(8,128)S(1)}, f32[8,8,256]{2,1,0:T(8,128)S(1)}, u32[]{:S(2)}, u32[]{:S(2)}) collective-permute-start(f32[8,8,256]{2,1,0:T(8,128)S(1)} %get-tuple-element.43), channel_id=1, source_target_pairs={{0,2},{2,0},{4,6},{6,4},{8,10},{10,8},{12,14},{14,12},{16,18},{18,... | collective-permute-start | bytes 196616 | tf_op jit(solution)/shard_map/ppermute | solution.py:303
  31.2 5.7 %collective-permute-start.6 = (f32[8,8,256]{2,1,0:T(8,128)S(1)}, f32[8,8,256]{2,1,0:T(8,128)S(1)}, u32[]{:S(2)}, u32[]{:S(2)}) collective-permute-start(f32[8,8,256]{2,1,0:T(8,128)S(1)} %get-tuple-element.44), channel_id=1, source_target_pairs={{0,4},{2,6},{4,0},{6,2},{8,12},{10,14},{12,8},{14,10},{16,20},{18,... | collective-permute-start | bytes 196616 | tf_op jit(solution)/shard_map/ppermute | solution.py:303
  32.6 6.2 %collective-permute-start.7 = (f32[8,8,256]{2,1,0:T(8,128)S(1)}, f32[8,8,256]{2,1,0:T(8,128)S(1)}, u32[]{:S(2)}, u32[]{:S(2)}) collective-permute-start(f32[8,8,256]{2,1,0:T(8,128)S(1)} %get-tuple-element.45), channel_id=1, source_target_pairs={{0,6},{2,4},{4,2},{6,0},{8,14},{10,12},{12,10},{14,8},{16,22},{18,... | collective-permute-start | bytes 196616 | tf_op jit(solution)/shard_map/ppermute | solution.py:303

commit v8 on v6

--- a/solution.py
+++ b/solution.py
@@ -110,25 +110,29 @@
         result[half, :, at] = block[:, :, half * LANES : (half + 1) * LANES]
 
 
-def pack(result, band_rows, bands, copies):
+def pack(result, turned, band_rows, bands, copies):
     halves, channels, count, _ = result.shape
     part = channels // 2
     total = bands.shape[0]
+    for half in range(halves):
+        for i in range(channels):
+            turned[half, i] = pltpu.roll(result[half, i], i % part * CAP, 1)
     lane = lax.broadcasted_iota(jnp.int32, (count, LANES), 1)
     start = jnp.int32(0)
     for b in range(total):
         half = start // LANES
         offset = start - half * LANES
         beyond = lax.rem(half + 1, halves)
+        place = jnp.bitwise_and(lane + (LANES - offset), LANES - 1)
+        over = jnp.bitwise_and(place, CAP - 1) >= LANES - offset
         for v in range(2):
-            packed = None
-            for l in range(part):
-                i = v * part + l
-                window = jnp.where(lane >= offset, result[half, i], result[beyond, i])
-                shift = lax.rem(LANES + l * CAP - offset, LANES)
-                turned = pltpu.roll(window, shift, 1)
-                packed = turned if l == 0 else jnp.where(lane >= l * CAP, turned, packed)
-            bands[b, v] = packed
+            here, there = turned[half, v * part], turned[beyond, v * part]
+            for l in range(1, part):
+                chosen = place >= l * CAP
+                here = jnp.where(chosen, turned[half, v * part + l], here)
+                there = jnp.where(chosen, turned[beyond, v * part + l], there)
+            together = jnp.where(over, there, here)
+            bands[b, v] = pltpu.roll(together, lax.rem(LANES - offset, LANES), 1)
         start = start + band_rows[b]
         if (b + 1) * len(copies) % total == 0:
             copies[(b + 1) * len(copies) // total - 1].start()
@@ -136,7 +140,7 @@
 
 def inner_kernel(groups, band_rows, *refs):
     pieces, field, along_x, along_y, down_y = refs[:groups], *refs[groups : groups + 4]
-    sides, result, bands, ready, sems = refs[groups + 4 :]
+    sides, result, bands, ready, turned, sems = refs[groups + 4 :]
     width = pieces[0].shape[0]
     me = member(groups)
     for k, piece in enumerate(pieces):
@@ -156,13 +160,13 @@
     for s in range(1, groups - 1):
         turn(field[pl.ds(s * width, width)], result, pl.ds((s - 1) * width, width))
     copy = pltpu.make_async_copy(ready, bands.at[:, :, pl.ds(0, span - 2 * width)], sems.at[0])
-    pack(result, band_rows, ready, [copy])
+    pack(result, turned, band_rows, ready, [copy])
     copy.wait()
 
 
 def end_kernel(groups, side, rows_far, halo, *refs):
     inner, sides, _, bands, result = refs[:4], *refs[4:8]
-    end, ready, band_rows, sems = refs[8:12], *refs[12:]
+    end, ready, turned, band_rows, sems = refs[8:12], *refs[12:]
     rows_copy = pltpu.make_async_copy(rows_far, band_rows, sems.at[groups])
     rows_copy.start()
     width = halo.shape[0]
@@ -183,7 +187,7 @@
         target = bands.at[near, :, pl.ds(span - (2 - side) * width, width)]
         copies.append(pltpu.make_async_copy(ready.at[near], target, sems.at[i]))
     rows_copy.wait()
-    pack(result, band_rows, ready, copies)
+    pack(result, turned, band_rows, ready, copies)
     for copy in copies:
         copy.wait()
 
@@ -334,6 +338,7 @@
         out_specs=[VMEM] * 6 + [HBM],
         scratch_shapes=[
             pltpu.VMEM((count, variables, inside, LANES), f32),
+            pltpu.VMEM((halves, both, inside, LANES), f32),
             pltpu.SemaphoreType.DMA((1,)),
         ],
         compiler_params=ROOM,
@@ -357,6 +362,7 @@
             scratch_shapes=[pltpu.VMEM((2 * width, both, rows), f32)] * 4
             + [
                 pltpu.VMEM((count, variables, width, LANES), f32),
+                pltpu.VMEM((halves, both, width, LANES), f32),
                 pltpu.SMEM(band_rows.shape, band_rows.dtype),
                 pltpu.SemaphoreType.DMA((groups + 1,)),
             ],

time: 44.6 us -> 44.5 us (level)
  no operation moved by 1% of the time
where the time goes in v8:
time: 44.5 us; the launch traced here: 44.2 us
  starting transfers between devices  17.9 us (40%)
  waiting for transfers between devices  15.7 us (35%)
  Pallas kernels  9.81 us (22%)
  between operations  0.72 us (2%)
    ppermute x6, waiting for transfers between devices, exchanged(): lax.ppermute(pieces[k], 'band', [(i, i ^ k) for i in range(count)])  12 us
    ppermute x6, starting transfers between devices, exchanged(): lax.ppermute(pieces[k], 'band', [(i, i ^ k) for i in range(count)])  8.1 us
    all_to_all x1, starting transfers between devices, shards(): lax.all_to_all(bands, 'band', split_axis=0, concat_axis=0, tiled=True)  6.22 us
    pallas_call x2, Pallas kernels, finished(): pl.pallas_call(functools.partial(end_kernel, groups, side), out_shape=[st...  3.25 us
    pallas_call x1, Pallas kernels, shards(): pl.pallas_call(functools.partial(inner_kernel, groups), out_shape=[struct...  2.85 us
    all_to_all x1, waiting for transfers between devices, shards(): lax.all_to_all(bands, 'band', split_axis=0, concat_axis=0, tiled=True)  2.7 us
    ppermute x1, starting transfers between devices, shards(): high = lax.ppermute(first, axes, shifted(-groups))  1.97 us
    ppermute x1, starting transfers between devices, shards(): low = lax.ppermute(last, axes, shifted(groups))  1.64 us
  transfers between devices with their start and end apart: 9, of which 6 were waited for; matrix products, arithmetic and copies ran while one was open for 0% of the time, Pallas kernels for 14%

profile of v8, /device:TPU:0, one launch (start us, length us, event | category | flops | bytes accessed | tf_op | source)
XLA Modules:
  0.0 44.2 jit_solution(4387995857787133855)
XLA Ops:
  0.6 1.2 %regroup.1 = (f32[8,16,256]{2,1,0:T(8,128)S(1)}, f32[8,16,256]{2,1,0:T(8,128)S(1)}, f32[8,16,256]{2,1,0:T(8,128)S(1)}, f32[8,16,256]{2,1,0:T(8,128)S(1)}) custom-call(f32[2,16,8,256]{3,2,1,0:T(8,128)} %background.1, f32[16,8,256]{2,1,0:T(8,128)} %scale_x.1, f32[16,8,256]{2,1,0:T(8,128)} %scale_y.1), custom_call_target="tpu_custom_call" | custom-call | tf_op jit(solution)/shard_map/regroup/pallas_call | solution.py:281
  1.8 3.0 %collective-permute-start = (f32[8,16,256]{2,1,0:T(8,128)S(1)}, f32[8,16,256]{2,1,0:T(8,128)S(1)}, u32[]{:S(2)}, u32[]{:S(2)}) collective-permute-start(f32[8,16,256]{2,1,0:T(8,128)S(1)} %get-tuple-element.27), channel_id=1, source_target_pairs={{0,2},{2,0},{4,6},{6,4},{8,10},{10,8},{12,14},{14,12},{16,18},{18,... | collective-permute-start | bytes 393224 | tf_op jit(solution)/shard_map/ppermute | solution.py:295
  4.8 1.5 %collective-permute-start.1 = (f32[8,16,256]{2,1,0:T(8,128)S(1)}, f32[8,16,256]{2,1,0:T(8,128)S(1)}, u32[]{:S(2)}, u32[]{:S(2)}) collective-permute-start(f32[8,16,256]{2,1,0:T(8,128)S(1)} %get-tuple-element.28), channel_id=1, source_target_pairs={{0,4},{2,6},{4,0},{6,2},{8,12},{10,14},{12,8},{14,10},{16,20},{18,... | collective-permute-start | bytes 393224 | tf_op jit(solution)/shard_map/ppermute | solution.py:295
  6.3 0.0 collective-permute-start.2
  6.4 2.4 %collective-permute-done.refs_1_ = f32[8,16,256]{2,1,0:T(8,128)S(1)} collective-permute-done((f32[8,16,256]{2,1,0:T(8,128)S(1)}, f32[8,16,256]{2,1,0:T(8,128)S(1)}, u32[]{:S(2)}, u32[]{:S(2)}) %collective-permute-start) | collective-permute-done | bytes 131104 | tf_op jit(solution)/shard_map/ppermute | solution.py:295
  8.7 3.9 %collective-permute-done.1.refs_2_ = f32[8,16,256]{2,1,0:T(8,128)S(1)} collective-permute-done((f32[8,16,256]{2,1,0:T(8,128)S(1)}, f32[8,16,256]{2,1,0:T(8,128)S(1)}, u32[]{:S(2)}, u32[]{:S(2)}) %collective-permute-start.1) | collective-permute-done | bytes 131104 | tf_op jit(solution)/shard_map/ppermute | solution.py:295
  12.6 0.0 collective-permute-done.2.refs_3_
  12.7 0.0 copy-start
  12.7 1.6 %collective-permute-start.3 = (f32[8,16,256]{2,1,0:T(8,128)S(1)}, f32[8,16,256]{2,1,0:T(8,128)S(1)}, u32[]{:S(2)}, u32[]{:S(2)}) collective-permute-start(f32[8,16,256]{2,1,0:T(8,128)S(1)} %get-tuple-element.30), channel_id=1, source_target_pairs={{0,8},{2,10},{4,12},{6,14},{8,16},{10,18},{12,20},{14,22},{16,24},... | collective-permute-start | bytes 393224 | tf_op jit(solution)/shard_map/ppermute | solution.py:323
  14.3 2.0 %collective-permute-start.4 = (f32[8,16,256]{2,1,0:T(8,128)S(1)}, f32[8,16,256]{2,1,0:T(8,128)S(1)}, u32[]{:S(2)}, u32[]{:S(2)}) collective-permute-start(f32[8,16,256]{2,1,0:T(8,128)S(1)} %get-tuple-element.39), channel_id=1, source_target_pairs={{0,25},{2,27},{4,29},{6,31},{8,0},{10,2},{12,4},{14,6},{16,8},{18,... | collective-permute-start | bytes 393224 | tf_op jit(solution)/shard_map/ppermute | solution.py:324
  16.3 0.0 copy-done
  16.3 2.9 %inner.1 = (f32[32,8,256]{2,1,0:T(8,128)S(1)}, f32[32,8,256]{2,1,0:T(8,128)S(1)}, f32[32,8,256]{2,1,0:T(8,128)S(1)}, f32[32,8,256]{2,1,0:T(8,128)S(1)}, f32[2,8,...) custom-call(s32[16]{0:T(128)S(1)} %copy-done, ...), custom_call_target="tpu_custom_call" | custom-call | flops 10485760 | bytes 1048576 | tf_op jit(solution)/shard_map/inner/pallas_call | solution.py:329
  19.1 1.1 %collective-permute-done.3.halo = f32[8,16,256]{2,1,0:T(8,128)S(1)} collective-permute-done((f32[8,16,256]{2,1,0:T(8,128)S(1)}, f32[8,16,256]{2,1,0:T(8,128)S(1)}, u32[]{:S(2)}, u32[]{:S(2)}) %collective-permute-start.3) | collective-permute-done | bytes 131104 | tf_op jit(solution)/shard_map/ppermute | solution.py:323
  20.2 1.6 %low_end.1 = (f32[16,2,32,128]{3,2,1,0:T(8,128)}, f32[2,8,8,128]{3,2,1,0:T(8,128)S(1)}) custom-call(s32[16]{0:T(128)S(1)} %copy-done, f32[8,16,256]{2,1,0:T(8,128)S(1)} %collective-permute-done.3.halo, f32[32,8,256]{2,1,0:T(8,128)S(1)} %get-tuple-element.31.refs_0_, f32[32,8,256]{2,1,0:T(8,128)S(1)} %get-tuple-element.32.refs_1_, ...), custom_call_target="tpu_custom_call", output_to_operand_aliasing={{0}: (7, {})} | custom-call | tf_op jit(solution)/shard_map/low_end/pallas_call | solution.py:353
  21.9 0.0 collective-permute-done.4.halo
  21.9 1.6 %high_end.1 = (f32[16,2,32,128]{3,2,1,0:T(8,128)}, f32[2,8,8,128]{3,2,1,0:T(8,128)S(1)}) custom-call(s32[16]{0:T(128)S(1)} %copy-done, f32[8,16,256]{2,1,0:T(8,128)S(1)} %collective-permute-done.4.halo, f32[32,8,256]{2,1,0:T(8,128)S(1)} %get-tuple-element.31.refs_0_, f32[32,8,256]{2,1,0:T(8,128)S(1)} %get-tuple-element.32.refs_1_, ...), custom_call_target="tpu_custom_call", output_to_operand_aliasing={{0}: (7, {})} | custom-call | tf_op jit(solution)/shard_map/high_end/pallas_call | solution.py:353
  23.5 6.2 %all-to-all-start = ((f32[16,2,32,128]{3,2,1,0:T(8,128)}), f32[16,2,32,128]{3,2,1,0:T(8,128)S(1)}, u32[]{:S(2)}, u32[]{:S(2)}) async-start(f32[16,2,32,128]{3,2,1,0:T(8,128)} %get-tuple-element.49), calls=%async_computation | async-start | bytes 1048576 | tf_op jit(solution)/shard_map/all_to_all | solution.py:384
  29.7 0.1 strips.1
  29.8 0.0 copy-start.1
  29.8 2.0 %collective-permute-start.5 = (f32[8,8,256]{2,1,0:T(8,128)S(1)}, f32[8,8,256]{2,1,0:T(8,128)S(1)}, u32[]{:S(2)}, u32[]{:S(2)}) collective-permute-start(f32[8,8,256]{2,1,0:T(8,128)S(1)} %get-tuple-element.43), channel_id=1, source_target_pairs={{0,2},{2,0},{4,6},{6,4},{8,10},{10,8},{12,14},{14,12},{16,18},{18,... | collective-permute-start | bytes 196616 | tf_op jit(solution)/shard_map/ppermute | solution.py:295
  31.8 1.5 %collective-permute-start.6 = (f32[8,8,256]{2,1,0:T(8,128)S(1)}, f32[8,8,256]{2,1,0:T(8,128)S(1)}, u32[]{:S(2)}, u32[]{:S(2)}) collective-permute-start(f32[8,8,256]{2,1,0:T(8,128)S(1)} %get-tuple-element.44), channel_id=1, source_target_pairs={{0,4},{2,6},{4,0},{6,2},{8,12},{10,14},{12,8},{14,10},{16,20},{18,... | collective-permute-start | bytes 196616 | tf_op jit(solution)/shard_map/ppermute | solution.py:295
  33.2 0.1 collective-permute-start.7
  33.3 3.8 %collective-permute-done.5.refs_1_ = f32[8,8,256]{2,1,0:T(8,128)S(1)} collective-permute-done((f32[8,8,256]{2,1,0:T(8,128)S(1)}, f32[8,8,256]{2,1,0:T(8,128)S(1)}, u32[]{:S(2)}, u32[]{:S(2)}) %collective-permute-start.5) | collective-permute-done | bytes 65568 | tf_op jit(solution)/shard_map/ppermute | solution.py:295
  37.1 0.0 collective-permute-done.6.refs_2_
  37.1 2.0 %collective-permute-done.7.refs_3_ = f32[8,8,256]{2,1,0:T(8,128)S(1)} collective-permute-done((f32[8,8,256]{2,1,0:T(8,128)S(1)}, f32[8,8,256]{2,1,0:T(8,128)S(1)}, u32[]{:S(2)}, u32[]{:S(2)}) %collective-permute-start.7) | collective-permute-done | bytes 65568 | tf_op jit(solution)/shard_map/ppermute | solution.py:295
  39.1 0.0 copy-done.1
  39.1 1.5 %increment.1 = (f32[2,16,8,256]{3,2,1,0:T(8,128)}, f32[5,2,16,1,128]{4,3,2,1,0:T(1,128)S(1)}, s32[32,128]{1,0:T(8,128)S(1)}) custom-call(s32[16]{0:T(128)S(1)} %copy-done, f32[5,2,16]{2,1,0:T(2,128)S(1)} %bitcast.1, f32[8,8,256]{2,1,0:T(8,128)S(1)} %get-tuple-element.42.refs_0_, f32[8,8,256]{2,1,0:T(8,128)S(1)} %collective-permute-done.5.refs_1_, ...), custom_call_target="tpu_custom_call" | custom-call | tf_op jit(solution)/shard_map/increment/pallas_call | solution.py:386
  40.5 2.7 %all-to-all-done.arrived = f32[16,2,32,128]{3,2,1,0:T(8,128)S(1)} async-done(((f32[16,2,32,128]{3,2,1,0:T(8,128)}), f32[16,2,32,128]{3,2,1,0:T(8,128)S(1)}, u32[]{:S(2)}, u32[]{:S(2)}) %all-to-all-start) | async-done | bytes 524320 | tf_op jit(solution)/shard_map/all_to_all | solution.py:384
  43.2 1.0 %bands.1 = f32[2,16,32,128]{3,2,1,0:T(8,128)} custom-call(f32[5,2,16,1,128]{4,3,2,1,0:T(1,128)S(1)} %get-tuple-element.47.taps, s32[32,128]{1,0:T(8,128)S(1)} %get-tuple-element.48.keep, f32[16,2,32,128]{3,2,1,0:T(8,128)S(1)} %all-to-all-done.arrived), custom_call_target="tpu_custom_call" | custom-call | tf_op jit(solution)/shard_map/bands/pallas_call | solution.py:399
  (1 shorter events, 0.0 us)
Async XLA Ops:
  1.8 6.9 %collective-permute-start = (f32[8,16,256]{2,1,0:T(8,128)S(1)}, f32[8,16,256]{2,1,0:T(8,128)S(1)}, u32[]{:S(2)}, u32[]{:S(2)}) collective-permute-start(f32[8,16,256]{2,1,0:T(8,128)S(1)} %get-tuple-element.27), channel_id=1, source_target_pairs={{0,2},{2,0},{4,6},{6,4},{8,10},{10,8},{12,14},{14,12},{16,18},{18,... | collective-permute-start | bytes 393224 | tf_op jit(solution)/shard_map/ppermute | solution.py:295
  4.8 7.8 %collective-permute-start.1 = (f32[8,16,256]{2,1,0:T(8,128)S(1)}, f32[8,16,256]{2,1,0:T(8,128)S(1)}, u32[]{:S(2)}, u32[]{:S(2)}) collective-permute-start(f32[8,16,256]{2,1,0:T(8,128)S(1)} %get-tuple-element.28), channel_id=1, source_target_pairs={{0,4},{2,6},{4,0},{6,2},{8,12},{10,14},{12,8},{14,10},{16,20},{18,... | collective-permute-start | bytes 393224 | tf_op jit(solution)/shard_map/ppermute | solution.py:295
  6.3 6.3 %collective-permute-start.2 = (f32[8,16,256]{2,1,0:T(8,128)S(1)}, f32[8,16,256]{2,1,0:T(8,128)S(1)}, u32[]{:S(2)}, u32[]{:S(2)}) collective-permute-start(f32[8,16,256]{2,1,0:T(8,128)S(1)} %get-tuple-element.29), channel_id=1, source_target_pairs={{0,6},{2,4},{4,2},{6,0},{8,14},{10,12},{12,10},{14,8},{16,22},{18,... | collective-permute-start | bytes 393224 | tf_op jit(solution)/shard_map/ppermute | solution.py:295
  12.7 3.6 %copy-start = (s32[16]{0:T(128)S(1)}, s32[16]{0:T(128)}, u32[]{:S(2)}) copy-start(s32[16]{0:T(128)} %band_rows.3) | copy-start | bytes 196
  12.7 7.5 %collective-permute-start.3 = (f32[8,16,256]{2,1,0:T(8,128)S(1)}, f32[8,16,256]{2,1,0:T(8,128)S(1)}, u32[]{:S(2)}, u32[]{:S(2)}) collective-permute-start(f32[8,16,256]{2,1,0:T(8,128)S(1)} %get-tuple-element.30), channel_id=1, source_target_pairs={{0,8},{2,10},{4,12},{6,14},{8,16},{10,18},{12,20},{14,22},{16,24},... | collective-permute-start | bytes 393224 | tf_op jit(solution)/shard_map/ppermute | solution.py:323
  14.3 7.6 %collective-permute-start.4 = (f32[8,16,256]{2,1,0:T(8,128)S(1)}, f32[8,16,256]{2,1,0:T(8,128)S(1)}, u32[]{:S(2)}, u32[]{:S(2)}) collective-permute-start(f32[8,16,256]{2,1,0:T(8,128)S(1)} %get-tuple-element.39), channel_id=1, source_target_pairs={{0,25},{2,27},{4,29},{6,31},{8,0},{10,2},{12,4},{14,6},{16,8},{18,... | collective-permute-start | bytes 393224 | tf_op jit(solution)/shard_map/ppermute | solution.py:324
  23.5 19.7 %all-to-all-start = ((f32[16,2,32,128]{3,2,1,0:T(8,128)}), f32[16,2,32,128]{3,2,1,0:T(8,128)S(1)}, u32[]{:S(2)}, u32[]{:S(2)}) async-start(f32[16,2,32,128]{3,2,1,0:T(8,128)} %get-tuple-element.49), calls=%async_computation | async-start | bytes 1048576 | tf_op jit(solution)/shard_map/all_to_all | solution.py:384
  29.8 9.3 %copy-start.1 = (f32[2,5,16]{2,0,1:T(2,128)S(1)}, f32[2,5,16]{2,0,1:T(2,128)}, u32[]{:S(2)}) copy-start(f32[2,5,16]{2,0,1:T(2,128)} %param.8) | copy-start | bytes 1924
  29.8 7.3 %collective-permute-start.5 = (f32[8,8,256]{2,1,0:T(8,128)S(1)}, f32[8,8,256]{2,1,0:T(8,128)S(1)}, u32[]{:S(2)}, u32[]{:S(2)}) collective-permute-start(f32[8,8,256]{2,1,0:T(8,128)S(1)} %get-tuple-element.43), channel_id=1, source_target_pairs={{0,2},{2,0},{4,6},{6,4},{8,10},{10,8},{12,14},{14,12},{16,18},{18,... | collective-permute-start | bytes 196616 | tf_op jit(solution)/shard_map/ppermute | solution.py:295
  31.8 5.3 %collective-permute-start.6 = (f32[8,8,256]{2,1,0:T(8,128)S(1)}, f32[8,8,256]{2,1,0:T(8,128)S(1)}, u32[]{:S(2)}, u32[]{:S(2)}) collective-permute-start(f32[8,8,256]{2,1,0:T(8,128)S(1)} %get-tuple-element.44), channel_id=1, source_target_pairs={{0,4},{2,6},{4,0},{6,2},{8,12},{10,14},{12,8},{14,10},{16,20},{18,... | collective-permute-start | bytes 196616 | tf_op jit(solution)/shard_map/ppermute | solution.py:295
  33.2 5.8 %collective-permute-start.7 = (f32[8,8,256]{2,1,0:T(8,128)S(1)}, f32[8,8,256]{2,1,0:T(8,128)S(1)}, u32[]{:S(2)}, u32[]{:S(2)}) collective-permute-start(f32[8,8,256]{2,1,0:T(8,128)S(1)} %get-tuple-element.45), channel_id=1, source_target_pairs={{0,6},{2,4},{4,2},{6,0},{8,14},{10,12},{12,10},{14,8},{16,22},{18,... | collective-permute-start | bytes 196616 | tf_op jit(solution)/shard_map/ppermute | solution.py:295

commit v9 on v6

--- a/solution.py
+++ b/solution.py
@@ -24,29 +24,22 @@
 
 
 def regroup_kernel(background, scale_x, scale_y, *refs):
-    *pieces, field, along_x, along_y, sems = refs
+    *pieces, sems = refs
     variables, levels = background.shape[:2]
     part = levels // len(pieces)
     me = member(len(pieces))
-    parts, copies = [], []
-    for k in range(len(pieces)):
+    copies = []
+    for k, piece in enumerate(pieces):
         near = pl.ds(jnp.bitwise_xor(me, k) * part, part)
-        parts.append(near)
-        copies.append(
-            [
-                pltpu.make_async_copy(background.at[:, near], field.at[:, near], sems.at[k, 0]),
-                pltpu.make_async_copy(scale_x.at[near], along_x.at[near], sems.at[k, 1]),
-                pltpu.make_async_copy(scale_y.at[near], along_y.at[near], sems.at[k, 2]),
-            ]
-        )
-        for copy in copies[k]:
-            copy.start()
-    for near, piece, each in zip(parts, pieces, copies):
-        for copy in each:
-            copy.wait()
-        sources = [field[v, near] for v in range(variables)]
-        sources += [along_x[near], along_y[near]]
-        piece[...] = jnp.swapaxes(jnp.concatenate(sources, 0), 0, 1)
+        sources = [background.at[v, near] for v in range(variables)]
+        sources += [scale_x.at[near], scale_y.at[near]]
+        for i, source in enumerate(sources):
+            target = piece.at[pl.ds(i * part, part)]
+            copies.append(pltpu.make_async_copy(source, target, sems.at[k, i]))
+    for copy in copies:
+        copy.start()
+    for copy in copies:
+        copy.wait()
 
 
 def edges_kernel(*refs):
@@ -65,13 +58,14 @@
 
 
 def spread_out(source, near, field, along_x, along_y, down_y):
-    _, channels, rows = source.shape
+    channels, _, rows = source.shape
     part = channels // 4
     pairs = 2 * part
     upper = lax.broadcasted_iota(jnp.int32, (1, pairs, rows), 1) < part
     inside = lax.broadcasted_iota(jnp.int32, (1, pairs, rows), 2) < rows - 1
-    field[near] = source[:, :pairs]
-    coefs = source[:, pairs:]
+    flow = jnp.swapaxes(source[...], 0, 1)
+    field[near] = flow[:, :pairs]
+    coefs = flow[:, pairs:]
     swapped = pltpu.roll(coefs, part, 1)
     along_x[near] = jnp.where(upper, coefs, swapped)
     flow_y = jnp.where(inside, jnp.where(upper, swapped, coefs), 0.0)
@@ -137,7 +131,7 @@
 def inner_kernel(groups, band_rows, *refs):
     pieces, field, along_x, along_y, down_y = refs[:groups], *refs[groups : groups + 4]
     sides, result, bands, ready, sems = refs[groups + 4 :]
-    width = pieces[0].shape[0]
+    width = pieces[0].shape[1]
     me = member(groups)
     for k, piece in enumerate(pieces):
         near = pl.ds(jnp.bitwise_xor(me, k) * width, width)
@@ -165,7 +159,7 @@
     end, ready, band_rows, sems = refs[8:12], *refs[12:]
     rows_copy = pltpu.make_async_copy(rows_far, band_rows, sems.at[groups])
     rows_copy.start()
-    width = halo.shape[0]
+    width = halo.shape[1]
     span = groups * width
     spread_out(halo, pl.ds(side * width, width), *end)
     for here, array in zip(end, inner):
@@ -273,14 +267,13 @@
     def struct(*shape):
         return jax.ShapeDtypeStruct(shape, f32)
 
-    piece = struct(width, channels, rows)
+    piece = struct(channels, width, rows)
     parted = pl.pallas_call(
         regroup_kernel,
         out_shape=[piece] * groups,
         in_specs=[HBM] * 3,
         out_specs=[VMEM] * groups,
-        scratch_shapes=[pltpu.VMEM(a.shape, f32) for a in (background, scale_x, scale_y)]
-        + [pltpu.SemaphoreType.DMA((groups, 3))],
+        scratch_shapes=[pltpu.SemaphoreType.DMA((groups, variables + 2))],
         compiler_params=ROOM,
         name="regroup",
     )(*(pltpu.with_memory_space_constraint(a, pltpu.HBM) for a in (background, scale_x, scale_y)))

time: 44.6 us -> 44.5 us (level)
  no operation moved by 1% of the time
where the time goes in v9:
time: 44.5 us; the launch traced here: 44.2 us
  starting transfers between devices  17.9 us (40%)
  waiting for transfers between devices  15.5 us (35%)
  Pallas kernels  10.1 us (23%)
  between operations  0.72 us (2%)
    ppermute x6, waiting for transfers between devices, exchanged(): lax.ppermute(pieces[k], 'band', [(i, i ^ k) for i in range(count)])  11.9 us
    ppermute x6, starting transfers between devices, exchanged(): lax.ppermute(pieces[k], 'band', [(i, i ^ k) for i in range(count)])  8.1 us
    all_to_all x1, starting transfers between devices, shards(): lax.all_to_all(bands, 'band', split_axis=0, concat_axis=0, tiled=True)  6.22 us
    pallas_call x2, Pallas kernels, finished(): pl.pallas_call(functools.partial(end_kernel, groups, side), out_shape=[st...  3.39 us
    pallas_call x1, Pallas kernels, shards(): pl.pallas_call(functools.partial(inner_kernel, groups), out_shape=[struct...  3 us
    all_to_all x1, waiting for transfers between devices, shards(): lax.all_to_all(bands, 'band', split_axis=0, concat_axis=0, tiled=True)  2.69 us
    ppermute x1, starting transfers between devices, shards(): high = lax.ppermute(first, axes, shifted(-groups))  1.97 us
    ppermute x1, starting transfers between devices, shards(): low = lax.ppermute(last, axes, shifted(groups))  1.64 us
  transfers between devices with their start and end apart: 9, of which 6 were waited for; matrix products, arithmetic and copies ran while one was open for 0% of the time, Pallas kernels for 14%

profile of v9, /device:TPU:0, one launch (start us, length us, event | category | flops | bytes accessed | tf_op | source)
XLA Modules:
  0.0 44.2 jit_solution(14946258078165389357)
XLA Ops:
  0.6 1.2 %regroup.1 = (f32[16,8,256]{2,1,0:T(8,128)S(1)}, f32[16,8,256]{2,1,0:T(8,128)S(1)}, f32[16,8,256]{2,1,0:T(8,128)S(1)}, f32[16,8,256]{2,1,0:T(8,128)S(1)}) custom-call(f32[2,16,8,256]{3,2,1,0:T(8,128)} %background.1, f32[16,8,256]{2,1,0:T(8,128)} %scale_x.1, f32[16,8,256]{2,1,0:T(8,128)} %scale_y.1), custom_call_target="tpu_custom_call" | custom-call | tf_op jit(solution)/shard_map/regroup/pallas_call | solution.py:271
  1.8 3.0 %collective-permute-start = (f32[16,8,256]{2,1,0:T(8,128)S(1)}, f32[16,8,256]{2,1,0:T(8,128)S(1)}, u32[]{:S(2)}, u32[]{:S(2)}) collective-permute-start(f32[16,8,256]{2,1,0:T(8,128)S(1)} %get-tuple-element.27), channel_id=1, source_target_pairs={{0,2},{2,0},{4,6},{6,4},{8,10},{10,8},{12,14},{14,12},{16,18},{18,... | collective-permute-start | bytes 393224 | tf_op jit(solution)/shard_map/ppermute | solution.py:284
  4.8 1.5 %collective-permute-start.1 = (f32[16,8,256]{2,1,0:T(8,128)S(1)}, f32[16,8,256]{2,1,0:T(8,128)S(1)}, u32[]{:S(2)}, u32[]{:S(2)}) collective-permute-start(f32[16,8,256]{2,1,0:T(8,128)S(1)} %get-tuple-element.28), channel_id=1, source_target_pairs={{0,4},{2,6},{4,0},{6,2},{8,12},{10,14},{12,8},{14,10},{16,20},{18,... | collective-permute-start | bytes 393224 | tf_op jit(solution)/shard_map/ppermute | solution.py:284
  6.3 0.0 collective-permute-start.2
  6.3 2.4 %collective-permute-done.refs_1_ = f32[16,8,256]{2,1,0:T(8,128)S(1)} collective-permute-done((f32[16,8,256]{2,1,0:T(8,128)S(1)}, f32[16,8,256]{2,1,0:T(8,128)S(1)}, u32[]{:S(2)}, u32[]{:S(2)}) %collective-permute-start) | collective-permute-done | bytes 131104 | tf_op jit(solution)/shard_map/ppermute | solution.py:284
  8.7 3.9 %collective-permute-done.1.refs_2_ = f32[16,8,256]{2,1,0:T(8,128)S(1)} collective-permute-done((f32[16,8,256]{2,1,0:T(8,128)S(1)}, f32[16,8,256]{2,1,0:T(8,128)S(1)}, u32[]{:S(2)}, u32[]{:S(2)}) %collective-permute-start.1) | collective-permute-done | bytes 131104 | tf_op jit(solution)/shard_map/ppermute | solution.py:284
  12.6 0.0 collective-permute-done.2.refs_3_
  12.6 0.0 copy-start
  12.6 1.6 %collective-permute-start.3 = (f32[16,8,256]{2,1,0:T(8,128)S(1)}, f32[16,8,256]{2,1,0:T(8,128)S(1)}, u32[]{:S(2)}, u32[]{:S(2)}) collective-permute-start(f32[16,8,256]{2,1,0:T(8,128)S(1)} %get-tuple-element.30), channel_id=1, source_target_pairs={{0,8},{2,10},{4,12},{6,14},{8,16},{10,18},{12,20},{14,22},{16,24},... | collective-permute-start | bytes 393224 | tf_op jit(solution)/shard_map/ppermute | solution.py:312
  14.3 2.0 %collective-permute-start.4 = (f32[16,8,256]{2,1,0:T(8,128)S(1)}, f32[16,8,256]{2,1,0:T(8,128)S(1)}, u32[]{:S(2)}, u32[]{:S(2)}) collective-permute-start(f32[16,8,256]{2,1,0:T(8,128)S(1)} %get-tuple-element.39), channel_id=1, source_target_pairs={{0,25},{2,27},{4,29},{6,31},{8,0},{10,2},{12,4},{14,6},{16,8},{18,... | collective-permute-start | bytes 393224 | tf_op jit(solution)/shard_map/ppermute | solution.py:313
  16.2 0.0 copy-done
  16.2 3.0 %inner.1 = (f32[32,8,256]{2,1,0:T(8,128)S(1)}, f32[32,8,256]{2,1,0:T(8,128)S(1)}, f32[32,8,256]{2,1,0:T(8,128)S(1)}, f32[32,8,256]{2,1,0:T(8,128)S(1)}, f32[2,8,...) custom-call(s32[16]{0:T(128)S(1)} %copy-done, ...), custom_call_target="tpu_custom_call" | custom-call | flops 10485760 | bytes 1048576 | tf_op jit(solution)/shard_map/inner/pallas_call | solution.py:318
  19.2 0.9 %collective-permute-done.3.halo = f32[16,8,256]{2,1,0:T(8,128)S(1)} collective-permute-done((f32[16,8,256]{2,1,0:T(8,128)S(1)}, f32[16,8,256]{2,1,0:T(8,128)S(1)}, u32[]{:S(2)}, u32[]{:S(2)}) %collective-permute-start.3) | collective-permute-done | bytes 131104 | tf_op jit(solution)/shard_map/ppermute | solution.py:312
  20.2 1.7 %low_end.1 = (f32[16,2,32,128]{3,2,1,0:T(8,128)}, f32[2,8,8,128]{3,2,1,0:T(8,128)S(1)}) custom-call(s32[16]{0:T(128)S(1)} %copy-done, f32[16,8,256]{2,1,0:T(8,128)S(1)} %collective-permute-done.3.halo, f32[32,8,256]{2,1,0:T(8,128)S(1)} %get-tuple-element.31.refs_0_, f32[32,8,256]{2,1,0:T(8,128)S(1)} %get-tuple-element.32.refs_1_, ...), custom_call_target="tpu_custom_call", output_to_operand_aliasing={{0}: (7, {})} | custom-call | tf_op jit(solution)/shard_map/low_end/pallas_call | solution.py:341
  21.9 0.0 collective-permute-done.4.halo
  21.9 1.7 %high_end.1 = (f32[16,2,32,128]{3,2,1,0:T(8,128)}, f32[2,8,8,128]{3,2,1,0:T(8,128)S(1)}) custom-call(s32[16]{0:T(128)S(1)} %copy-done, f32[16,8,256]{2,1,0:T(8,128)S(1)} %collective-permute-done.4.halo, f32[32,8,256]{2,1,0:T(8,128)S(1)} %get-tuple-element.31.refs_0_, f32[32,8,256]{2,1,0:T(8,128)S(1)} %get-tuple-element.32.refs_1_, ...), custom_call_target="tpu_custom_call", output_to_operand_aliasing={{0}: (7, {})} | custom-call | tf_op jit(solution)/shard_map/high_end/pallas_call | solution.py:341
  23.6 6.2 %all-to-all-start = ((f32[16,2,32,128]{3,2,1,0:T(8,128)}), f32[16,2,32,128]{3,2,1,0:T(8,128)S(1)}, u32[]{:S(2)}, u32[]{:S(2)}) async-start(f32[16,2,32,128]{3,2,1,0:T(8,128)} %get-tuple-element.49), calls=%async_computation | async-start | bytes 1048576 | tf_op jit(solution)/shard_map/all_to_all | solution.py:371
  29.8 0.1 strips.1
  29.9 0.0 copy-start.1
  29.9 2.0 %collective-permute-start.5 = (f32[8,8,256]{2,1,0:T(8,128)S(1)}, f32[8,8,256]{2,1,0:T(8,128)S(1)}, u32[]{:S(2)}, u32[]{:S(2)}) collective-permute-start(f32[8,8,256]{2,1,0:T(8,128)S(1)} %get-tuple-element.43), channel_id=1, source_target_pairs={{0,2},{2,0},{4,6},{6,4},{8,10},{10,8},{12,14},{14,12},{16,18},{18,... | collective-permute-start | bytes 196616 | tf_op jit(solution)/shard_map/ppermute | solution.py:284
  31.9 1.5 %collective-permute-start.6 = (f32[8,8,256]{2,1,0:T(8,128)S(1)}, f32[8,8,256]{2,1,0:T(8,128)S(1)}, u32[]{:S(2)}, u32[]{:S(2)}) collective-permute-start(f32[8,8,256]{2,1,0:T(8,128)S(1)} %get-tuple-element.44), channel_id=1, source_target_pairs={{0,4},{2,6},{4,0},{6,2},{8,12},{10,14},{12,8},{14,10},{16,20},{18,... | collective-permute-start | bytes 196616 | tf_op jit(solution)/shard_map/ppermute | solution.py:284
  33.3 0.1 collective-permute-start.7
  33.5 3.6 %collective-permute-done.5.refs_1_ = f32[8,8,256]{2,1,0:T(8,128)S(1)} collective-permute-done((f32[8,8,256]{2,1,0:T(8,128)S(1)}, f32[8,8,256]{2,1,0:T(8,128)S(1)}, u32[]{:S(2)}, u32[]{:S(2)}) %collective-permute-start.5) | collective-permute-done | bytes 65568 | tf_op jit(solution)/shard_map/ppermute | solution.py:284
  37.0 0.0 collective-permute-done.6.refs_2_
  37.0 2.1 %collective-permute-done.7.refs_3_ = f32[8,8,256]{2,1,0:T(8,128)S(1)} collective-permute-done((f32[8,8,256]{2,1,0:T(8,128)S(1)}, f32[8,8,256]{2,1,0:T(8,128)S(1)}, u32[]{:S(2)}, u32[]{:S(2)}) %collective-permute-start.7) | collective-permute-done | bytes 65568 | tf_op jit(solution)/shard_map/ppermute | solution.py:284
  39.1 0.0 copy-done.1
  39.1 1.5 %increment.1 = (f32[2,16,8,256]{3,2,1,0:T(8,128)}, f32[5,2,16,1,128]{4,3,2,1,0:T(1,128)S(1)}, s32[32,128]{1,0:T(8,128)S(1)}) custom-call(s32[16]{0:T(128)S(1)} %copy-done, f32[5,2,16]{2,1,0:T(2,128)S(1)} %bitcast.1, f32[8,8,256]{2,1,0:T(8,128)S(1)} %get-tuple-element.42.refs_0_, f32[8,8,256]{2,1,0:T(8,128)S(1)} %collective-permute-done.5.refs_1_, ...), custom_call_target="tpu_custom_call" | custom-call | tf_op jit(solution)/shard_map/increment/pallas_call | solution.py:373
  40.6 2.7 %all-to-all-done.arrived = f32[16,2,32,128]{3,2,1,0:T(8,128)S(1)} async-done(((f32[16,2,32,128]{3,2,1,0:T(8,128)}), f32[16,2,32,128]{3,2,1,0:T(8,128)S(1)}, u32[]{:S(2)}, u32[]{:S(2)}) %all-to-all-start) | async-done | bytes 524320 | tf_op jit(solution)/shard_map/all_to_all | solution.py:371
  43.2 1.0 %bands.1 = f32[2,16,32,128]{3,2,1,0:T(8,128)} custom-call(f32[5,2,16,1,128]{4,3,2,1,0:T(1,128)S(1)} %get-tuple-element.47.taps, s32[32,128]{1,0:T(8,128)S(1)} %get-tuple-element.48.keep, f32[16,2,32,128]{3,2,1,0:T(8,128)S(1)} %all-to-all-done.arrived), custom_call_target="tpu_custom_call" | custom-call | tf_op jit(solution)/shard_map/bands/pallas_call | solution.py:386
  (1 shorter events, 0.0 us)
Async XLA Ops:
  1.8 6.9 %collective-permute-start = (f32[16,8,256]{2,1,0:T(8,128)S(1)}, f32[16,8,256]{2,1,0:T(8,128)S(1)}, u32[]{:S(2)}, u32[]{:S(2)}) collective-permute-start(f32[16,8,256]{2,1,0:T(8,128)S(1)} %get-tuple-element.27), channel_id=1, source_target_pairs={{0,2},{2,0},{4,6},{6,4},{8,10},{10,8},{12,14},{14,12},{16,18},{18,... | collective-permute-start | bytes 393224 | tf_op jit(solution)/shard_map/ppermute | solution.py:284
  4.8 7.8 %collective-permute-start.1 = (f32[16,8,256]{2,1,0:T(8,128)S(1)}, f32[16,8,256]{2,1,0:T(8,128)S(1)}, u32[]{:S(2)}, u32[]{:S(2)}) collective-permute-start(f32[16,8,256]{2,1,0:T(8,128)S(1)} %get-tuple-element.28), channel_id=1, source_target_pairs={{0,4},{2,6},{4,0},{6,2},{8,12},{10,14},{12,8},{14,10},{16,20},{18,... | collective-permute-start | bytes 393224 | tf_op jit(solution)/shard_map/ppermute | solution.py:284
  6.3 6.3 %collective-permute-start.2 = (f32[16,8,256]{2,1,0:T(8,128)S(1)}, f32[16,8,256]{2,1,0:T(8,128)S(1)}, u32[]{:S(2)}, u32[]{:S(2)}) collective-permute-start(f32[16,8,256]{2,1,0:T(8,128)S(1)} %get-tuple-element.29), channel_id=1, source_target_pairs={{0,6},{2,4},{4,2},{6,0},{8,14},{10,12},{12,10},{14,8},{16,22},{18,... | collective-permute-start | bytes 393224 | tf_op jit(solution)/shard_map/ppermute | solution.py:284
  12.6 3.6 %copy-start = (s32[16]{0:T(128)S(1)}, s32[16]{0:T(128)}, u32[]{:S(2)}) copy-start(s32[16]{0:T(128)} %band_rows.3) | copy-start | bytes 196
  12.6 7.5 %collective-permute-start.3 = (f32[16,8,256]{2,1,0:T(8,128)S(1)}, f32[16,8,256]{2,1,0:T(8,128)S(1)}, u32[]{:S(2)}, u32[]{:S(2)}) collective-permute-start(f32[16,8,256]{2,1,0:T(8,128)S(1)} %get-tuple-element.30), channel_id=1, source_target_pairs={{0,8},{2,10},{4,12},{6,14},{8,16},{10,18},{12,20},{14,22},{16,24},... | collective-permute-start | bytes 393224 | tf_op jit(solution)/shard_map/ppermute | solution.py:312
  14.3 7.6 %collective-permute-start.4 = (f32[16,8,256]{2,1,0:T(8,128)S(1)}, f32[16,8,256]{2,1,0:T(8,128)S(1)}, u32[]{:S(2)}, u32[]{:S(2)}) collective-permute-start(f32[16,8,256]{2,1,0:T(8,128)S(1)} %get-tuple-element.39), channel_id=1, source_target_pairs={{0,25},{2,27},{4,29},{6,31},{8,0},{10,2},{12,4},{14,6},{16,8},{18,... | collective-permute-start | bytes 393224 | tf_op jit(solution)/shard_map/ppermute | solution.py:313
  23.6 19.7 %all-to-all-start = ((f32[16,2,32,128]{3,2,1,0:T(8,128)}), f32[16,2,32,128]{3,2,1,0:T(8,128)S(1)}, u32[]{:S(2)}, u32[]{:S(2)}) async-start(f32[16,2,32,128]{3,2,1,0:T(8,128)} %get-tuple-element.49), calls=%async_computation | async-start | bytes 1048576 | tf_op jit(solution)/shard_map/all_to_all | solution.py:371
  29.9 9.2 %copy-start.1 = (f32[2,5,16]{2,0,1:T(2,128)S(1)}, f32[2,5,16]{2,0,1:T(2,128)}, u32[]{:S(2)}) copy-start(f32[2,5,16]{2,0,1:T(2,128)} %param.8) | copy-start | bytes 1924
  29.9 7.1 %collective-permute-start.5 = (f32[8,8,256]{2,1,0:T(8,128)S(1)}, f32[8,8,256]{2,1,0:T(8,128)S(1)}, u32[]{:S(2)}, u32[]{:S(2)}) collective-permute-start(f32[8,8,256]{2,1,0:T(8,128)S(1)} %get-tuple-element.43), channel_id=1, source_target_pairs={{0,2},{2,0},{4,6},{6,4},{8,10},{10,8},{12,14},{14,12},{16,18},{18,... | collective-permute-start | bytes 196616 | tf_op jit(solution)/shard_map/ppermute | solution.py:284
  31.9 5.2 %collective-permute-start.6 = (f32[8,8,256]{2,1,0:T(8,128)S(1)}, f32[8,8,256]{2,1,0:T(8,128)S(1)}, u32[]{:S(2)}, u32[]{:S(2)}) collective-permute-start(f32[8,8,256]{2,1,0:T(8,128)S(1)} %get-tuple-element.44), channel_id=1, source_target_pairs={{0,4},{2,6},{4,0},{6,2},{8,12},{10,14},{12,8},{14,10},{16,20},{18,... | collective-permute-start | bytes 196616 | tf_op jit(solution)/shard_map/ppermute | solution.py:284
  33.3 5.8 %collective-permute-start.7 = (f32[8,8,256]{2,1,0:T(8,128)S(1)}, f32[8,8,256]{2,1,0:T(8,128)S(1)}, u32[]{:S(2)}, u32[]{:S(2)}) collective-permute-start(f32[8,8,256]{2,1,0:T(8,128)S(1)} %get-tuple-element.45), channel_id=1, source_target_pairs={{0,6},{2,4},{4,2},{6,0},{8,14},{10,12},{12,10},{14,8},{16,22},{18,... | collective-permute-start | bytes 196616 | tf_op jit(solution)/shard_map/ppermute | solution.py:284

commit v10 on v9

--- a/solution.py
+++ b/solution.py
@@ -104,25 +104,29 @@
         result[half, :, at] = block[:, :, half * LANES : (half + 1) * LANES]
 
 
-def pack(result, band_rows, bands, copies):
+def pack(result, turned, band_rows, bands, copies):
     halves, channels, count, _ = result.shape
     part = channels // 2
     total = bands.shape[0]
+    for half in range(halves):
+        for i in range(channels):
+            turned[half, i] = pltpu.roll(result[half, i], i % part * CAP, 1)
     lane = lax.broadcasted_iota(jnp.int32, (count, LANES), 1)
     start = jnp.int32(0)
     for b in range(total):
         half = start // LANES
         offset = start - half * LANES
         beyond = lax.rem(half + 1, halves)
+        place = jnp.bitwise_and(lane + (LANES - offset), LANES - 1)
+        over = jnp.bitwise_and(place, CAP - 1) >= LANES - offset
         for v in range(2):
-            packed = None
-            for l in range(part):
-                i = v * part + l
-                window = jnp.where(lane >= offset, result[half, i], result[beyond, i])
-                shift = lax.rem(LANES + l * CAP - offset, LANES)
-                turned = pltpu.roll(window, shift, 1)
-                packed = turned if l == 0 else jnp.where(lane >= l * CAP, turned, packed)
-            bands[b, v] = packed
+            here, there = turned[half, v * part], turned[beyond, v * part]
+            for l in range(1, part):
+                chosen = place >= l * CAP
+                here = jnp.where(chosen, turned[half, v * part + l], here)
+                there = jnp.where(chosen, turned[beyond, v * part + l], there)
+            together = jnp.where(over, there, here)
+            bands[b, v] = pltpu.roll(together, lax.rem(LANES - offset, LANES), 1)
         start = start + band_rows[b]
         if (b + 1) * len(copies) % total == 0:
             copies[(b + 1) * len(copies) // total - 1].start()
@@ -130,7 +134,7 @@
 
 def inner_kernel(groups, band_rows, *refs):
     pieces, field, along_x, along_y, down_y = refs[:groups], *refs[groups : groups + 4]
-    sides, result, bands, ready, sems = refs[groups + 4 :]
+    sides, result, bands, ready, turned, sems = refs[groups + 4 :]
     width = pieces[0].shape[1]
     me = member(groups)
     for k, piece in enumerate(pieces):
@@ -150,13 +154,13 @@
     for s in range(1, groups - 1):
         turn(field[pl.ds(s * width, width)], result, pl.ds((s - 1) * width, width))
     copy = pltpu.make_async_copy(ready, bands.at[:, :, pl.ds(0, span - 2 * width)], sems.at[0])
-    pack(result, band_rows, ready, [copy])
+    pack(result, turned, band_rows, ready, [copy])
     copy.wait()
 
 
 def end_kernel(groups, side, rows_far, halo, *refs):
     inner, sides, _, bands, result = refs[:4], *refs[4:8]
-    end, ready, band_rows, sems = refs[8:12], *refs[12:]
+    end, ready, turned, band_rows, sems = refs[8:12], *refs[12:]
     rows_copy = pltpu.make_async_copy(rows_far, band_rows, sems.at[groups])
     rows_copy.start()
     width = halo.shape[1]
@@ -177,7 +181,7 @@
         target = bands.at[near, :, pl.ds(span - (2 - side) * width, width)]
         copies.append(pltpu.make_async_copy(ready.at[near], target, sems.at[i]))
     rows_copy.wait()
-    pack(result, band_rows, ready, copies)
+    pack(result, turned, band_rows, ready, copies)
     for copy in copies:
         copy.wait()
 
@@ -327,6 +331,7 @@
         out_specs=[VMEM] * 6 + [HBM],
         scratch_shapes=[
             pltpu.VMEM((count, variables, inside, LANES), f32),
+            pltpu.VMEM((halves, both, inside, LANES), f32),
             pltpu.SemaphoreType.DMA((1,)),
         ],
         compiler_params=ROOM,
@@ -350,6 +355,7 @@
             scratch_shapes=[pltpu.VMEM((2 * width, both, rows), f32)] * 4
             + [
                 pltpu.VMEM((count, variables, width, LANES), f32),
+                pltpu.VMEM((halves, both, width, LANES), f32),
                 pltpu.SMEM(band_rows.shape, band_rows.dtype),
                 pltpu.SemaphoreType.DMA((groups + 1,)),
             ],

time: 44.5 us -> 44.5 us (level)
  no operation moved by 1% of the time
where the time goes in v10:
time: 44.5 us; the launch traced here: 44.1 us
  starting transfers between devices  17.9 us (40%)
  waiting for transfers between devices  15.7 us (35%)
  Pallas kernels  9.81 us (22%)
  between operations  0.72 us (2%)
    ppermute x6, waiting for transfers between devices, exchanged(): lax.ppermute(pieces[k], 'band', [(i, i ^ k) for i in range(count)])  12 us
    ppermute x6, starting transfers between devices, exchanged(): lax.ppermute(pieces[k], 'band', [(i, i ^ k) for i in range(count)])  8.1 us
    all_to_all x1, starting transfers between devices, shards(): lax.all_to_all(bands, 'band', split_axis=0, concat_axis=0, tiled=True)  6.22 us
    pallas_call x2, Pallas kernels, finished(): pl.pallas_call(functools.partial(end_kernel, groups, side), out_shape=[st...  3.23 us
    pallas_call x1, Pallas kernels, shards(): pl.pallas_call(functools.partial(inner_kernel, groups), out_shape=[struct...  2.9 us
    all_to_all x1, waiting for transfers between devices, shards(): lax.all_to_all(bands, 'band', split_axis=0, concat_axis=0, tiled=True)  2.7 us
    ppermute x1, starting transfers between devices, shards(): high = lax.ppermute(first, axes, shifted(-groups))  1.97 us
    ppermute x1, starting transfers between devices, shards(): low = lax.ppermute(last, axes, shifted(groups))  1.64 us
  transfers between devices with their start and end apart: 9, of which 6 were waited for; matrix products, arithmetic and copies ran while one was open for 0% of the time, Pallas kernels for 14%

profile of v10, /device:TPU:0, one launch (start us, length us, event | category | flops | bytes accessed | tf_op | source)
XLA Modules:
  0.0 44.1 jit_solution(18381787577905185510)
XLA Ops:
  0.6 1.2 %regroup.1 = (f32[16,8,256]{2,1,0:T(8,128)S(1)}, f32[16,8,256]{2,1,0:T(8,128)S(1)}, f32[16,8,256]{2,1,0:T(8,128)S(1)}, f32[16,8,256]{2,1,0:T(8,128)S(1)}) custom-call(f32[2,16,8,256]{3,2,1,0:T(8,128)} %background.1, f32[16,8,256]{2,1,0:T(8,128)} %scale_x.1, f32[16,8,256]{2,1,0:T(8,128)} %scale_y.1), custom_call_target="tpu_custom_call" | custom-call | tf_op jit(solution)/shard_map/regroup/pallas_call | solution.py:275
  1.8 3.0 %collective-permute-start = (f32[16,8,256]{2,1,0:T(8,128)S(1)}, f32[16,8,256]{2,1,0:T(8,128)S(1)}, u32[]{:S(2)}, u32[]{:S(2)}) collective-permute-start(f32[16,8,256]{2,1,0:T(8,128)S(1)} %get-tuple-element.27), channel_id=1, source_target_pairs={{0,2},{2,0},{4,6},{6,4},{8,10},{10,8},{12,14},{14,12},{16,18},{18,... | collective-permute-start | bytes 393224 | tf_op jit(solution)/shard_map/ppermute | solution.py:288
  4.8 1.5 %collective-permute-start.1 = (f32[16,8,256]{2,1,0:T(8,128)S(1)}, f32[16,8,256]{2,1,0:T(8,128)S(1)}, u32[]{:S(2)}, u32[]{:S(2)}) collective-permute-start(f32[16,8,256]{2,1,0:T(8,128)S(1)} %get-tuple-element.28), channel_id=1, source_target_pairs={{0,4},{2,6},{4,0},{6,2},{8,12},{10,14},{12,8},{14,10},{16,20},{18,... | collective-permute-start | bytes 393224 | tf_op jit(solution)/shard_map/ppermute | solution.py:288
  6.3 0.0 collective-permute-start.2
  6.3 2.4 %collective-permute-done.refs_1_ = f32[16,8,256]{2,1,0:T(8,128)S(1)} collective-permute-done((f32[16,8,256]{2,1,0:T(8,128)S(1)}, f32[16,8,256]{2,1,0:T(8,128)S(1)}, u32[]{:S(2)}, u32[]{:S(2)}) %collective-permute-start) | collective-permute-done | bytes 131104 | tf_op jit(solution)/shard_map/ppermute | solution.py:288
  8.7 3.9 %collective-permute-done.1.refs_2_ = f32[16,8,256]{2,1,0:T(8,128)S(1)} collective-permute-done((f32[16,8,256]{2,1,0:T(8,128)S(1)}, f32[16,8,256]{2,1,0:T(8,128)S(1)}, u32[]{:S(2)}, u32[]{:S(2)}) %collective-permute-start.1) | collective-permute-done | bytes 131104 | tf_op jit(solution)/shard_map/ppermute | solution.py:288
  12.6 0.0 collective-permute-done.2.refs_3_
  12.6 0.0 copy-start
  12.6 1.6 %collective-permute-start.3 = (f32[16,8,256]{2,1,0:T(8,128)S(1)}, f32[16,8,256]{2,1,0:T(8,128)S(1)}, u32[]{:S(2)}, u32[]{:S(2)}) collective-permute-start(f32[16,8,256]{2,1,0:T(8,128)S(1)} %get-tuple-element.30), channel_id=1, source_target_pairs={{0,8},{2,10},{4,12},{6,14},{8,16},{10,18},{12,20},{14,22},{16,24},... | collective-permute-start | bytes 393224 | tf_op jit(solution)/shard_map/ppermute | solution.py:316
  14.3 2.0 %collective-permute-start.4 = (f32[16,8,256]{2,1,0:T(8,128)S(1)}, f32[16,8,256]{2,1,0:T(8,128)S(1)}, u32[]{:S(2)}, u32[]{:S(2)}) collective-permute-start(f32[16,8,256]{2,1,0:T(8,128)S(1)} %get-tuple-element.39), channel_id=1, source_target_pairs={{0,25},{2,27},{4,29},{6,31},{8,0},{10,2},{12,4},{14,6},{16,8},{18,... | collective-permute-start | bytes 393224 | tf_op jit(solution)/shard_map/ppermute | solution.py:317
  16.2 0.0 copy-done
  16.2 2.9 %inner.1 = (f32[32,8,256]{2,1,0:T(8,128)S(1)}, f32[32,8,256]{2,1,0:T(8,128)S(1)}, f32[32,8,256]{2,1,0:T(8,128)S(1)}, f32[32,8,256]{2,1,0:T(8,128)S(1)}, f32[2,8,...) custom-call(s32[16]{0:T(128)S(1)} %copy-done, ...), custom_call_target="tpu_custom_call" | custom-call | flops 10485760 | bytes 1048576 | tf_op jit(solution)/shard_map/inner/pallas_call | solution.py:322
  19.1 1.0 %collective-permute-done.3.halo = f32[16,8,256]{2,1,0:T(8,128)S(1)} collective-permute-done((f32[16,8,256]{2,1,0:T(8,128)S(1)}, f32[16,8,256]{2,1,0:T(8,128)S(1)}, u32[]{:S(2)}, u32[]{:S(2)}) %collective-permute-start.3) | collective-permute-done | bytes 131104 | tf_op jit(solution)/shard_map/ppermute | solution.py:316
  20.2 1.6 %low_end.1 = (f32[16,2,32,128]{3,2,1,0:T(8,128)}, f32[2,8,8,128]{3,2,1,0:T(8,128)S(1)}) custom-call(s32[16]{0:T(128)S(1)} %copy-done, f32[16,8,256]{2,1,0:T(8,128)S(1)} %collective-permute-done.3.halo, f32[32,8,256]{2,1,0:T(8,128)S(1)} %get-tuple-element.31.refs_0_, f32[32,8,256]{2,1,0:T(8,128)S(1)} %get-tuple-element.32.refs_1_, ...), custom_call_target="tpu_custom_call", output_to_operand_aliasing={{0}: (7, {})} | custom-call | tf_op jit(solution)/shard_map/low_end/pallas_call | solution.py:346
  21.8 0.0 collective-permute-done.4.halo
  21.8 1.6 %high_end.1 = (f32[16,2,32,128]{3,2,1,0:T(8,128)}, f32[2,8,8,128]{3,2,1,0:T(8,128)S(1)}) custom-call(s32[16]{0:T(128)S(1)} %copy-done, f32[16,8,256]{2,1,0:T(8,128)S(1)} %collective-permute-done.4.halo, f32[32,8,256]{2,1,0:T(8,128)S(1)} %get-tuple-element.31.refs_0_, f32[32,8,256]{2,1,0:T(8,128)S(1)} %get-tuple-element.32.refs_1_, ...), custom_call_target="tpu_custom_call", output_to_operand_aliasing={{0}: (7, {})} | custom-call | tf_op jit(solution)/shard_map/high_end/pallas_call | solution.py:346
  23.4 6.2 %all-to-all-start = ((f32[16,2,32,128]{3,2,1,0:T(8,128)}), f32[16,2,32,128]{3,2,1,0:T(8,128)S(1)}, u32[]{:S(2)}, u32[]{:S(2)}) async-start(f32[16,2,32,128]{3,2,1,0:T(8,128)} %get-tuple-element.49), calls=%async_computation | async-start | bytes 1048576 | tf_op jit(solution)/shard_map/all_to_all | solution.py:377
  29.7 0.1 strips.1
  29.7 0.0 copy-start.1
  29.7 2.0 %collective-permute-start.5 = (f32[8,8,256]{2,1,0:T(8,128)S(1)}, f32[8,8,256]{2,1,0:T(8,128)S(1)}, u32[]{:S(2)}, u32[]{:S(2)}) collective-permute-start(f32[8,8,256]{2,1,0:T(8,128)S(1)} %get-tuple-element.43), channel_id=1, source_target_pairs={{0,2},{2,0},{4,6},{6,4},{8,10},{10,8},{12,14},{14,12},{16,18},{18,... | collective-permute-start | bytes 196616 | tf_op jit(solution)/shard_map/ppermute | solution.py:288
  31.7 1.5 %collective-permute-start.6 = (f32[8,8,256]{2,1,0:T(8,128)S(1)}, f32[8,8,256]{2,1,0:T(8,128)S(1)}, u32[]{:S(2)}, u32[]{:S(2)}) collective-permute-start(f32[8,8,256]{2,1,0:T(8,128)S(1)} %get-tuple-element.44), channel_id=1, source_target_pairs={{0,4},{2,6},{4,0},{6,2},{8,12},{10,14},{12,8},{14,10},{16,20},{18,... | collective-permute-start | bytes 196616 | tf_op jit(solution)/shard_map/ppermute | solution.py:288
  33.2 0.1 collective-permute-start.7
  33.3 3.8 %collective-permute-done.5.refs_1_ = f32[8,8,256]{2,1,0:T(8,128)S(1)} collective-permute-done((f32[8,8,256]{2,1,0:T(8,128)S(1)}, f32[8,8,256]{2,1,0:T(8,128)S(1)}, u32[]{:S(2)}, u32[]{:S(2)}) %collective-permute-start.5) | collective-permute-done | bytes 65568 | tf_op jit(solution)/shard_map/ppermute | solution.py:288
  37.1 0.0 collective-permute-done.6.refs_2_
  37.1 1.9 %collective-permute-done.7.refs_3_ = f32[8,8,256]{2,1,0:T(8,128)S(1)} collective-permute-done((f32[8,8,256]{2,1,0:T(8,128)S(1)}, f32[8,8,256]{2,1,0:T(8,128)S(1)}, u32[]{:S(2)}, u32[]{:S(2)}) %collective-permute-start.7) | collective-permute-done | bytes 65568 | tf_op jit(solution)/shard_map/ppermute | solution.py:288
  39.0 0.0 copy-done.1
  39.0 1.5 %increment.1 = (f32[2,16,8,256]{3,2,1,0:T(8,128)}, f32[5,2,16,1,128]{4,3,2,1,0:T(1,128)S(1)}, s32[32,128]{1,0:T(8,128)S(1)}) custom-call(s32[16]{0:T(128)S(1)} %copy-done, f32[5,2,16]{2,1,0:T(2,128)S(1)} %bitcast.1, f32[8,8,256]{2,1,0:T(8,128)S(1)} %get-tuple-element.42.refs_0_, f32[8,8,256]{2,1,0:T(8,128)S(1)} %collective-permute-done.5.refs_1_, ...), custom_call_target="tpu_custom_call" | custom-call | tf_op jit(solution)/shard_map/increment/pallas_call | solution.py:379
  40.5 2.7 %all-to-all-done.arrived = f32[16,2,32,128]{3,2,1,0:T(8,128)S(1)} async-done(((f32[16,2,32,128]{3,2,1,0:T(8,128)}), f32[16,2,32,128]{3,2,1,0:T(8,128)S(1)}, u32[]{:S(2)}, u32[]{:S(2)}) %all-to-all-start) | async-done | bytes 524320 | tf_op jit(solution)/shard_map/all_to_all | solution.py:377
  43.2 1.0 %bands.1 = f32[2,16,32,128]{3,2,1,0:T(8,128)} custom-call(f32[5,2,16,1,128]{4,3,2,1,0:T(1,128)S(1)} %get-tuple-element.47.taps, s32[32,128]{1,0:T(8,128)S(1)} %get-tuple-element.48.keep, f32[16,2,32,128]{3,2,1,0:T(8,128)S(1)} %all-to-all-done.arrived), custom_call_target="tpu_custom_call" | custom-call | tf_op jit(solution)/shard_map/bands/pallas_call | solution.py:392
  (1 shorter events, 0.0 us)
Async XLA Ops:
  1.8 6.9 %collective-permute-start = (f32[16,8,256]{2,1,0:T(8,128)S(1)}, f32[16,8,256]{2,1,0:T(8,128)S(1)}, u32[]{:S(2)}, u32[]{:S(2)}) collective-permute-start(f32[16,8,256]{2,1,0:T(8,128)S(1)} %get-tuple-element.27), channel_id=1, source_target_pairs={{0,2},{2,0},{4,6},{6,4},{8,10},{10,8},{12,14},{14,12},{16,18},{18,... | collective-permute-start | bytes 393224 | tf_op jit(solution)/shard_map/ppermute | solution.py:288
  4.8 7.8 %collective-permute-start.1 = (f32[16,8,256]{2,1,0:T(8,128)S(1)}, f32[16,8,256]{2,1,0:T(8,128)S(1)}, u32[]{:S(2)}, u32[]{:S(2)}) collective-permute-start(f32[16,8,256]{2,1,0:T(8,128)S(1)} %get-tuple-element.28), channel_id=1, source_target_pairs={{0,4},{2,6},{4,0},{6,2},{8,12},{10,14},{12,8},{14,10},{16,20},{18,... | collective-permute-start | bytes 393224 | tf_op jit(solution)/shard_map/ppermute | solution.py:288
  6.3 6.3 %collective-permute-start.2 = (f32[16,8,256]{2,1,0:T(8,128)S(1)}, f32[16,8,256]{2,1,0:T(8,128)S(1)}, u32[]{:S(2)}, u32[]{:S(2)}) collective-permute-start(f32[16,8,256]{2,1,0:T(8,128)S(1)} %get-tuple-element.29), channel_id=1, source_target_pairs={{0,6},{2,4},{4,2},{6,0},{8,14},{10,12},{12,10},{14,8},{16,22},{18,... | collective-permute-start | bytes 393224 | tf_op jit(solution)/shard_map/ppermute | solution.py:288
  12.6 3.6 %copy-start = (s32[16]{0:T(128)S(1)}, s32[16]{0:T(128)}, u32[]{:S(2)}) copy-start(s32[16]{0:T(128)} %band_rows.3) | copy-start | bytes 196
  12.6 7.5 %collective-permute-start.3 = (f32[16,8,256]{2,1,0:T(8,128)S(1)}, f32[16,8,256]{2,1,0:T(8,128)S(1)}, u32[]{:S(2)}, u32[]{:S(2)}) collective-permute-start(f32[16,8,256]{2,1,0:T(8,128)S(1)} %get-tuple-element.30), channel_id=1, source_target_pairs={{0,8},{2,10},{4,12},{6,14},{8,16},{10,18},{12,20},{14,22},{16,24},... | collective-permute-start | bytes 393224 | tf_op jit(solution)/shard_map/ppermute | solution.py:316
  14.3 7.5 %collective-permute-start.4 = (f32[16,8,256]{2,1,0:T(8,128)S(1)}, f32[16,8,256]{2,1,0:T(8,128)S(1)}, u32[]{:S(2)}, u32[]{:S(2)}) collective-permute-start(f32[16,8,256]{2,1,0:T(8,128)S(1)} %get-tuple-element.39), channel_id=1, source_target_pairs={{0,25},{2,27},{4,29},{6,31},{8,0},{10,2},{12,4},{14,6},{16,8},{18,... | collective-permute-start | bytes 393224 | tf_op jit(solution)/shard_map/ppermute | solution.py:317
  23.4 19.7 %all-to-all-start = ((f32[16,2,32,128]{3,2,1,0:T(8,128)}), f32[16,2,32,128]{3,2,1,0:T(8,128)S(1)}, u32[]{:S(2)}, u32[]{:S(2)}) async-start(f32[16,2,32,128]{3,2,1,0:T(8,128)} %get-tuple-element.49), calls=%async_computation | async-start | bytes 1048576 | tf_op jit(solution)/shard_map/all_to_all | solution.py:377
  29.7 9.3 %copy-start.1 = (f32[2,5,16]{2,0,1:T(2,128)S(1)}, f32[2,5,16]{2,0,1:T(2,128)}, u32[]{:S(2)}) copy-start(f32[2,5,16]{2,0,1:T(2,128)} %param.8) | copy-start | bytes 1924
  29.7 7.3 %collective-permute-start.5 = (f32[8,8,256]{2,1,0:T(8,128)S(1)}, f32[8,8,256]{2,1,0:T(8,128)S(1)}, u32[]{:S(2)}, u32[]{:S(2)}) collective-permute-start(f32[8,8,256]{2,1,0:T(8,128)S(1)} %get-tuple-element.43), channel_id=1, source_target_pairs={{0,2},{2,0},{4,6},{6,4},{8,10},{10,8},{12,14},{14,12},{16,18},{18,... | collective-permute-start | bytes 196616 | tf_op jit(solution)/shard_map/ppermute | solution.py:288
  31.7 5.3 %collective-permute-start.6 = (f32[8,8,256]{2,1,0:T(8,128)S(1)}, f32[8,8,256]{2,1,0:T(8,128)S(1)}, u32[]{:S(2)}, u32[]{:S(2)}) collective-permute-start(f32[8,8,256]{2,1,0:T(8,128)S(1)} %get-tuple-element.44), channel_id=1, source_target_pairs={{0,4},{2,6},{4,0},{6,2},{8,12},{10,14},{12,8},{14,10},{16,20},{18,... | collective-permute-start | bytes 196616 | tf_op jit(solution)/shard_map/ppermute | solution.py:288
  33.2 5.8 %collective-permute-start.7 = (f32[8,8,256]{2,1,0:T(8,128)S(1)}, f32[8,8,256]{2,1,0:T(8,128)S(1)}, u32[]{:S(2)}, u32[]{:S(2)}) collective-permute-start(f32[8,8,256]{2,1,0:T(8,128)S(1)} %get-tuple-element.45), channel_id=1, source_target_pairs={{0,6},{2,4},{4,2},{6,0},{8,14},{10,12},{12,10},{14,8},{16,22},{18,... | collective-permute-start | bytes 196616 | tf_op jit(solution)/shard_map/ppermute | solution.py:288

commit v11 on v6

--- a/solution.py
+++ b/solution.py
@@ -23,6 +23,16 @@
     return lax.rem(lax.axis_index("band"), groups)
 
 
+def partners(groups, odd):
+    between = list(range(1, groups - 1))
+    return [0, groups - 1] + (between[::-1] if odd else between)
+
+
+def partner(groups, i):
+    odd = lax.rem(lax.axis_index("lon"), 2) == 1
+    return jnp.where(odd, partners(groups, True)[i], partners(groups, False)[i])
+
+
 def regroup_kernel(background, scale_x, scale_y, *refs):
     *pieces, field, along_x, along_y, sems = refs
     variables, levels = background.shape[:2]
@@ -30,7 +40,7 @@
     me = member(len(pieces))
     parts, copies = [], []
     for k in range(len(pieces)):
-        near = pl.ds(jnp.bitwise_xor(me, k) * part, part)
+        near = pl.ds(jnp.bitwise_xor(me, partner(len(pieces), k)) * part, part)
         parts.append(near)
         copies.append(
             [
@@ -53,13 +63,14 @@
     *pieces, first, last = refs
     groups = len(pieces)
     me = member(groups)
-    for k, piece in enumerate(pieces):
-
-        @pl.when(me == k)
+    for i, piece in enumerate(pieces):
+        apart = jnp.bitwise_xor(me, partner(groups, i))
+
+        @pl.when(apart == 0)
         def _(piece=piece):
             first[...] = piece[...]
 
-        @pl.when(me == groups - 1 - k)
+        @pl.when(apart == groups - 1)
         def _(piece=piece):
             last[...] = piece[...]
 
@@ -140,7 +151,7 @@
     width = pieces[0].shape[0]
     me = member(groups)
     for k, piece in enumerate(pieces):
-        near = pl.ds(jnp.bitwise_xor(me, k) * width, width)
+        near = pl.ds(jnp.bitwise_xor(me, partner(groups, k)) * width, width)
         spread_out(piece, near, field, along_x, along_y, down_y)
     span = groups * width
     for step in range(STEPS):
@@ -292,7 +303,19 @@
             for k in range(1, groups)
         ]
 
-    mine = exchanged(parted)
+    crossed = [partners(groups, lon % 2 == 1) for lon in range(blocks)]
+    mine = [parted[0]] + [
+        lax.ppermute(
+            parted[i],
+            ("band", "lon"),
+            [
+                (band * blocks + lon, (band ^ crossed[lon][i]) * blocks + lon)
+                for band in range(count)
+                for lon in range(blocks)
+            ],
+        )
+        for i in range(1, groups)
+    ]
     first, last = pl.pallas_call(
         edges_kernel,
         out_shape=[piece] * 2,

time: 44.6 us -> 44.5 us (level)
    ppermute x6 -> x3, waiting for transfers between devices: 11.9 us -> 5.67 us  [exchanged(): lax.ppermute(pieces[k], 'band', [(i, i ^ k) for i in range(count)])]
    ppermute x0 -> x3, waiting for transfers between devices: none -> 5.91 us  [shards(): lax.ppermute(parted[i], ('band', 'lon'), [(band * blocks + lon, (band ^ c...]
    ppermute x0 -> x3, starting transfers between devices: none -> 4.6 us  [shards(): lax.ppermute(parted[i], ('band', 'lon'), [(band * blocks + lon, (band ^ c...]
    ppermute x6 -> x3, starting transfers between devices: 8.1 us -> 3.55 us  [exchanged(): lax.ppermute(pieces[k], 'band', [(i, i ^ k) for i in range(count)])]
  transfers between devices with their start and end apart: 9 -> 9, of which waited for: 6 -> 7; matrix products, arithmetic and copies ran while one was open for 0% -> 0% of each run, Pallas kernels for 14% -> 14%
where the time goes in v11:
time: 44.5 us; the launch traced here: 44.2 us
  starting transfers between devices  18.2 us (41%)
  waiting for transfers between devices  15.2 us (34%)
  Pallas kernels  10.1 us (23%)
  between operations  0.72 us (2%)
    all_to_all x1, starting transfers between devices, shards(): lax.all_to_all(bands, 'band', split_axis=0, concat_axis=0, tiled=True)  6.43 us
    ppermute x3, waiting for transfers between devices, shards(): lax.ppermute(parted[i], ('band', 'lon'), [(band * blocks + lon, (band ^ c...  5.91 us
    ppermute x3, waiting for transfers between devices, exchanged(): lax.ppermute(pieces[k], 'band', [(i, i ^ k) for i in range(count)])  5.67 us
    ppermute x3, starting transfers between devices, shards(): lax.ppermute(parted[i], ('band', 'lon'), [(band * blocks + lon, (band ^ c...  4.6 us
    ppermute x3, starting transfers between devices, exchanged(): lax.ppermute(pieces[k], 'band', [(i, i ^ k) for i in range(count)])  3.55 us
    pallas_call x2, Pallas kernels, finished(): pl.pallas_call(functools.partial(end_kernel, groups, side), out_shape=[st...  3.41 us
    pallas_call x1, Pallas kernels, shards(): pl.pallas_call(functools.partial(inner_kernel, groups), out_shape=[struct...  2.96 us
    all_to_all x1, waiting for transfers between devices, shards(): lax.all_to_all(bands, 'band', split_axis=0, concat_axis=0, tiled=True)  2.63 us
  transfers between devices with their start and end apart: 9, of which 7 were waited for; matrix products, arithmetic and copies ran while one was open for 0% of the time, Pallas kernels for 14%

profile of v11, /device:TPU:0, one launch (start us, length us, event | category | flops | bytes accessed | tf_op | source)
XLA Modules:
  0.0 44.2 jit_solution(9024897694137298694)
XLA Ops:
  0.6 1.2 %regroup.1 = (f32[8,16,256]{2,1,0:T(8,128)S(1)}, f32[8,16,256]{2,1,0:T(8,128)S(1)}, f32[8,16,256]{2,1,0:T(8,128)S(1)}, f32[8,16,256]{2,1,0:T(8,128)S(1)}) custom-call(f32[2,16,8,256]{3,2,1,0:T(8,128)} %background.1, f32[16,8,256]{2,1,0:T(8,128)} %scale_x.1, f32[16,8,256]{2,1,0:T(8,128)} %scale_y.1), custom_call_target="tpu_custom_call" | custom-call | tf_op jit(solution)/shard_map/regroup/pallas_call | solution.py:288
  1.8 4.0 %collective-permute-start = (f32[8,16,256]{2,1,0:T(8,128)S(1)}, f32[8,16,256]{2,1,0:T(8,128)S(1)}, u32[]{:S(2)}, u32[]{:S(2)}) collective-permute-start(f32[8,16,256]{2,1,0:T(8,128)S(1)} %get-tuple-element.27), channel_id=1, source_target_pairs={{0,6},{1,7},{2,4},{3,5},{4,2},{5,3},{6,0},{7,1},{8,14},{9,15},{10,... | collective-permute-start | bytes 393224 | tf_op jit(solution)/shard_map/ppermute | solution.py:308
  5.8 0.5 %collective-permute-start.1 = (f32[8,16,256]{2,1,0:T(8,128)S(1)}, f32[8,16,256]{2,1,0:T(8,128)S(1)}, u32[]{:S(2)}, u32[]{:S(2)}) collective-permute-start(f32[8,16,256]{2,1,0:T(8,128)S(1)} %get-tuple-element.28), channel_id=1, source_target_pairs={{0,2},{1,5},{2,0},{3,7},{4,6},{5,1},{6,4},{7,3},{8,10},{9,13},{10,... | collective-permute-start | bytes 393224 | tf_op jit(solution)/shard_map/ppermute | solution.py:308
  6.3 0.1 collective-permute-start.2
  6.4 3.3 %collective-permute-done.refs_1_ = f32[8,16,256]{2,1,0:T(8,128)S(1)} collective-permute-done((f32[8,16,256]{2,1,0:T(8,128)S(1)}, f32[8,16,256]{2,1,0:T(8,128)S(1)}, u32[]{:S(2)}, u32[]{:S(2)}) %collective-permute-start) | collective-permute-done | bytes 131104 | tf_op jit(solution)/shard_map/ppermute | solution.py:308
  9.7 2.6 %collective-permute-done.1.refs_2_ = f32[8,16,256]{2,1,0:T(8,128)S(1)} collective-permute-done((f32[8,16,256]{2,1,0:T(8,128)S(1)}, f32[8,16,256]{2,1,0:T(8,128)S(1)}, u32[]{:S(2)}, u32[]{:S(2)}) %collective-permute-start.1) | collective-permute-done | bytes 131104 | tf_op jit(solution)/shard_map/ppermute | solution.py:308
  12.3 0.0 collective-permute-done.2.refs_3_
  12.3 0.1 edges.1
  12.4 0.0 copy-start
  12.4 1.6 %collective-permute-start.3 = (f32[8,16,256]{2,1,0:T(8,128)S(1)}, f32[8,16,256]{2,1,0:T(8,128)S(1)}, u32[]{:S(2)}, u32[]{:S(2)}) collective-permute-start(f32[8,16,256]{2,1,0:T(8,128)S(1)} %get-tuple-element.30), channel_id=1, source_target_pairs={{0,8},{2,10},{4,12},{6,14},{8,16},{10,18},{12,20},{14,22},{16,24},... | collective-permute-start | bytes 393224 | tf_op jit(solution)/shard_map/ppermute | solution.py:342
  14.1 2.0 %collective-permute-start.4 = (f32[8,16,256]{2,1,0:T(8,128)S(1)}, f32[8,16,256]{2,1,0:T(8,128)S(1)}, u32[]{:S(2)}, u32[]{:S(2)}) collective-permute-start(f32[8,16,256]{2,1,0:T(8,128)S(1)} %get-tuple-element.39), channel_id=1, source_target_pairs={{0,25},{2,27},{4,29},{6,31},{8,0},{10,2},{12,4},{14,6},{16,8},{18,... | collective-permute-start | bytes 393224 | tf_op jit(solution)/shard_map/ppermute | solution.py:343
  16.0 0.0 copy-done
  16.0 3.0 %inner.1 = (f32[32,8,256]{2,1,0:T(8,128)S(1)}, f32[32,8,256]{2,1,0:T(8,128)S(1)}, f32[32,8,256]{2,1,0:T(8,128)S(1)}, f32[32,8,256]{2,1,0:T(8,128)S(1)}, f32[2,8,...) custom-call(s32[16]{0:T(128)S(1)} %copy-done, ...), custom_call_target="tpu_custom_call" | custom-call | flops 10485760 | bytes 1048576 | tf_op jit(solution)/shard_map/inner/pallas_call | solution.py:348
  19.0 1.0 %collective-permute-done.3.halo = f32[8,16,256]{2,1,0:T(8,128)S(1)} collective-permute-done((f32[8,16,256]{2,1,0:T(8,128)S(1)}, f32[8,16,256]{2,1,0:T(8,128)S(1)}, u32[]{:S(2)}, u32[]{:S(2)}) %collective-permute-start.3) | collective-permute-done | bytes 131104 | tf_op jit(solution)/shard_map/ppermute | solution.py:342
  20.0 1.7 %low_end.1 = (f32[16,2,32,128]{3,2,1,0:T(8,128)}, f32[2,8,8,128]{3,2,1,0:T(8,128)S(1)}) custom-call(s32[16]{0:T(128)S(1)} %copy-done, f32[8,16,256]{2,1,0:T(8,128)S(1)} %collective-permute-done.3.halo, f32[32,8,256]{2,1,0:T(8,128)S(1)} %get-tuple-element.31.refs_0_, f32[32,8,256]{2,1,0:T(8,128)S(1)} %get-tuple-element.32.refs_1_, ...), custom_call_target="tpu_custom_call", output_to_operand_aliasing={{0}: (7, {})} | custom-call | tf_op jit(solution)/shard_map/low_end/pallas_call | solution.py:371
  21.7 0.0 collective-permute-done.4.halo
  21.7 1.7 %high_end.1 = (f32[16,2,32,128]{3,2,1,0:T(8,128)}, f32[2,8,8,128]{3,2,1,0:T(8,128)S(1)}) custom-call(s32[16]{0:T(128)S(1)} %copy-done, f32[8,16,256]{2,1,0:T(8,128)S(1)} %collective-permute-done.4.halo, f32[32,8,256]{2,1,0:T(8,128)S(1)} %get-tuple-element.31.refs_0_, f32[32,8,256]{2,1,0:T(8,128)S(1)} %get-tuple-element.32.refs_1_, ...), custom_call_target="tpu_custom_call", output_to_operand_aliasing={{0}: (7, {})} | custom-call | tf_op jit(solution)/shard_map/high_end/pallas_call | solution.py:371
  23.4 6.4 %all-to-all-start = ((f32[16,2,32,128]{3,2,1,0:T(8,128)}), f32[16,2,32,128]{3,2,1,0:T(8,128)S(1)}, u32[]{:S(2)}, u32[]{:S(2)}) async-start(f32[16,2,32,128]{3,2,1,0:T(8,128)} %get-tuple-element.49), calls=%async_computation | async-start | bytes 1048576 | tf_op jit(solution)/shard_map/all_to_all | solution.py:401
  29.8 0.1 strips.1
  29.9 0.0 copy-start.1
  29.9 2.0 %collective-permute-start.5 = (f32[8,8,256]{2,1,0:T(8,128)S(1)}, f32[8,8,256]{2,1,0:T(8,128)S(1)}, u32[]{:S(2)}, u32[]{:S(2)}) collective-permute-start(f32[8,8,256]{2,1,0:T(8,128)S(1)} %get-tuple-element.43), channel_id=1, source_target_pairs={{0,2},{2,0},{4,6},{6,4},{8,10},{10,8},{12,14},{14,12},{16,18},{18,... | collective-permute-start | bytes 196616 | tf_op jit(solution)/shard_map/ppermute | solution.py:302
  31.9 1.5 %collective-permute-start.6 = (f32[8,8,256]{2,1,0:T(8,128)S(1)}, f32[8,8,256]{2,1,0:T(8,128)S(1)}, u32[]{:S(2)}, u32[]{:S(2)}) collective-permute-start(f32[8,8,256]{2,1,0:T(8,128)S(1)} %get-tuple-element.44), channel_id=1, source_target_pairs={{0,4},{2,6},{4,0},{6,2},{8,12},{10,14},{12,8},{14,10},{16,20},{18,... | collective-permute-start | bytes 196616 | tf_op jit(solution)/shard_map/ppermute | solution.py:302
  33.4 0.1 collective-permute-start.7
  33.5 3.5 %collective-permute-done.5.refs_1_ = f32[8,8,256]{2,1,0:T(8,128)S(1)} collective-permute-done((f32[8,8,256]{2,1,0:T(8,128)S(1)}, f32[8,8,256]{2,1,0:T(8,128)S(1)}, u32[]{:S(2)}, u32[]{:S(2)}) %collective-permute-start.5) | collective-permute-done | bytes 65568 | tf_op jit(solution)/shard_map/ppermute | solution.py:302
  37.0 0.1 collective-permute-done.6.refs_2_
  37.1 2.1 %collective-permute-done.7.refs_3_ = f32[8,8,256]{2,1,0:T(8,128)S(1)} collective-permute-done((f32[8,8,256]{2,1,0:T(8,128)S(1)}, f32[8,8,256]{2,1,0:T(8,128)S(1)}, u32[]{:S(2)}, u32[]{:S(2)}) %collective-permute-start.7) | collective-permute-done | bytes 65568 | tf_op jit(solution)/shard_map/ppermute | solution.py:302
  39.1 0.0 copy-done.1
  39.1 1.5 %increment.1 = (f32[2,16,8,256]{3,2,1,0:T(8,128)}, f32[5,2,16,1,128]{4,3,2,1,0:T(1,128)S(1)}, s32[32,128]{1,0:T(8,128)S(1)}) custom-call(s32[16]{0:T(128)S(1)} %copy-done, f32[5,2,16]{2,1,0:T(2,128)S(1)} %bitcast.1, f32[8,8,256]{2,1,0:T(8,128)S(1)} %get-tuple-element.42.refs_0_, f32[8,8,256]{2,1,0:T(8,128)S(1)} %collective-permute-done.5.refs_1_, ...), custom_call_target="tpu_custom_call" | custom-call | tf_op jit(solution)/shard_map/increment/pallas_call | solution.py:403
  40.6 2.6 %all-to-all-done.arrived = f32[16,2,32,128]{3,2,1,0:T(8,128)S(1)} async-done(((f32[16,2,32,128]{3,2,1,0:T(8,128)}), f32[16,2,32,128]{3,2,1,0:T(8,128)S(1)}, u32[]{:S(2)}, u32[]{:S(2)}) %all-to-all-start) | async-done | bytes 524320 | tf_op jit(solution)/shard_map/all_to_all | solution.py:401
  43.2 1.0 %bands.1 = f32[2,16,32,128]{3,2,1,0:T(8,128)} custom-call(f32[5,2,16,1,128]{4,3,2,1,0:T(1,128)S(1)} %get-tuple-element.47.taps, s32[32,128]{1,0:T(8,128)S(1)} %get-tuple-element.48.keep, f32[16,2,32,128]{3,2,1,0:T(8,128)S(1)} %all-to-all-done.arrived), custom_call_target="tpu_custom_call" | custom-call | tf_op jit(solution)/shard_map/bands/pallas_call | solution.py:416
Async XLA Ops:
  1.8 7.9 %collective-permute-start = (f32[8,16,256]{2,1,0:T(8,128)S(1)}, f32[8,16,256]{2,1,0:T(8,128)S(1)}, u32[]{:S(2)}, u32[]{:S(2)}) collective-permute-start(f32[8,16,256]{2,1,0:T(8,128)S(1)} %get-tuple-element.27), channel_id=1, source_target_pairs={{0,6},{1,7},{2,4},{3,5},{4,2},{5,3},{6,0},{7,1},{8,14},{9,15},{10,... | collective-permute-start | bytes 393224 | tf_op jit(solution)/shard_map/ppermute | solution.py:308
  5.8 6.6 %collective-permute-start.1 = (f32[8,16,256]{2,1,0:T(8,128)S(1)}, f32[8,16,256]{2,1,0:T(8,128)S(1)}, u32[]{:S(2)}, u32[]{:S(2)}) collective-permute-start(f32[8,16,256]{2,1,0:T(8,128)S(1)} %get-tuple-element.28), channel_id=1, source_target_pairs={{0,2},{1,5},{2,0},{3,7},{4,6},{5,1},{6,4},{7,3},{8,10},{9,13},{10,... | collective-permute-start | bytes 393224 | tf_op jit(solution)/shard_map/ppermute | solution.py:308
  6.3 6.0 %collective-permute-start.2 = (f32[8,16,256]{2,1,0:T(8,128)S(1)}, f32[8,16,256]{2,1,0:T(8,128)S(1)}, u32[]{:S(2)}, u32[]{:S(2)}) collective-permute-start(f32[8,16,256]{2,1,0:T(8,128)S(1)} %get-tuple-element.29), channel_id=1, source_target_pairs={{0,4},{1,3},{2,6},{3,1},{4,0},{5,7},{6,2},{7,5},{8,12},{9,11},{10,... | collective-permute-start | bytes 393224 | tf_op jit(solution)/shard_map/ppermute | solution.py:308
  12.4 3.6 %copy-start = (s32[16]{0:T(128)S(1)}, s32[16]{0:T(128)}, u32[]{:S(2)}) copy-start(s32[16]{0:T(128)} %band_rows.3) | copy-start | bytes 196
  12.4 7.5 %collective-permute-start.3 = (f32[8,16,256]{2,1,0:T(8,128)S(1)}, f32[8,16,256]{2,1,0:T(8,128)S(1)}, u32[]{:S(2)}, u32[]{:S(2)}) collective-permute-start(f32[8,16,256]{2,1,0:T(8,128)S(1)} %get-tuple-element.30), channel_id=1, source_target_pairs={{0,8},{2,10},{4,12},{6,14},{8,16},{10,18},{12,20},{14,22},{16,24},... | collective-permute-start | bytes 393224 | tf_op jit(solution)/shard_map/ppermute | solution.py:342
  14.1 7.6 %collective-permute-start.4 = (f32[8,16,256]{2,1,0:T(8,128)S(1)}, f32[8,16,256]{2,1,0:T(8,128)S(1)}, u32[]{:S(2)}, u32[]{:S(2)}) collective-permute-start(f32[8,16,256]{2,1,0:T(8,128)S(1)} %get-tuple-element.39), channel_id=1, source_target_pairs={{0,25},{2,27},{4,29},{6,31},{8,0},{10,2},{12,4},{14,6},{16,8},{18,... | collective-permute-start | bytes 393224 | tf_op jit(solution)/shard_map/ppermute | solution.py:343
  23.4 19.8 %all-to-all-start = ((f32[16,2,32,128]{3,2,1,0:T(8,128)}), f32[16,2,32,128]{3,2,1,0:T(8,128)S(1)}, u32[]{:S(2)}, u32[]{:S(2)}) async-start(f32[16,2,32,128]{3,2,1,0:T(8,128)} %get-tuple-element.49), calls=%async_computation | async-start | bytes 1048576 | tf_op jit(solution)/shard_map/all_to_all | solution.py:401
  29.9 9.2 %copy-start.1 = (f32[2,5,16]{2,0,1:T(2,128)S(1)}, f32[2,5,16]{2,0,1:T(2,128)}, u32[]{:S(2)}) copy-start(f32[2,5,16]{2,0,1:T(2,128)} %param.8) | copy-start | bytes 1924
  29.9 7.1 %collective-permute-start.5 = (f32[8,8,256]{2,1,0:T(8,128)S(1)}, f32[8,8,256]{2,1,0:T(8,128)S(1)}, u32[]{:S(2)}, u32[]{:S(2)}) collective-permute-start(f32[8,8,256]{2,1,0:T(8,128)S(1)} %get-tuple-element.43), channel_id=1, source_target_pairs={{0,2},{2,0},{4,6},{6,4},{8,10},{10,8},{12,14},{14,12},{16,18},{18,... | collective-permute-start | bytes 196616 | tf_op jit(solution)/shard_map/ppermute | solution.py:302
  31.9 5.2 %collective-permute-start.6 = (f32[8,8,256]{2,1,0:T(8,128)S(1)}, f32[8,8,256]{2,1,0:T(8,128)S(1)}, u32[]{:S(2)}, u32[]{:S(2)}) collective-permute-start(f32[8,8,256]{2,1,0:T(8,128)S(1)} %get-tuple-element.44), channel_id=1, source_target_pairs={{0,4},{2,6},{4,0},{6,2},{8,12},{10,14},{12,8},{14,10},{16,20},{18,... | collective-permute-start | bytes 196616 | tf_op jit(solution)/shard_map/ppermute | solution.py:302
  33.4 5.8 %collective-permute-start.7 = (f32[8,8,256]{2,1,0:T(8,128)S(1)}, f32[8,8,256]{2,1,0:T(8,128)S(1)}, u32[]{:S(2)}, u32[]{:S(2)}) collective-permute-start(f32[8,8,256]{2,1,0:T(8,128)S(1)} %get-tuple-element.45), channel_id=1, source_target_pairs={{0,6},{2,4},{4,2},{6,0},{8,14},{10,12},{12,10},{14,8},{16,22},{18,... | collective-permute-start | bytes 196616 | tf_op jit(solution)/shard_map/ppermute | solution.py:302
